TPU v7x, 256 devices: a whole 4x4x8 slice. The times are simulated.
256 devices in a mesh: aux: 2 (over core), row: 16 (over x, z_lo), col: 8 (over z_hi, y).
Axes of the slice: x: 4, y: 4, z: 8 (z_hi: 2, z_lo: 4; z = z_hi * 4 + z_lo), core: 2. Of those that a mesh axis runs over, the one named last changes fastest.
Arguments:
- three_index: float32 [4, 6144, 6144], P('aux', 'row', 'col'), as said below
- occupied: float32 [6144, 800], P('col'), may hold values from -0.078125 to 0.078125
Outputs:
- exchange: float32 [6144, 6144], P('row', ('col', 'aux'))
Inputs may be any that keep to these rules, and one draw needn't show every extreme that they name: three_index[P, m, l] equals three_index[P, l, m].
All inputs are finite; a program needn't handle non-finite values.
Results may differ from a plain program's by a relative error of at most 0.000065.
Values sent between devices are 32-bit elements; how exact they have to be, the bound alone decides.
No kernel may reach another device: no remote copies, remote signals or barrier semaphores. Data moves between devices by JAX's collectives and lax.ppermute only.
A program may use at most 64 MiB of HBM per device.

v0:
```python
import jax
import jax.numpy as jnp
from jax import lax
from jax.sharding import PartitionSpec as P


def spread(value, axis, source):
    kept = jnp.where(lax.axis_index(axis) == source, value, 0).astype(value.dtype)
    return lax.psum(kept, axis)


def body(three_index, occupied):
    highest = lax.Precision.HIGHEST
    row_block = three_index.shape[1]
    blocks_per = lax.axis_size("row") // lax.axis_size("col")
    row_half = jnp.einsum("pml,li->pmi", three_index, occupied, precision=highest)
    row_half = lax.psum(row_half, "col")
    owner_col = lax.axis_index("row") // blocks_per
    coeff_block = spread(occupied, "col", owner_col)
    coeff_local = lax.dynamic_slice_in_dim(
        coeff_block, lax.axis_index("row") % blocks_per * row_block, row_block, 0
    )
    col_half = jnp.einsum("pml,mi->pli", three_index, coeff_local, precision=highest)
    col_half = lax.psum(col_half, "row")
    partial_tile = jnp.einsum("pmi,pni->mn", row_half, col_half, precision=highest)
    return lax.psum_scatter(partial_tile, "aux", scatter_dimension=1, tiled=True)


def solution(mesh):
    in_specs = (P("aux", "row", "col"), P("col", None))
    out_specs = P("row", ("col", "aux"))
    return jax.shard_map(body, mesh=mesh, in_specs=in_specs, out_specs=out_specs, check_vma=False)
```

profile of v0, /device:TPU:1, one launch (start us, length us, event | category | flops | bytes accessed | tf_op | source)
XLA Modules:
  0.0 512.8 jit_solution(36881608559296190)
XLA Ops:
  6.5 0.0 copy-start
  6.5 0.0 all-reduce.6.cloned.1.call-start
  6.5 0.0 copy-start.1
  6.5 3.5 broadcast_select_fusion
  10.0 0.0 copy-done
  10.0 0.1 copy-done.1
  10.1 7.5 %fusion = f32[2,384,800]{1,2,0:T(8,128)} fusion(f32[2,384,768]{2,1,0:T(8,128)S(1)} %copy-done, f32[768,800]{0,1:T(8,128)S(1)} %copy-done.1), kind=kOutput, calls=%fused_computation | convolution fusion | flops 5662310400 | bytes 7274496 | tf_op jit(solution)/shard_map/pml,li->pmi/dot_general | solution.py:16
  17.6 0.0 all-reduce.6.cloned.1.call-update
  17.6 0.0 all-reduce.4.cloned.1.call-start
  17.7 226.6 %all-reduce.6.cloned.1.call-done = (f32[2,384,800]{1,2,0:T(8,128)}, f32[768,800]{0,1:T(8,128)}) async-done(((f32[2,384,800]{1,2,0:T(8,128)}, f32[768,800]{0,1:T(8,128)}), (f32[2,384,800]{1,2,0:T(8,128)}, f32[768,800]{0,1:T(8,128)})) %all-reduce.6.cloned.1.call-update) | async-done | bytes 4915216 | tf_op jit(solution)/shard_map/psum | solution.py:17
  244.3 11.1 %convolution_bitcast_fusion = f32[2,768,800]{1,2,0:T(8,128)} fusion(f32[2,384,768]{2,1,0:T(8,128)S(1)} %copy-done, f32[768,800]{0,1:T(8,128)} %get-tuple-element.6, s32[]{:T(128)S(6)} %select_n.26), kind=kOutput, calls=%fused_computation.2 | convolution fusion | flops 5662310400 | bytes 8503300 | tf_op jit(solution)/shard_map/pml,mi->pli/dot_general | solution.py:23
  255.3 0.0 all-reduce.4.cloned.1.call-update
  255.4 0.2 reduce-scatter.2.cloned.1.call-start
  255.6 227.1 %all-reduce.4.cloned.1.call-done = f32[2,768,800]{1,2,0:T(8,128)} async-done(((f32[2,768,800]{1,2,0:T(8,128)}), f32[2,768,800]{1,2,0:T(8,128)}) %all-reduce.4.cloned.1.call-update) | async-done | bytes 4915216 | tf_op jit(solution)/shard_map/psum | solution.py:24
  482.7 11.0 %convolution_bitcast_fusion.1 = f32[384,768]{1,0:T(8,128)} fusion(f32[2,384,800]{1,2,0:T(8,128)} %get-tuple-element.5, f32[2,768,800]{1,2,0:T(8,128)} %all-reduce.4.cloned.1.call-done), kind=kOutput, calls=%fused_computation.3 | convolution fusion | flops 5662310400 | bytes 8552448 | tf_op jit(solution)/shard_map/pmi,pni->mn/dot_general | solution.py:25
  493.7 0.0 reduce-scatter.2.cloned.1.call-update
  493.7 12.5 %reduce-scatter.2.cloned.1.call-done = f32[384,384]{1,0:T(8,128)} async-done(((f32[384,768]{1,0:T(8,128)}), f32[384,384]{1,0:T(8,128)}) %reduce-scatter.2.cloned.1.call-update) | async-done | bytes 589840 | tf_op jit(solution)/shard_map/reduce_scatter | solution.py:26
Async XLA Ops:
  6.5 3.5 copy-start
  6.5 237.7 %all-reduce.6.cloned.1.call-start = ((), (), s32[]{:S(2)}) async-start(), calls=%async_computation.3 | async-start | bytes 9830400 | tf_op jit(solution)/shard_map/psum | solution.py:17
  6.5 3.5 copy-start.1
  17.6 465.1 %all-reduce.4.cloned.1.call-start = ((), (), s32[]{:S(2)}) async-start(), calls=%async_computation.1 | async-start | bytes 9830400 | tf_op jit(solution)/shard_map/psum | solution.py:24
  255.4 250.9 %reduce-scatter.2.cloned.1.call-start = ((), (), s32[]{:S(2)}) async-start(), calls=%async_computation.2 | async-start | bytes 1769472 | tf_op jit(solution)/shard_map/reduce_scatter | solution.py:26
Sparse Core Ops, SparseCore 0:
  17.7 226.4 all-reduce.5
  255.5 227.2 all-reduce.3
  493.9 12.3 reduce-scatter.1
where the time goes:
time: 513 us
  waiting for transfers between devices  466 us (91%)
  matrix products  29.6 us (6%)
  between operations  13.1 us (3%)
    psum x1, waiting for transfers between devices, body(): col_half = lax.psum(col_half, 'row')  227 us
    psum x1, waiting for transfers between devices, body(): row_half = lax.psum(row_half, 'col')  227 us
    reduce_scatter x1, waiting for transfers between devices, body(): lax.psum_scatter(partial_tile, 'aux', scatter_dimension=1, tiled=True)  12.5 us
    dot_general x1, matrix products, body(): jnp.einsum('pml,mi->pli', three_index, coeff_local, precision=highest)  11.1 us
    dot_general x1, matrix products, body(): jnp.einsum('pmi,pni->mn', row_half, col_half, precision=highest)  11 us
  transfers between devices with their start and end apart: 3, of which 3 were waited for; matrix products, arithmetic and copies ran while one was open for 0% of the time, Pallas kernels for 0%

commit v1 on v0

v1 whole, which is shorter than its diff:
```python
import jax
import jax.numpy as jnp
from jax import lax
from jax.sharding import Mesh, PartitionSpec as P

HIGH = lax.Precision.HIGH


def swapped(value, axis):
    return lax.ppermute(value, axis, [(0, 1), (1, 0)])


def shifted(value, axis, distance):
    size = lax.axis_size(axis)
    return lax.ppermute(value, axis, [(i, (i + distance) % size) for i in range(size)])


def body(three_index, occupied):
    aux_here, rows, cols = three_index.shape
    nocc = occupied.shape[1]
    x_size, y_size = lax.axis_size("x"), lax.axis_size("y")
    zl, zh, y = lax.axis_index("zl"), lax.axis_index("zh"), lax.axis_index("y")

    parts = y_size // aux_here
    group = nocc // (parts * x_size)
    padded = -(-group // 8) * 8
    coeff = occupied.reshape(cols, parts * x_size, group)
    coeff = jnp.pad(coeff, ((0, 0), (0, 0), (0, padded - group)))
    coeff = coeff.reshape(cols, parts * x_size * padded)

    half = jnp.einsum("li,pml->pim", coeff, three_index, precision=HIGH)
    half = half.reshape(y_size, x_size, padded, rows)
    half = lax.all_to_all(half, "y", 0, 0, tiled=True)
    part = jnp.sum(half, axis=0)
    part = part + swapped(part, "zh")
    part = lax.all_to_all(part, "x", 0, 0, tiled=True)
    gathered = jnp.stack([part] + [shifted(part, "y", d) for d in (1, 2, 3)])
    mine = lax.dynamic_index_in_dim(gathered, 2 * zh + y // 2, 1, keepdims=False)
    pairs = []
    for yy in range(4):
        for j in range(2):
            source, target = 2 * (yy % 2) + j, 2 * (1 - yy % 2) + j
            pairs.append((source * 4 + yy, target * 4 + yy))
    crossed = lax.ppermute(mine, ("zl", "y"), pairs)
    mine = jnp.where(zl // 2 == y % 2, mine, crossed)
    other = lax.ppermute(mine, "zl", [(0, 1), (1, 0), (2, 3), (3, 2)])
    low = jnp.where(zl % 2 == 0, mine, other)
    high = jnp.where(zl % 2 == 0, other, mine)
    column = jnp.concatenate([low, high], axis=-1)

    tile = jnp.einsum("yxkm,ykn->xmn", gathered, column, precision=HIGH)
    aux = lax.axis_index("aux")
    cut = tile.shape[-1] // 2
    keep = lax.dynamic_slice_in_dim(tile, aux * cut, cut, 2)
    give = lax.dynamic_slice_in_dim(tile, (1 - aux) * cut, cut, 2)
    tile = keep + swapped(give, "aux")
    tile = lax.all_to_all(tile, "x", 0, 0, tiled=True)
    return jnp.sum(tile, axis=0)


def solution(mesh):
    fine = Mesh(mesh.devices.reshape(2, 4, 4, 2, 4), ("aux", "x", "zl", "zh", "y"))
    in_specs = (P("aux", ("x", "zl"), ("zh", "y")), P(("zh", "y"), None))
    out_specs = P(("x", "zl"), ("zh", "y", "aux"))
    return jax.shard_map(body, mesh=fine, in_specs=in_specs, out_specs=out_specs, check_vma=False)
```

time: 513 us -> 230 us (0.45)
  waiting for transfers between devices: 466 us -> 76.4 us
  blocking collectives: 0 us -> 77.8 us
  starting transfers between devices: 0.27 us -> 39.9 us
  matrix products: 29.6 us -> 9.79 us
  between operations: 13.1 us -> 0.08 us
  local copies, waits for them, and re-layouts: 0.06 us -> 11.1 us
  other arithmetic: 3.48 us -> 12.3 us
    psum x2 -> x0, waiting for transfers between devices: 454 us -> none  [the longest x1 227 us: body(): col_half = lax.psum(col_half, 'row')]
    all_to_all x0 -> x3, blocking collectives: none -> 77.8 us  [the longest x1 34.3 us: body(): half = lax.all_to_all(half, 'y', 0, 0, tiled=True)]
    ppermute x0 -> x7, waiting for transfers between devices: none -> 76.4 us  [the longest x3 30.4 us: shifted(): lax.ppermute(value, axis, [(i, (i + distance) % size) for i in range(size)])]
    ppermute x0 -> x7, starting transfers between devices: none -> 39.9 us  [the longest x1 18.9 us: body(): crossed = lax.ppermute(mine, ('zl', 'y'), pairs)]
    dot_general x3 -> x2, matrix products: 29.6 us -> 9.79 us  [the longest x1 6.47 us: body(): tile = jnp.einsum('yxkm,ykn->xmn', gathered, column, precision=HIGH)]
    reduce_scatter x1 -> x0, waiting for transfers between devices: 12.5 us -> none  [body(): lax.psum_scatter(partial_tile, 'aux', scatter_dimension=1, tiled=True)]
  transfers between devices with their start and end apart: 3 -> 7, of which waited for: 3 -> 7; matrix products, arithmetic and copies ran while one was open for 0% -> 0% of each run, Pallas kernels for 0% -> 0%
where the time goes in v1:
time: 230 us; the launch traced here: 227 us
  blocking collectives  77.8 us (34%)
  waiting for transfers between devices  76.4 us (33%)
  starting transfers between devices  39.9 us (17%)
  other arithmetic  12.3 us (5%)
  local copies, waits for them, and re-layouts  11.1 us (5%)
  matrix products  9.79 us (4%)
    all_to_all x1, blocking collectives, body(): half = lax.all_to_all(half, 'y', 0, 0, tiled=True)  34.3 us
    all_to_all x1, blocking collectives, body(): tile = lax.all_to_all(tile, 'x', 0, 0, tiled=True)  32.2 us
    ppermute x3, waiting for transfers between devices, shifted(): lax.ppermute(value, axis, [(i, (i + distance) % size) for i in range(size)])  30.4 us
    ppermute x2, waiting for transfers between devices, swapped(): return lax.ppermute(value, axis, [(0, 1), (1, 0)])  19.2 us
    ppermute x1, starting transfers between devices, body(): crossed = lax.ppermute(mine, ('zl', 'y'), pairs)  18.9 us
    ppermute x1, waiting for transfers between devices, body(): other = lax.ppermute(mine, 'zl', [(0, 1), (1, 0), (2, 3), (3, 2)])  14 us
    ppermute x1, waiting for transfers between devices, body(): crossed = lax.ppermute(mine, ('zl', 'y'), pairs)  12.8 us
    all_to_all x1, blocking collectives, body(): part = lax.all_to_all(part, 'x', 0, 0, tiled=True)  11.3 us
  transfers between devices with their start and end apart: 7, of which 7 were waited for; matrix products, arithmetic and copies ran while one was open for 0% of the time, Pallas kernels for 0%

profile of v1, /device:TPU:1, one launch (start us, length us, event | category | flops | bytes accessed | tf_op | source)
XLA Modules:
  0.0 227.3 jit_solution(15215482411307057791)
XLA Ops:
  0.0 0.0 copy-start
  0.0 3.1 %reshape.9 = f32[768,8,100]{0,2,1:T(8,128)} reshape(f32[768,800]{0,1:T(8,128)} %param.3) | data formatting | bytes 4915200 | tf_op jit(solution)/shard_map/reshape | solution.py:27
  3.1 1.9 pad.4
  5.0 0.0 copy-done
  5.0 3.3 %fusion.3 = f32[832,2,384]{2,0,1:T(8,128)S(1)} fusion(f32[768,832,1]{0,1,2:T(8,128)S(1)} %bitcast.31, f32[2,384,768]{2,1,0:T(8,128)S(1)} %copy-done), kind=kOutput, calls=%fused_computation.12 | convolution fusion | flops 2944401408 | bytes 7471104 | tf_op jit(solution)/shard_map/li,pml->pim/dot_general | solution.py:31
  8.3 34.3 %all_to_all.15 = f32[4,4,104,384]{3,2,1,0:T(8,128)} all-to-all(f32[4,4,104,384]{3,2,1,0:T(8,128)S(1)} %bitcast.30), channel_id=1, replica_groups=mesh['aux'=2,'x'=4,'zl'=4,'zh'=2,'y'=4] {'y'}, dimensions={0} | all-to-all | bytes 5111808 | tf_op jit(solution)/shard_map/all_to_all | solution.py:33
  42.6 1.9 reduce_sum.18
  44.5 7.7 %collective-permute-start = (f32[4,104,384]{2,1,0:T(8,128)S(1)}, f32[4,104,384]{2,1,0:T(8,128)S(1)}, u32[]{:S(2)}, u32[]{:S(2)}) collective-permute-start(f32[4,104,384]{2,1,0:T(8,128)S(1)} %reduce_sum.18), channel_id=1, source_target_pairs={{0,4},{4,0},{1,5},{5,1},{2,6},{6,2},{3,7},{7,3},{8,12},{12,8},{9,1... | collective-permute-start | bytes 1916936 | tf_op jit(solution)/shard_map/ppermute | solution.py:10
  52.2 14.7 %collective-permute-done = f32[4,104,384]{2,1,0:T(8,128)S(1)} collective-permute-done((f32[4,104,384]{2,1,0:T(8,128)S(1)}, f32[4,104,384]{2,1,0:T(8,128)S(1)}, u32[]{:S(2)}, u32[]{:S(2)}) %collective-permute-start) | collective-permute-done | bytes 639008 | tf_op jit(solution)/shard_map/ppermute | solution.py:10
  66.9 0.1 add.31
  67.0 11.3 %all_to_all.16 = f32[4,104,384]{2,1,0:T(8,128)S(1)} all-to-all(f32[4,104,384]{2,1,0:T(8,128)S(1)} %add.31), channel_id=1, replica_groups=mesh['aux'=2,'x'=4,'zl'=4,'zh'=2,'y'=4] {'x'}, dimensions={0} | all-to-all | bytes 1277952 | tf_op jit(solution)/shard_map/all_to_all | solution.py:36
  78.3 0.9 collective-permute-start.3
  79.2 1.2 collective-permute-start.2
  80.4 0.0 collective-permute-start.1
  80.4 8.4 %collective-permute-done.3 = f32[4,104,384]{2,1,0:T(8,128)} collective-permute-done((f32[4,104,384]{2,1,0:T(8,128)S(1)}, f32[4,104,384]{2,1,0:T(8,128)}, u32[]{:S(2)}, u32[]{:S(2)}) %collective-permute-start.3) | collective-permute-done | bytes 639008 | tf_op jit(solution)/shard_map/ppermute | solution.py:15
  88.8 2.2 collective-permute-done.2
  90.9 19.9 %collective-permute-done.1 = f32[4,104,384]{2,1,0:T(8,128)} collective-permute-done((f32[4,104,384]{2,1,0:T(8,128)S(1)}, f32[4,104,384]{2,1,0:T(8,128)}, u32[]{:S(2)}, u32[]{:S(2)}) %collective-permute-start.1) | collective-permute-done | bytes 639008 | tf_op jit(solution)/shard_map/ppermute | solution.py:15
  110.8 1.6 pad_maximum_fusion
  112.4 0.0 copy-start.2
  112.4 1.5 copy-done.2
  113.9 0.9 dynamic-slice_bitcast_fusion
  114.8 18.9 %collective-permute-start.4 = (f32[4,104,384]{2,1,0:T(8,128)}, f32[4,104,384]{2,1,0:T(8,128)}, u32[]{:S(2)}, u32[]{:S(2)}) collective-permute-start(f32[4,104,384]{2,1,0:T(8,128)} %dynamic-slice_bitcast_fusion), channel_id=1, source_target_pairs={{0,16},{8,24},{17,1},{25,9},{2,18},{10,26},{19,3},{27,11},{4,20},{... | collective-permute-start | bytes 1916936 | tf_op jit(solution)/shard_map/ppermute | solution.py:44
  133.8 12.8 %collective-permute-done.4 = f32[4,104,384]{2,1,0:T(8,128)} collective-permute-done((f32[4,104,384]{2,1,0:T(8,128)}, f32[4,104,384]{2,1,0:T(8,128)}, u32[]{:S(2)}, u32[]{:S(2)}) %collective-permute-start.4) | collective-permute-done | bytes 639008 | tf_op jit(solution)/shard_map/ppermute | solution.py:44
  146.5 2.0 broadcast_select_fusion
  148.5 9.6 %collective-permute-start.5 = (f32[4,104,384]{2,1,0:T(8,128)}, f32[4,104,384]{2,1,0:T(8,128)}, u32[]{:S(2)}, u32[]{:S(2)}) collective-permute-start(f32[4,104,384]{2,1,0:T(8,128)} %broadcast_select_fusion), channel_id=1, source_target_pairs={{0,8},{8,0},{16,24},{24,16},{1,9},{9,1},{17,25},{25,17},{2,10},{10... | collective-permute-start | bytes 1916936 | tf_op jit(solution)/shard_map/ppermute | solution.py:46
  158.1 14.0 %collective-permute-done.5 = f32[4,104,384]{2,1,0:T(8,128)} collective-permute-done((f32[4,104,384]{2,1,0:T(8,128)}, f32[4,104,384]{2,1,0:T(8,128)}, u32[]{:S(2)}, u32[]{:S(2)}) %collective-permute-start.5) | collective-permute-done | bytes 639008 | tf_op jit(solution)/shard_map/ppermute | solution.py:46
  172.2 1.4 broadcast_select_fusion.2
  173.5 6.5 %convolution_bitcast_fusion = f32[4,384,768]{2,1,0:T(8,128)S(1)} fusion(f32[4,104,384]{2,1,0:T(8,128)S(1)} %get-tuple-element.6, f32[4,104,384]{2,1,0:T(8,128)S(1)} %get-tuple-element.5, f32[1,4,104,384]{3,2,0,1:T(8,128)} %bitcast.10, f32[1,4,104,384]{3,2,0,1:T(8,128)} %bitcast.9, f32[1,4,104,384]{3,2,0,1:T(8,128)} %bitcast.7, ...), kind=kOutput, calls=%fused_computation.2 | convolution fusion | flops 2946637824 | bytes 8552448 | tf_op jit(solution)/shard_map/yxkm,ykn->xmn/dot_general | solution.py:51
  180.0 0.0 copy-start.1
  180.0 2.1 copy-done.1
  182.1 1.6 constant_dynamic-slice_fusion
  183.8 1.6 collective-permute-start.6
  185.4 4.5 %collective-permute-done.6 = f32[4,384,384]{2,1,0:T(8,128)} collective-permute-done((f32[4,384,384]{2,1,0:T(8,128)}, f32[4,384,384]{2,1,0:T(8,128)}, u32[]{:S(2)}, u32[]{:S(2)}) %collective-permute-start.6) | collective-permute-done | bytes 2359328 | tf_op jit(solution)/shard_map/ppermute | solution.py:10
  189.9 2.6 %dynamic-slice_add_fusion = f32[4,384,384]{2,1,0:T(8,128)S(1)} fusion(f32[4,384,384]{2,1,0:T(8,128)} %collective-permute-done.6, f32[4,384,768]{2,1,0:T(8,128)} %copy-done.1, s32[]{:T(128)S(6)} %select_n.58), kind=kLoop, calls=%fused_computation.1 | loop fusion | flops 589824 | bytes 7077892 | tf_op jit(solution)/shard_map/add | solution.py:56
  192.5 32.2 %all_to_all.17 = f32[4,384,384]{2,1,0:T(8,128)} all-to-all(f32[4,384,384]{2,1,0:T(8,128)S(1)} %dynamic-slice_add_fusion), channel_id=1, replica_groups=mesh['aux'=2,'x'=4,'zl'=4,'zh'=2,'y'=4] {'x'}, dimensions={0} | all-to-all | bytes 4718592 | tf_op jit(solution)/shard_map/all_to_all | solution.py:57
  224.6 2.7 %reduce_sum.19 = f32[384,384]{1,0:T(8,128)} reduce(f32[4,384,384]{2,1,0:T(8,128)} %all_to_all.17, f32[]{:T(128)} %constant.55.clone.1), dimensions={0}, to_apply=%region_1.2 | reduce | flops 442368 | bytes 2949124 | tf_op jit(solution)/shard_map/reduce_sum | solution.py:58
Async XLA Ops:
  0.0 5.0 %copy-start = (f32[2,384,768]{2,1,0:T(8,128)S(1)}, f32[2,384,768]{2,1,0:T(8,128)}, u32[]{:S(2)}) copy-start(f32[2,384,768]{2,1,0:T(8,128)} %param.2) | copy-start | bytes 7077892
  44.5 22.4 %collective-permute-start = (f32[4,104,384]{2,1,0:T(8,128)S(1)}, f32[4,104,384]{2,1,0:T(8,128)S(1)}, u32[]{:S(2)}, u32[]{:S(2)}) collective-permute-start(f32[4,104,384]{2,1,0:T(8,128)S(1)} %reduce_sum.18), channel_id=1, source_target_pairs={{0,4},{4,0},{1,5},{5,1},{2,6},{6,2},{3,7},{7,3},{8,12},{12,8},{9,1... | collective-permute-start | bytes 1916936 | tf_op jit(solution)/shard_map/ppermute | solution.py:10
  78.3 10.4 %collective-permute-start.3 = (f32[4,104,384]{2,1,0:T(8,128)S(1)}, f32[4,104,384]{2,1,0:T(8,128)}, u32[]{:S(2)}, u32[]{:S(2)}) collective-permute-start(f32[4,104,384]{2,1,0:T(8,128)S(1)} %all_to_all.16), channel_id=1, source_target_pairs={{0,3},{1,0},{2,1},{3,2},{4,7},{5,4},{6,5},{7,6},{8,11},{9,8},{10,9... | collective-permute-start | bytes 1916936 | tf_op jit(solution)/shard_map/ppermute | solution.py:15
  79.2 11.7 %collective-permute-start.2 = (f32[4,104,384]{2,1,0:T(8,128)S(1)}, f32[4,104,384]{2,1,0:T(8,128)}, u32[]{:S(2)}, u32[]{:S(2)}) collective-permute-start(f32[4,104,384]{2,1,0:T(8,128)S(1)} %all_to_all.16), channel_id=1, source_target_pairs={{0,2},{1,3},{2,0},{3,1},{4,6},{5,7},{6,4},{7,5},{8,10},{9,11},{10,... | collective-permute-start | bytes 1916936 | tf_op jit(solution)/shard_map/ppermute | solution.py:15
  80.4 30.4 %collective-permute-start.1 = (f32[4,104,384]{2,1,0:T(8,128)S(1)}, f32[4,104,384]{2,1,0:T(8,128)}, u32[]{:S(2)}, u32[]{:S(2)}) collective-permute-start(f32[4,104,384]{2,1,0:T(8,128)S(1)} %all_to_all.16), channel_id=1, source_target_pairs={{0,1},{1,2},{2,3},{3,0},{4,5},{5,6},{6,7},{7,4},{8,9},{9,10},{10,1... | collective-permute-start | bytes 1916936 | tf_op jit(solution)/shard_map/ppermute | solution.py:15
  112.4 1.5 copy-start.2
  114.8 31.7 %collective-permute-start.4 = (f32[4,104,384]{2,1,0:T(8,128)}, f32[4,104,384]{2,1,0:T(8,128)}, u32[]{:S(2)}, u32[]{:S(2)}) collective-permute-start(f32[4,104,384]{2,1,0:T(8,128)} %dynamic-slice_bitcast_fusion), channel_id=1, source_target_pairs={{0,16},{8,24},{17,1},{25,9},{2,18},{10,26},{19,3},{27,11},{4,20},{... | collective-permute-start | bytes 1916936 | tf_op jit(solution)/shard_map/ppermute | solution.py:44
  148.5 23.7 %collective-permute-start.5 = (f32[4,104,384]{2,1,0:T(8,128)}, f32[4,104,384]{2,1,0:T(8,128)}, u32[]{:S(2)}, u32[]{:S(2)}) collective-permute-start(f32[4,104,384]{2,1,0:T(8,128)} %broadcast_select_fusion), channel_id=1, source_target_pairs={{0,8},{8,0},{16,24},{24,16},{1,9},{9,1},{17,25},{25,17},{2,10},{10... | collective-permute-start | bytes 1916936 | tf_op jit(solution)/shard_map/ppermute | solution.py:46
  180.0 2.1 copy-start.1
  183.8 6.1 %collective-permute-start.6 = (f32[4,384,384]{2,1,0:T(8,128)}, f32[4,384,384]{2,1,0:T(8,128)}, u32[]{:S(2)}, u32[]{:S(2)}) collective-permute-start(f32[4,384,384]{2,1,0:T(8,128)} %constant_dynamic-slice_fusion), channel_id=1, source_target_pairs={{0,128},{128,0},{1,129},{129,1},{2,130},{130,2},{3,131},{131,3},{4... | collective-permute-start | bytes 7077896 | tf_op jit(solution)/shard_map/ppermute | solution.py:10

commit v2 on v1

v2 whole, which is shorter than its diff:
```python
import jax
import jax.numpy as jnp
from jax import lax
from jax.sharding import Mesh, PartitionSpec as P

HIGH = lax.Precision.HIGH
CHUNK = 128
SPLIT = (104, 96, 104, 96)


def swapped(value, axis):
    return lax.ppermute(value, axis, [(0, 1), (1, 0)])


def shifted(value, axis, distance):
    size = lax.axis_size(axis)
    return lax.ppermute(value, axis, [(i, (i + distance) % size) for i in range(size)])


def sum_scattered(pieces, axis):
    here = lax.axis_index(axis)
    size = lax.axis_size(axis)
    total = lax.dynamic_index_in_dim(pieces, here, 0, keepdims=False)
    arrived = []
    for d in (2, 1, 3):
        piece = lax.dynamic_index_in_dim(pieces, (here + d) % size, 0, keepdims=False)
        arrived.append(shifted(piece, axis, d))
    return total + arrived[0] + arrived[1] + arrived[2]


def crossing(value):
    pairs = []
    for y in range(4):
        if y % 2 == 0:
            moves = {0: (3, y), 2: (1, y ^ 1)}
        else:
            moves = {3: (0, y), 1: (2, y ^ 1)}
        for z, (to_z, to_y) in moves.items():
            pairs.append((z * 4 + y, to_z * 4 + to_y))
    return lax.ppermute(value, ("zl", "y"), pairs)


def body(three_index, occupied):
    aux_here, rows, cols = three_index.shape
    nocc = occupied.shape[1]
    x_size, y_size = lax.axis_size("x"), lax.axis_size("y")
    aux, zl, zh, y = (lax.axis_index(a) for a in ("aux", "zl", "zh", "y"))
    parts = y_size // aux_here
    padded = max(SPLIT)

    gathered = []
    for start in range(0, rows, CHUNK):
        block = three_index[:, start : start + CHUNK]
        half = jnp.einsum("li,pml->pim", occupied, block, precision=HIGH)
        half = half.reshape(y_size, nocc // parts, CHUNK)
        part = sum_scattered(half, "y")
        part = part + swapped(part, "zh")
        pieces, at = [], 0
        for size in SPLIT:
            pieces.append(jnp.pad(part[at : at + size], ((0, padded - size), (0, 0))))
            at += size
        pieces = jnp.broadcast_to(jnp.stack(pieces)[:, None], (x_size, y_size, padded, CHUNK))
        pieces = pieces.reshape(x_size * y_size, padded, CHUNK)
        pieces = lax.all_to_all(pieces, ("x", "y"), 0, 0, tiled=True)
        gathered.append(pieces.reshape(x_size, y_size * padded, CHUNK))
    left = jnp.concatenate(gathered, axis=-1)

    home = (zl // 2) == (y % 2)
    which = (zl + zl // 2 + y) % 2
    out = []
    for piece in gathered:
        mine = lax.dynamic_index_in_dim(piece, 2 * zh + y // 2, 0, keepdims=False)
        have = jnp.where(home, mine, crossing(mine))
        other = lax.ppermute(have, "zl", [(0, 1), (1, 0), (2, 3), (3, 2)])
        keep = jnp.where(which == aux, have, other)
        give = jnp.where(which == aux, other, have)
        give = jnp.einsum("xkm,kn->xmn", left, give, precision=HIGH)
        keep = jnp.einsum("xkm,kn->xmn", left, keep, precision=HIGH)
        out.append(sum_scattered(keep + swapped(give, "aux"), "x"))
    return jnp.concatenate(out, axis=-1)


def solution(mesh):
    fine = Mesh(mesh.devices.reshape(2, 4, 4, 2, 4), ("aux", "x", "zl", "zh", "y"))
    in_specs = (P("aux", ("x", "zl"), ("zh", "y")), P(("zh", "y"), None))
    out_specs = P(("x", "zl"), ("zh", "y", "aux"))
    return jax.shard_map(body, mesh=fine, in_specs=in_specs, out_specs=out_specs, check_vma=False)
```

time: 230 us -> 183 us (0.80)
  the two profiles are of different devices: /device:TPU:1 before, /device:TPU:26 now
where the time goes in v2:
time: 183 us; the launch traced here: 182 us
  starting transfers between devices  85.4 us (47%)
  local copies, waits for them, and re-layouts  30.4 us (17%)
  waiting for transfers between devices  29.8 us (16%)
  matrix products  23 us (13%)
  other arithmetic  12.6 us (7%)
    ppermute x18, starting transfers between devices, shifted(): lax.ppermute(value, axis, [(i, (i + distance) % size) for i in range(size)])  32.1 us
    all_to_all x3, starting transfers between devices, body(): pieces = lax.all_to_all(pieces, ('x', 'y'), 0, 0, tiled=True)  26.7 us
    ppermute x6, starting transfers between devices, swapped(): return lax.ppermute(value, axis, [(0, 1), (1, 0)])  15.4 us
    dynamic_slice x9, local copies, waits for them, and re-layouts, sum_scattered(): lax.dynamic_index_in_dim(pieces, (here + d) % size, 0, keepdims=False)  12.2 us
    all_to_all x3, waiting for transfers between devices, body(): pieces = lax.all_to_all(pieces, ('x', 'y'), 0, 0, tiled=True)  10.5 us
    dot_general x3, matrix products, body(): give = jnp.einsum('xkm,kn->xmn', left, give, precision=HIGH)  9.61 us
    dot_general x3, matrix products, body(): keep = jnp.einsum('xkm,kn->xmn', left, keep, precision=HIGH)  8.61 us
    ppermute x18, waiting for transfers between devices, shifted(): lax.ppermute(value, axis, [(i, (i + distance) % size) for i in range(size)])  8.12 us
  transfers between devices with their start and end apart: 33, of which 9 were waited for; matrix products, arithmetic and copies ran while one was open for 32% of the time, Pallas kernels for 0%

profile of v2, /device:TPU:26, one launch (start us, length us, event | category | flops | bytes accessed | tf_op | source)
XLA Modules:
  0.0 181.6 jit_solution(6735639728973833494)
XLA Ops:
  0.0 1.7 copy-done
  1.7 2.4 %fusion.4 = f32[2,128,800]{1,2,0:T(8,128)S(1)} fusion(f32[768,800]{0,1:T(8,128)S(1)} %copy-done, f32[2,384,768]{2,1,0:T(8,128)} %param.2), kind=kOutput, calls=%fused_computation.5 | convolution fusion | flops 943718400 | bytes 4063232 | tf_op jit(solution)/shard_map/li,pml->pim/dot_general | solution.py:54
  6.3 2.2 %collective-permute-start.1 = (f32[400,128]{1,0:T(8,128)}, f32[400,128]{1,0:T(8,128)}, u32[]{:S(2)}, u32[]{:S(2)}) collective-permute-start(f32[400,128]{1,0:T(8,128)} %get-tuple-element.7), channel_id=1, source_target_pairs={{0,1},{1,2},{2,3},{3,0},{4,5},{5,6},{6,7},{7,4},{8,9},{9,10},{10,1... | collective-permute-start | bytes 614408 | tf_op jit(solution)/shard_map/ppermute | solution.py:17
  10.6 2.1 %collective-permute-start.4 = (f32[400,128]{1,0:T(8,128)}, f32[400,128]{1,0:T(8,128)S(1)}, u32[]{:S(2)}, u32[]{:S(2)}) collective-permute-start(f32[400,128]{1,0:T(8,128)} %get-tuple-element.8), channel_id=1, source_target_pairs={{0,2},{1,3},{2,0},{3,1},{4,6},{5,7},{6,4},{7,5},{8,10},{9,11},{10,... | collective-permute-start | bytes 614408 | tf_op jit(solution)/shard_map/ppermute | solution.py:17
  12.7 1.3 collective-permute-start.5
  16.9 3.2 %collective-permute-start.10 = (f32[400,128]{1,0:T(8,128)}, f32[400,128]{1,0:T(8,128)}, u32[]{:S(2)}, u32[]{:S(2)}) collective-permute-start(f32[400,128]{1,0:T(8,128)} %get-tuple-element.12), channel_id=1, source_target_pairs={{0,3},{1,0},{2,1},{3,2},{4,7},{5,4},{6,5},{7,6},{8,11},{9,8},{10,9... | collective-permute-start | bytes 614408 | tf_op jit(solution)/shard_map/ppermute | solution.py:17
  20.1 3.9 %collective-permute-start.8 = (f32[400,128]{1,0:T(8,128)}, f32[400,128]{1,0:T(8,128)}, u32[]{:S(2)}, u32[]{:S(2)}) collective-permute-start(f32[400,128]{1,0:T(8,128)} %get-tuple-element.11), channel_id=1, source_target_pairs={{0,2},{1,3},{2,0},{3,1},{4,6},{5,7},{6,4},{7,5},{8,10},{9,11},{10,... | collective-permute-start | bytes 614408 | tf_op jit(solution)/shard_map/ppermute | solution.py:17
  25.5 7.2 %collective-permute-start.3 = (f32[400,128]{1,0:T(8,128)S(1)}, f32[400,128]{1,0:T(8,128)S(1)}, u32[]{:S(2)}, u32[]{:S(2)}) collective-permute-start(f32[400,128]{1,0:T(8,128)S(1)} %fusion.29), channel_id=1, source_target_pairs={{0,4},{4,0},{1,5},{5,1},{2,6},{6,2},{3,7},{7,3},{8,12},{12,8},{9,1... | collective-permute-start | bytes 614408 | tf_op jit(solution)/shard_map/ppermute | solution.py:12
  33.9 1.4 collective-permute-start.7
  35.3 4.1 %collective-permute-done.3 = f32[400,128]{1,0:T(8,128)S(1)} collective-permute-done((f32[400,128]{1,0:T(8,128)S(1)}, f32[400,128]{1,0:T(8,128)S(1)}, u32[]{:S(2)}, u32[]{:S(2)}) %collective-permute-start.3) | collective-permute-done | bytes 204832 | tf_op jit(solution)/shard_map/ppermute | solution.py:12
  40.5 11.6 %all-to-all-start = ((f32[16,104,128]{2,1,0:T(8,128)}), f32[16,104,128]{2,1,0:T(8,128)S(1)}, u32[]{:S(2)}, u32[]{:S(2)}) async-start(f32[16,104,128]{2,1,0:T(8,128)} %bitcast.148), calls=%async_computation | async-start | bytes 1703936 | tf_op jit(solution)/shard_map/all_to_all | solution.py:64
  52.1 2.0 %fusion.25 = f32[400,128]{1,0:T(8,128)} fusion(f32[400,128]{1,0:T(8,128)} %collective-permute-done.10, f32[400,128]{1,0:T(8,128)} %collective-permute-done.9, f32[400,128]{1,0:T(8,128)} %collective-permute-done.8, f32[4,400,128]{2,1,0:T(8,128)} %bitcast.151, s32[]{:T(128)S(6)} %select_n.159), kind=kLoop, calls=%fused_computation.37 | loop fusion | flops 153600 | bytes 1024004 | tf_op jit(solution)/shard_map/add | solution.py:28
  54.1 6.5 %collective-permute-start.11 = (f32[400,128]{1,0:T(8,128)}, f32[400,128]{1,0:T(8,128)}, u32[]{:S(2)}, u32[]{:S(2)}) collective-permute-start(f32[400,128]{1,0:T(8,128)} %fusion.25), channel_id=1, source_target_pairs={{0,4},{4,0},{1,5},{5,1},{2,6},{6,2},{3,7},{7,3},{8,12},{12,8},{9,1... | collective-permute-start | bytes 614408 | tf_op jit(solution)/shard_map/ppermute | solution.py:12
  62.6 7.2 %all-to-all-start.1 = ((f32[16,104,128]{2,1,0:T(8,128)}), f32[16,104,128]{2,1,0:T(8,128)}, u32[]{:S(2)}, u32[]{:S(2)}) async-start(f32[16,104,128]{2,1,0:T(8,128)} %bitcast.149), calls=%async_computation.1 | async-start | bytes 1703936 | tf_op jit(solution)/shard_map/all_to_all | solution.py:64
  71.0 7.2 %all-to-all-done.1 = f32[16,104,128]{2,1,0:T(8,128)} async-done(((f32[16,104,128]{2,1,0:T(8,128)}), f32[16,104,128]{2,1,0:T(8,128)}, u32[]{:S(2)}, u32[]{:S(2)}) %all-to-all-start.1) | async-done | bytes 852000 | tf_op jit(solution)/shard_map/all_to_all | solution.py:64
  79.2 7.9 %all-to-all-start.2 = ((f32[16,104,128]{2,1,0:T(8,128)}), f32[16,104,128]{2,1,0:T(8,128)}, u32[]{:S(2)}, u32[]{:S(2)}) async-start(f32[16,104,128]{2,1,0:T(8,128)} %bitcast.147), calls=%async_computation.2 | async-start | bytes 1703936 | tf_op jit(solution)/shard_map/all_to_all | solution.py:64
  87.8 1.3 collective-permute-start.12
  89.1 1.6 dynamic-slice_bitcast_fusion.1
  92.0 3.3 %all-to-all-done.2 = f32[16,104,128]{2,1,0:T(8,128)} async-done(((f32[16,104,128]{2,1,0:T(8,128)}), f32[16,104,128]{2,1,0:T(8,128)}, u32[]{:S(2)}, u32[]{:S(2)}) %all-to-all-start.2) | async-done | bytes 852000 | tf_op jit(solution)/shard_map/all_to_all | solution.py:64
  96.3 1.3 collective-permute-start.24
  97.6 2.4 %collective-permute-done.12 = f32[416,128]{1,0:T(8,128)} collective-permute-done((f32[416,128]{1,0:T(8,128)}, f32[416,128]{1,0:T(8,128)}, u32[]{:S(2)}, u32[]{:S(2)}) %collective-permute-start.12) | collective-permute-done | bytes 213024 | tf_op jit(solution)/shard_map/ppermute | solution.py:40
  100.9 5.1 %collective-permute-start.13 = (f32[416,128]{1,0:T(8,128)S(1)}, f32[416,128]{1,0:T(8,128)S(1)}, u32[]{:S(2)}, u32[]{:S(2)}) collective-permute-start(f32[416,128]{1,0:T(8,128)S(1)} %broadcast_select_fusion.2), channel_id=1, source_target_pairs={{0,8},{8,0},{16,24},{24,16},{1,9},{9,1},{17,25},{25,17},{2,10},{10... | collective-permute-start | bytes 638984 | tf_op jit(solution)/shard_map/ppermute | solution.py:74
  107.1 2.7 %collective-permute-done.13 = f32[416,128]{1,0:T(8,128)S(1)} collective-permute-done((f32[416,128]{1,0:T(8,128)S(1)}, f32[416,128]{1,0:T(8,128)S(1)}, u32[]{:S(2)}, u32[]{:S(2)}) %collective-permute-start.13) | collective-permute-done | bytes 213024 | tf_op jit(solution)/shard_map/ppermute | solution.py:74
  109.9 3.3 %fusion.15 = f32[4,384,128]{1,2,0:T(8,128)} fusion(f32[416,128]{1,0:T(8,128)S(1)} %collective-permute-done.13, f32[416,128]{1,0:T(8,128)S(1)} %broadcast_select_fusion.2, pred[]{:T(512)S(6)} %eq.32, f32[4,416,128]{2,1,0:T(8,128)} %bitcast.39, f32[4,416,128]{2,1,0:T(8,128)} %bitcast.26, f32[4,416,128]{2,1,0:T(8,128)S(1)} %bitcast.141), kind=kOutput, calls=%fused_computation.23 | convolution fusion | flops 492064768 | bytes 3768321 | tf_op jit(solution)/shard_map/xkm,kn->xmn/dot_general | solution.py:77
  114.1 2.1 %collective-permute-start.25 = (f32[416,128]{1,0:T(8,128)S(1)}, f32[416,128]{1,0:T(8,128)}, u32[]{:S(2)}, u32[]{:S(2)}) collective-permute-start(f32[416,128]{1,0:T(8,128)S(1)} %broadcast_select_fusion), channel_id=1, source_target_pairs={{0,8},{8,0},{16,24},{24,16},{1,9},{9,1},{17,25},{25,17},{2,10},{10... | collective-permute-start | bytes 638984 | tf_op jit(solution)/shard_map/ppermute | solution.py:74
  116.9 3.2 %fusion.12 = f32[4,384,128]{1,2,0:T(8,128)} fusion(f32[416,128]{1,0:T(8,128)S(1)} %collective-permute-done.19, f32[416,128]{1,0:T(8,128)S(1)} %broadcast_select_fusion.1, pred[]{:T(512)S(6)} %eq.32, f32[4,416,128]{2,1,0:T(8,128)} %bitcast.39, f32[4,416,128]{2,1,0:T(8,128)} %bitcast.26, f32[4,416,128]{2,1,0:T(8,128)S(1)} %bitcast.142), kind=kOutput, calls=%fused_computation.20 | convolution fusion | flops 492064768 | bytes 3768321 | tf_op jit(solution)/shard_map/xkm,kn->xmn/dot_general | solution.py:77
  120.3 1.9 %collective-permute-done.25 = f32[416,128]{1,0:T(8,128)} collective-permute-done((f32[416,128]{1,0:T(8,128)S(1)}, f32[416,128]{1,0:T(8,128)}, u32[]{:S(2)}, u32[]{:S(2)}) %collective-permute-start.25) | collective-permute-done | bytes 213024 | tf_op jit(solution)/shard_map/ppermute | solution.py:74
  122.2 3.2 %fusion.9 = f32[4,384,128]{1,2,0:T(8,128)} fusion(f32[416,128]{1,0:T(8,128)} %collective-permute-done.25, f32[416,128]{1,0:T(8,128)S(1)} %broadcast_select_fusion, pred[]{:T(512)S(6)} %eq.32, f32[4,416,128]{2,1,0:T(8,128)} %bitcast.39, f32[4,416,128]{2,1,0:T(8,128)} %bitcast.26, f32[4,416,128]{2,1,0:T(8,128)S(1)} %bitcast.143), kind=kOutput, calls=%fused_computation.17 | convolution fusion | flops 492064768 | bytes 3768321 | tf_op jit(solution)/shard_map/xkm,kn->xmn/dot_general | solution.py:77
  125.4 2.5 %convolution_add_fusion.2 = f32[4,384,128]{1,2,0:T(8,128)S(1)} fusion(f32[4,384,128]{1,2,0:T(8,128)} %collective-permute-done.14, f32[416,128]{1,0:T(8,128)S(1)} %copy-done.7, f32[416,128]{1,0:T(8,128)S(1)} %copy-done.10, pred[]{:T(512)S(6)} %eq.32, f32[4,416,128]{2,1,0:T(8,128)} %bitcast.39, f32[4,416,128]{2,1,0:T(8,128)} %bitcast.26, ...), kind=kOutput, calls=%fused_computation.9 | convolution fusion | flops 492261376 | bytes 4554753 | tf_op jit(solution)/shard_map/xkm,kn->xmn/dot_general | solution.py:78
  128.9 1.7 copy.8
  130.7 1.3 collective-permute-start.15
  132.0 1.7 copy.9
  133.7 5.0 %collective-permute-start.16 = (f32[384,128]{1,0:T(8,128)}, f32[384,128]{1,0:T(8,128)}, u32[]{:S(2)}, u32[]{:S(2)}) collective-permute-start(f32[384,128]{1,0:T(8,128)} %bitcast.157), channel_id=1, source_target_pairs={{0,32},{32,64},{64,96},{96,0},{1,33},{33,65},{65,97},{97,1},{2,34}... | collective-permute-start | bytes 589832 | tf_op jit(solution)/shard_map/ppermute | solution.py:17
  138.7 1.8 copy.10
  140.5 2.1 %collective-permute-start.17 = (f32[384,128]{1,0:T(8,128)}, f32[384,128]{1,0:T(8,128)}, u32[]{:S(2)}, u32[]{:S(2)}) collective-permute-start(f32[384,128]{1,0:T(8,128)} %bitcast.156), channel_id=1, source_target_pairs={{0,96},{32,0},{64,32},{96,64},{1,97},{33,1},{65,33},{97,65},{2,98}... | collective-permute-start | bytes 589832 | tf_op jit(solution)/shard_map/ppermute | solution.py:17
  142.6 1.7 copy.7
  144.3 2.6 %convolution_add_fusion.1 = f32[4,384,128]{1,2,0:T(8,128)S(1)} fusion(f32[4,384,128]{1,2,0:T(8,128)} %collective-permute-done.20, f32[416,128]{1,0:T(8,128)} %copy-done.5, f32[416,128]{1,0:T(8,128)} %copy-done.8, pred[]{:T(512)S(6)} %eq.32, f32[4,416,128]{2,1,0:T(8,128)} %bitcast.39, f32[4,416,128]{2,1,0:T(8,128)} %bitcast.26, f32[4,416,128]{2,1,0:T(8,128)S(1)} %bitcast.145), kind=kOutput, calls=%fused_computation.8 | convolution fusion | flops 492261376 | bytes 4554753 | tf_op jit(solution)/shard_map/xkm,kn->xmn/dot_general | solution.py:78
  147.8 1.7 copy.13
  149.5 2.1 %collective-permute-start.21 = (f32[384,128]{1,0:T(8,128)}, f32[384,128]{1,0:T(8,128)}, u32[]{:S(2)}, u32[]{:S(2)}) collective-permute-start(f32[384,128]{1,0:T(8,128)} %bitcast.160), channel_id=1, source_target_pairs={{0,64},{32,96},{64,0},{96,32},{1,65},{33,97},{65,1},{97,33},{2,66}... | collective-permute-start | bytes 589832 | tf_op jit(solution)/shard_map/ppermute | solution.py:17
  151.6 1.7 copy.14
  153.3 2.6 %collective-permute-start.22 = (f32[384,128]{1,0:T(8,128)}, f32[384,128]{1,0:T(8,128)}, u32[]{:S(2)}, u32[]{:S(2)}) collective-permute-start(f32[384,128]{1,0:T(8,128)} %bitcast.159), channel_id=1, source_target_pairs={{0,32},{32,64},{64,96},{96,0},{1,33},{33,65},{65,97},{97,1},{2,34}... | collective-permute-start | bytes 589832 | tf_op jit(solution)/shard_map/ppermute | solution.py:17
  156.0 3.5 %convolution_add_fusion = f32[4,384,128]{1,2,0:T(8,128)} fusion(f32[4,384,128]{1,2,0:T(8,128)} %collective-permute-done.26, f32[416,128]{1,0:T(8,128)S(1)} %broadcast_select_fusion, f32[416,128]{1,0:T(8,128)} %collective-permute-done.25, pred[]{:T(512)S(6)} %eq.32, f32[4,416,128]{2,1,0:T(8,128)} %bitcast.39, f32[4,416,128]{2,1,0:T(8,128)} %bitcast.26, ...), kind=kOutput, calls=%fused_computation.7 | convolution fusion | flops 492261376 | bytes 4554753 | tf_op jit(solution)/shard_map/xkm,kn->xmn/dot_general | solution.py:78
  159.4 1.8 copy.15
  161.2 1.7 copy.12
  166.2 1.4 collective-permute-start.27
  167.7 1.8 collective-permute-start.28
  171.6 5.8 %collective-permute-done.23 = f32[384,128]{1,0:T(8,128)S(1)} collective-permute-done((f32[384,128]{1,0:T(8,128)}, f32[384,128]{1,0:T(8,128)S(1)}, u32[]{:S(2)}, u32[]{:S(2)}) %collective-permute-start.23) | collective-permute-done | bytes 196640 | tf_op jit(solution)/shard_map/ppermute | solution.py:17
  178.6 2.1 %collective-permute-done.29 = f32[384,128]{1,0:T(8,128)S(1)} collective-permute-done((f32[384,128]{1,0:T(8,128)S(1)}, f32[384,128]{1,0:T(8,128)S(1)}, u32[]{:S(2)}, u32[]{:S(2)}) %collective-permute-start.29) | collective-permute-done | bytes 196640 | tf_op jit(solution)/shard_map/ppermute | solution.py:17
  (102 shorter events, 31.0 us)
Async XLA Ops:
  0.0 1.7 copy-start
  1.7 6.8 %copy-start.4 = (f32[2,384,768]{2,1,0:T(8,128)S(1)}, f32[2,384,768]{2,1,0:T(8,128)}, u32[]{:S(2)}) copy-start(f32[2,384,768]{2,1,0:T(8,128)} %param.2) | copy-start | bytes 7077892
  4.1 4.3 %copy-start.3 = (f32[2,128,800]{1,2,0:T(8,128)}, f32[2,128,800]{1,2,0:T(8,128)S(1)}, u32[]{:S(2)}) copy-start(f32[2,128,800]{1,2,0:T(8,128)S(1)} %fusion.4) | copy-start | bytes 2457604
  5.1 11.1 %collective-permute-start = (f32[400,128]{1,0:T(8,128)}, f32[400,128]{1,0:T(8,128)}, u32[]{:S(2)}, u32[]{:S(2)}) collective-permute-start(f32[400,128]{1,0:T(8,128)} %get-tuple-element.5), channel_id=1, source_target_pairs={{0,2},{1,3},{2,0},{3,1},{4,6},{5,7},{6,4},{7,5},{8,10},{9,11},{10,... | collective-permute-start | bytes 614408 | tf_op jit(solution)/shard_map/ppermute | solution.py:17
  6.3 10.5 %collective-permute-start.1 = (f32[400,128]{1,0:T(8,128)}, f32[400,128]{1,0:T(8,128)}, u32[]{:S(2)}, u32[]{:S(2)}) collective-permute-start(f32[400,128]{1,0:T(8,128)} %get-tuple-element.7), channel_id=1, source_target_pairs={{0,1},{1,2},{2,3},{3,0},{4,5},{5,6},{6,7},{7,4},{8,9},{9,10},{10,1... | collective-permute-start | bytes 614408 | tf_op jit(solution)/shard_map/ppermute | solution.py:17
  8.5 11.6 %collective-permute-start.2 = (f32[400,128]{1,0:T(8,128)}, f32[400,128]{1,0:T(8,128)}, u32[]{:S(2)}, u32[]{:S(2)}) collective-permute-start(f32[400,128]{1,0:T(8,128)} %get-tuple-element.6), channel_id=1, source_target_pairs={{0,3},{1,0},{2,1},{3,2},{4,7},{5,4},{6,5},{7,6},{8,11},{9,8},{10,9... | collective-permute-start | bytes 614408 | tf_op jit(solution)/shard_map/ppermute | solution.py:17
  9.7 3.0 %copy-start.2 = (f32[2,128,800]{1,2,0:T(8,128)}, f32[2,128,800]{1,2,0:T(8,128)S(1)}, u32[]{:S(2)}) copy-start(f32[2,128,800]{1,2,0:T(8,128)S(1)} %fusion.2) | copy-start | bytes 2457604
  10.6 14.7 %collective-permute-start.4 = (f32[400,128]{1,0:T(8,128)}, f32[400,128]{1,0:T(8,128)S(1)}, u32[]{:S(2)}, u32[]{:S(2)}) collective-permute-start(f32[400,128]{1,0:T(8,128)} %get-tuple-element.8), channel_id=1, source_target_pairs={{0,2},{1,3},{2,0},{3,1},{4,6},{5,7},{6,4},{7,5},{8,10},{9,11},{10,... | collective-permute-start | bytes 614408 | tf_op jit(solution)/shard_map/ppermute | solution.py:17
  12.7 12.8 %collective-permute-start.5 = (f32[400,128]{1,0:T(8,128)}, f32[400,128]{1,0:T(8,128)}, u32[]{:S(2)}, u32[]{:S(2)}) collective-permute-start(f32[400,128]{1,0:T(8,128)} %get-tuple-element.10), channel_id=1, source_target_pairs={{0,1},{1,2},{2,3},{3,0},{4,5},{5,6},{6,7},{7,4},{8,9},{9,10},{10,1... | collective-permute-start | bytes 614408 | tf_op jit(solution)/shard_map/ppermute | solution.py:17
  15.2 24.4 %copy-start.1 = (f32[2,128,800]{1,2,0:T(8,128)}, f32[2,128,800]{1,2,0:T(8,128)S(1)}, u32[]{:S(2)}) copy-start(f32[2,128,800]{1,2,0:T(8,128)S(1)} %fusion) | copy-start | bytes 2457604
  16.1 16.6 %collective-permute-start.6 = (f32[400,128]{1,0:T(8,128)}, f32[400,128]{1,0:T(8,128)S(1)}, u32[]{:S(2)}, u32[]{:S(2)}) collective-permute-start(f32[400,128]{1,0:T(8,128)} %get-tuple-element.9), channel_id=1, source_target_pairs={{0,3},{1,0},{2,1},{3,2},{4,7},{5,4},{6,5},{7,6},{8,11},{9,8},{10,9... | collective-permute-start | bytes 614408 | tf_op jit(solution)/shard_map/ppermute | solution.py:17
  16.9 35.2 %collective-permute-start.10 = (f32[400,128]{1,0:T(8,128)}, f32[400,128]{1,0:T(8,128)}, u32[]{:S(2)}, u32[]{:S(2)}) collective-permute-start(f32[400,128]{1,0:T(8,128)} %get-tuple-element.12), channel_id=1, source_target_pairs={{0,3},{1,0},{2,1},{3,2},{4,7},{5,4},{6,5},{7,6},{8,11},{9,8},{10,9... | collective-permute-start | bytes 614408 | tf_op jit(solution)/shard_map/ppermute | solution.py:17
  20.1 32.0 %collective-permute-start.8 = (f32[400,128]{1,0:T(8,128)}, f32[400,128]{1,0:T(8,128)}, u32[]{:S(2)}, u32[]{:S(2)}) collective-permute-start(f32[400,128]{1,0:T(8,128)} %get-tuple-element.11), channel_id=1, source_target_pairs={{0,2},{1,3},{2,0},{3,1},{4,6},{5,7},{6,4},{7,5},{8,10},{9,11},{10,... | collective-permute-start | bytes 614408 | tf_op jit(solution)/shard_map/ppermute | solution.py:17
  25.3 7.4 %copy-start.12 = (f32[400,128]{1,0:T(8,128)}, f32[400,128]{1,0:T(8,128)S(1)}, u32[]{:S(2)}) copy-start(f32[400,128]{1,0:T(8,128)S(1)} %collective-permute-done.4) | copy-start | bytes 614404
  25.3 26.9 %collective-permute-start.9 = (f32[400,128]{1,0:T(8,128)}, f32[400,128]{1,0:T(8,128)}, u32[]{:S(2)}, u32[]{:S(2)}) collective-permute-start(f32[400,128]{1,0:T(8,128)} %get-tuple-element.13), channel_id=1, source_target_pairs={{0,1},{1,2},{2,3},{3,0},{4,5},{5,6},{6,7},{7,4},{8,9},{9,10},{10,1... | collective-permute-start | bytes 614408 | tf_op jit(solution)/shard_map/ppermute | solution.py:17
  25.5 13.9 %collective-permute-start.3 = (f32[400,128]{1,0:T(8,128)S(1)}, f32[400,128]{1,0:T(8,128)S(1)}, u32[]{:S(2)}, u32[]{:S(2)}) collective-permute-start(f32[400,128]{1,0:T(8,128)S(1)} %fusion.29), channel_id=1, source_target_pairs={{0,4},{4,0},{1,5},{5,1},{2,6},{6,2},{3,7},{7,3},{8,12},{12,8},{9,1... | collective-permute-start | bytes 614408 | tf_op jit(solution)/shard_map/ppermute | solution.py:12
  33.9 26.7 %collective-permute-start.7 = (f32[400,128]{1,0:T(8,128)S(1)}, f32[400,128]{1,0:T(8,128)}, u32[]{:S(2)}, u32[]{:S(2)}) collective-permute-start(f32[400,128]{1,0:T(8,128)S(1)} %fusion.27), channel_id=1, source_target_pairs={{0,4},{4,0},{1,5},{5,1},{2,6},{6,2},{3,7},{7,3},{8,12},{12,8},{9,1... | collective-permute-start | bytes 614408 | tf_op jit(solution)/shard_map/ppermute | solution.py:12
  40.5 21.1 %all-to-all-start = ((f32[16,104,128]{2,1,0:T(8,128)}), f32[16,104,128]{2,1,0:T(8,128)S(1)}, u32[]{:S(2)}, u32[]{:S(2)}) async-start(f32[16,104,128]{2,1,0:T(8,128)} %bitcast.148), calls=%async_computation | async-start | bytes 1703936 | tf_op jit(solution)/shard_map/all_to_all | solution.py:64
  54.1 15.8 %collective-permute-start.11 = (f32[400,128]{1,0:T(8,128)}, f32[400,128]{1,0:T(8,128)}, u32[]{:S(2)}, u32[]{:S(2)}) collective-permute-start(f32[400,128]{1,0:T(8,128)} %fusion.25), channel_id=1, source_target_pairs={{0,4},{4,0},{1,5},{5,1},{2,6},{6,2},{3,7},{7,3},{8,12},{12,8},{9,1... | collective-permute-start | bytes 614408 | tf_op jit(solution)/shard_map/ppermute | solution.py:12
  62.6 15.5 %all-to-all-start.1 = ((f32[16,104,128]{2,1,0:T(8,128)}), f32[16,104,128]{2,1,0:T(8,128)}, u32[]{:S(2)}, u32[]{:S(2)}) async-start(f32[16,104,128]{2,1,0:T(8,128)} %bitcast.149), calls=%async_computation.1 | async-start | bytes 1703936 | tf_op jit(solution)/shard_map/all_to_all | solution.py:64
  79.2 16.2 %all-to-all-start.2 = ((f32[16,104,128]{2,1,0:T(8,128)}), f32[16,104,128]{2,1,0:T(8,128)}, u32[]{:S(2)}, u32[]{:S(2)}) async-start(f32[16,104,128]{2,1,0:T(8,128)} %bitcast.147), calls=%async_computation.2 | async-start | bytes 1703936 | tf_op jit(solution)/shard_map/all_to_all | solution.py:64
  87.8 12.2 %collective-permute-start.12 = (f32[416,128]{1,0:T(8,128)}, f32[416,128]{1,0:T(8,128)}, u32[]{:S(2)}, u32[]{:S(2)}) collective-permute-start(f32[416,128]{1,0:T(8,128)} %dynamic-slice_bitcast_fusion.2), channel_id=1, source_target_pairs={{0,24},{16,9},{25,1},{9,16},{2,26},{18,11},{27,3},{11,18},{4,28},{... | collective-permute-start | bytes 638984 | tf_op jit(solution)/shard_map/ppermute | solution.py:40
  90.7 15.3 %collective-permute-start.18 = (f32[416,128]{1,0:T(8,128)}, f32[416,128]{1,0:T(8,128)S(1)}, u32[]{:S(2)}, u32[]{:S(2)}) collective-permute-start(f32[416,128]{1,0:T(8,128)} %dynamic-slice_bitcast_fusion.1), channel_id=1, source_target_pairs={{0,24},{16,9},{25,1},{9,16},{2,26},{18,11},{27,3},{11,18},{4,28},{... | collective-permute-start | bytes 638984 | tf_op jit(solution)/shard_map/ppermute | solution.py:40
  96.3 16.8 %collective-permute-start.24 = (f32[416,128]{1,0:T(8,128)S(1)}, f32[416,128]{1,0:T(8,128)S(1)}, u32[]{:S(2)}, u32[]{:S(2)}) collective-permute-start(f32[416,128]{1,0:T(8,128)S(1)} %dynamic-slice_bitcast_fusion), channel_id=1, source_target_pairs={{0,24},{16,9},{25,1},{9,16},{2,26},{18,11},{27,3},{11,18},{4,28},{... | collective-permute-start | bytes 638984 | tf_op jit(solution)/shard_map/ppermute | solution.py:40
  100.9 13.2 %copy-start.6 = (f32[416,128]{1,0:T(8,128)}, f32[416,128]{1,0:T(8,128)S(1)}, u32[]{:S(2)}) copy-start(f32[416,128]{1,0:T(8,128)S(1)} %broadcast_select_fusion.2) | copy-start | bytes 638980
  100.9 8.9 %collective-permute-start.13 = (f32[416,128]{1,0:T(8,128)S(1)}, f32[416,128]{1,0:T(8,128)S(1)}, u32[]{:S(2)}, u32[]{:S(2)}) collective-permute-start(f32[416,128]{1,0:T(8,128)S(1)} %broadcast_select_fusion.2), channel_id=1, source_target_pairs={{0,8},{8,0},{16,24},{24,16},{1,9},{9,1},{17,25},{25,17},{2,10},{10... | collective-permute-start | bytes 638984 | tf_op jit(solution)/shard_map/ppermute | solution.py:74
  107.0 13.1 %copy-start.5 = (f32[416,128]{1,0:T(8,128)}, f32[416,128]{1,0:T(8,128)S(1)}, u32[]{:S(2)}) copy-start(f32[416,128]{1,0:T(8,128)S(1)} %broadcast_select_fusion.1) | copy-start | bytes 638980
  107.0 9.2 %collective-permute-start.19 = (f32[416,128]{1,0:T(8,128)S(1)}, f32[416,128]{1,0:T(8,128)S(1)}, u32[]{:S(2)}, u32[]{:S(2)}) collective-permute-start(f32[416,128]{1,0:T(8,128)S(1)} %broadcast_select_fusion.1), channel_id=1, source_target_pairs={{0,8},{8,0},{16,24},{24,16},{1,9},{9,1},{17,25},{25,17},{2,10},{10... | collective-permute-start | bytes 638984 | tf_op jit(solution)/shard_map/ppermute | solution.py:74
  109.9 10.2 %copy-start.9 = (f32[416,128]{1,0:T(8,128)}, f32[416,128]{1,0:T(8,128)S(1)}, u32[]{:S(2)}) copy-start(f32[416,128]{1,0:T(8,128)S(1)} %collective-permute-done.13) | copy-start | bytes 638980
  113.1 12.3 %collective-permute-start.14 = (f32[4,384,128]{1,2,0:T(8,128)}, f32[4,384,128]{1,2,0:T(8,128)}, u32[]{:S(2)}, u32[]{:S(2)}) collective-permute-start(f32[4,384,128]{1,2,0:T(8,128)} %fusion.15), channel_id=1, source_target_pairs={{0,128},{128,0},{1,129},{129,1},{2,130},{130,2},{3,131},{131,3},{4... | collective-permute-start | bytes 2359304 | tf_op jit(solution)/shard_map/ppermute | solution.py:12
  114.1 8.1 %collective-permute-start.25 = (f32[416,128]{1,0:T(8,128)S(1)}, f32[416,128]{1,0:T(8,128)}, u32[]{:S(2)}, u32[]{:S(2)}) collective-permute-start(f32[416,128]{1,0:T(8,128)S(1)} %broadcast_select_fusion), channel_id=1, source_target_pairs={{0,8},{8,0},{16,24},{24,16},{1,9},{9,1},{17,25},{25,17},{2,10},{10... | collective-permute-start | bytes 638984 | tf_op jit(solution)/shard_map/ppermute | solution.py:74
  116.2 0.7 copy-start.8
  120.1 24.2 %collective-permute-start.20 = (f32[4,384,128]{1,2,0:T(8,128)}, f32[4,384,128]{1,2,0:T(8,128)}, u32[]{:S(2)}, u32[]{:S(2)}) collective-permute-start(f32[4,384,128]{1,2,0:T(8,128)} %fusion.12), channel_id=1, source_target_pairs={{0,128},{128,0},{1,129},{129,1},{2,130},{130,2},{3,131},{131,3},{4... | collective-permute-start | bytes 2359304 | tf_op jit(solution)/shard_map/ppermute | solution.py:12
  120.3 5.1 %copy-start.7 = (f32[416,128]{1,0:T(8,128)S(1)}, f32[416,128]{1,0:T(8,128)}, u32[]{:S(2)}) copy-start(f32[416,128]{1,0:T(8,128)} %copy-done.6) | copy-start | bytes 638980
  120.3 5.1 %copy-start.10 = (f32[416,128]{1,0:T(8,128)S(1)}, f32[416,128]{1,0:T(8,128)}, u32[]{:S(2)}) copy-start(f32[416,128]{1,0:T(8,128)} %copy-done.9) | copy-start | bytes 638980
  125.4 27.9 %collective-permute-start.26 = (f32[4,384,128]{1,2,0:T(8,128)}, f32[4,384,128]{1,2,0:T(8,128)}, u32[]{:S(2)}, u32[]{:S(2)}) collective-permute-start(f32[4,384,128]{1,2,0:T(8,128)} %fusion.9), channel_id=1, source_target_pairs={{0,128},{128,0},{1,129},{129,1},{2,130},{130,2},{3,131},{131,3},{4... | collective-permute-start | bytes 2359304 | tf_op jit(solution)/shard_map/ppermute | solution.py:12
  130.7 35.5 %collective-permute-start.15 = (f32[384,128]{1,0:T(8,128)}, f32[384,128]{1,0:T(8,128)}, u32[]{:S(2)}, u32[]{:S(2)}) collective-permute-start(f32[384,128]{1,0:T(8,128)} %bitcast.158), channel_id=1, source_target_pairs={{0,64},{32,96},{64,0},{96,32},{1,65},{33,97},{65,1},{97,33},{2,66}... | collective-permute-start | bytes 589832 | tf_op jit(solution)/shard_map/ppermute | solution.py:17
  133.7 32.5 %collective-permute-start.16 = (f32[384,128]{1,0:T(8,128)}, f32[384,128]{1,0:T(8,128)}, u32[]{:S(2)}, u32[]{:S(2)}) collective-permute-start(f32[384,128]{1,0:T(8,128)} %bitcast.157), channel_id=1, source_target_pairs={{0,32},{32,64},{64,96},{96,0},{1,33},{33,65},{65,97},{97,1},{2,34}... | collective-permute-start | bytes 589832 | tf_op jit(solution)/shard_map/ppermute | solution.py:17
  140.5 27.2 %collective-permute-start.17 = (f32[384,128]{1,0:T(8,128)}, f32[384,128]{1,0:T(8,128)}, u32[]{:S(2)}, u32[]{:S(2)}) collective-permute-start(f32[384,128]{1,0:T(8,128)} %bitcast.156), channel_id=1, source_target_pairs={{0,96},{32,0},{64,32},{96,64},{1,97},{33,1},{65,33},{97,65},{2,98}... | collective-permute-start | bytes 589832 | tf_op jit(solution)/shard_map/ppermute | solution.py:17
  149.5 21.1 %collective-permute-start.21 = (f32[384,128]{1,0:T(8,128)}, f32[384,128]{1,0:T(8,128)}, u32[]{:S(2)}, u32[]{:S(2)}) collective-permute-start(f32[384,128]{1,0:T(8,128)} %bitcast.160), channel_id=1, source_target_pairs={{0,64},{32,96},{64,0},{96,32},{1,65},{33,97},{65,1},{97,33},{2,66}... | collective-permute-start | bytes 589832 | tf_op jit(solution)/shard_map/ppermute | solution.py:17
  153.3 18.2 %collective-permute-start.22 = (f32[384,128]{1,0:T(8,128)}, f32[384,128]{1,0:T(8,128)}, u32[]{:S(2)}, u32[]{:S(2)}) collective-permute-start(f32[384,128]{1,0:T(8,128)} %bitcast.159), channel_id=1, source_target_pairs={{0,32},{32,64},{64,96},{96,0},{1,33},{33,65},{65,97},{97,1},{2,34}... | collective-permute-start | bytes 589832 | tf_op jit(solution)/shard_map/ppermute | solution.py:17
  159.4 10.0 %copy-start.11 = (f32[1,384,128]{2,1,0:T(8,128)S(1)}, f32[1,384,128]{2,1,0:T(8,128)}, u32[]{:S(2)}) copy-start(f32[1,384,128]{2,1,0:T(8,128)} %copy.7) | copy-start | bytes 589828
  166.1 11.3 %collective-permute-start.23 = (f32[384,128]{1,0:T(8,128)}, f32[384,128]{1,0:T(8,128)S(1)}, u32[]{:S(2)}, u32[]{:S(2)}) collective-permute-start(f32[384,128]{1,0:T(8,128)} %bitcast.161), channel_id=1, source_target_pairs={{0,96},{32,0},{64,32},{96,64},{1,97},{33,1},{65,33},{97,65},{2,98}... | collective-permute-start | bytes 589832 | tf_op jit(solution)/shard_map/ppermute | solution.py:17
  166.2 12.3 %collective-permute-start.27 = (f32[384,128]{1,0:T(8,128)}, f32[384,128]{1,0:T(8,128)S(1)}, u32[]{:S(2)}, u32[]{:S(2)}) collective-permute-start(f32[384,128]{1,0:T(8,128)} %bitcast.164), channel_id=1, source_target_pairs={{0,64},{32,96},{64,0},{96,32},{1,65},{33,97},{65,1},{97,33},{2,66}... | collective-permute-start | bytes 589832 | tf_op jit(solution)/shard_map/ppermute | solution.py:17
  167.7 10.9 %collective-permute-start.28 = (f32[384,128]{1,0:T(8,128)}, f32[384,128]{1,0:T(8,128)S(1)}, u32[]{:S(2)}, u32[]{:S(2)}) collective-permute-start(f32[384,128]{1,0:T(8,128)} %bitcast.163), channel_id=1, source_target_pairs={{0,32},{32,64},{64,96},{96,0},{1,33},{33,65},{65,97},{97,1},{2,34}... | collective-permute-start | bytes 589832 | tf_op jit(solution)/shard_map/ppermute | solution.py:17
  170.6 10.1 %collective-permute-start.29 = (f32[384,128]{1,0:T(8,128)S(1)}, f32[384,128]{1,0:T(8,128)S(1)}, u32[]{:S(2)}, u32[]{:S(2)}) collective-permute-start(f32[384,128]{1,0:T(8,128)S(1)} %bitcast.162), channel_id=1, source_target_pairs={{0,96},{32,0},{64,32},{96,64},{1,97},{33,1},{65,33},{97,65},{2,98}... | collective-permute-start | bytes 589832 | tf_op jit(solution)/shard_map/ppermute | solution.py:17

commit v3 on v2

v3 whole, which is shorter than its diff:
```python
import functools

import jax
import jax.numpy as jnp
from jax import lax
from jax.experimental import pallas as pl
from jax.experimental.pallas import tpu as pltpu
from jax.sharding import Mesh, PartitionSpec as P

CHUNK = 128
SPLIT = (104, 96, 104, 96)
PADDED = 104
VMEM_LIMIT = 40 * 1024 * 1024


def halves(value):
    high = value.astype(jnp.bfloat16)
    low = (value - high.astype(jnp.float32)).astype(jnp.bfloat16)
    return high, low


def product(left, right):
    (lh, ll), (rh, rl) = left, right
    dot = functools.partial(jnp.dot, preferred_element_type=jnp.float32)
    return dot(lh, rh) + (dot(lh, rl) + dot(ll, rh))


def call(kernel, out_shape, spaces):
    vmem = pl.BlockSpec(memory_space=pltpu.VMEM)
    smem = pl.BlockSpec(memory_space=pltpu.SMEM)
    return pl.pallas_call(
        kernel,
        out_shape=out_shape,
        in_specs=[smem if s == "s" else vmem for s in spaces],
        out_specs=jax.tree.map(lambda _: vmem, out_shape),
        compiler_params=pltpu.CompilerParams(vmem_limit_bytes=VMEM_LIMIT),
    )


def f32(*shape):
    return jax.ShapeDtypeStruct(shape, jnp.float32)


def bf16(*shape):
    return jax.ShapeDtypeStruct(shape, jnp.bfloat16)


def half_kernel(here_ref, block_ref, coeff_ref, *outs):
    here = here_ref[0]
    coeff = halves(coeff_ref[...])
    size = outs[0].shape[0]
    for p in range(2):
        half = product(halves(block_ref[p]), coeff).T
        for part in range(2):
            piece = half[part * size : (part + 1) * size]
            distance = (2 * p + part - here + 4) % 4
            for d, out in enumerate(outs):

                @pl.when(distance == d)
                def _(out=out, piece=piece):
                    out[...] = piece


def left_kernel(value_ref, high_ref, low_ref):
    for x in range(4):
        high, low = halves(value_ref[x].T)
        high_ref[x] = high
        low_ref[x] = low


def give_kernel(*refs):
    *left, right_ref, out_ref = refs
    right = halves(right_ref[...])
    for c in range(len(left) // 2):
        for x in range(4):
            tile = product((left[2 * c][x], left[2 * c + 1][x]), right)
            out_ref[x, c * CHUNK : (c + 1) * CHUNK] = tile


def keep_kernel(here_ref, *refs):
    left, right_ref, given_ref, outs = refs[:6], refs[6], refs[7], refs[8:]
    here = here_ref[0]
    right = halves(right_ref[...])
    for c in range(len(left) // 2):
        rows = slice(c * CHUNK, (c + 1) * CHUNK)
        for d, out in enumerate(outs):
            x = (here + d) % 4
            tile = product((left[2 * c][x], left[2 * c + 1][x]), right)
            out[rows] = tile + given_ref[x, rows]


def swapped(value, axis):
    return lax.ppermute(value, axis, [(0, 1), (1, 0)])


def shifted(value, axis, distance):
    size = lax.axis_size(axis)
    return lax.ppermute(value, axis, [(i, (i + distance) % size) for i in range(size)])


def tie(value, *others):
    return lax.optimization_barrier((value,) + others)[0]


def crossing(value):
    pairs = []
    for y in range(4):
        if y % 2 == 0:
            moves = {0: (3, y), 2: (1, y ^ 1)}
        else:
            moves = {3: (0, y), 1: (2, y ^ 1)}
        for z, (to_z, to_y) in moves.items():
            pairs.append((z * 4 + y, to_z * 4 + to_y))
    return lax.ppermute(value, ("zl", "y"), pairs)


def body(three_index, occupied):
    aux_here, rows, cols = three_index.shape
    nocc = occupied.shape[1]
    x_size, y_size = lax.axis_size("x"), lax.axis_size("y")
    aux, x, zl, zh, y = (lax.axis_index(a) for a in ("aux", "x", "zl", "zh", "y"))
    share = nocc * aux_here // y_size
    chunks = rows // CHUNK
    x_here, y_here = (a.astype(jnp.int32).reshape(1) for a in (x, y))

    half_call = call(half_kernel, [f32(share, CHUNK)] * 4, "svv")
    left_call = call(left_kernel, [bf16(4, CHUNK, 4 * PADDED)] * 2, "v")
    give_call = call(give_kernel, f32(4, rows, CHUNK), "v" * 7)
    keep_call = call(keep_kernel, [f32(rows, CHUNK)] * 4, "s" + "v" * 8)

    sends = []
    for c in range(chunks):
        block = three_index[:, c * CHUNK : (c + 1) * CHUNK]
        if c:
            block = tie(block, sends[-1][0])
        sends.append(half_call(y_here, block, occupied))

    sums, pieces_of = [], []
    for c in range(chunks):
        own, one, two, three = sends[c]
        if c >= 2:
            two = tie(two, sums[c - 2])
        far = shifted(two, "y", 2)
        if c >= 1:
            one, three = tie(one, sums[c - 1]), tie(three, sums[c - 1])
        total = own + far + shifted(one, "y", 1) + shifted(three, "y", 3)
        sums.append(total)
    gathered = []
    for c in range(chunks):
        part = sums[c] + swapped(sums[c], "zh")
        pieces, at = [], 0
        for size in SPLIT:
            pieces.append(jnp.pad(part[at : at + size], ((0, PADDED - size), (0, 0))))
            at += size
        pieces = jnp.broadcast_to(jnp.stack(pieces)[:, None], (x_size, y_size, PADDED, CHUNK))
        pieces = pieces.reshape(x_size * y_size, PADDED, CHUNK)
        pieces = lax.all_to_all(pieces, ("x", "y"), 0, 0, tiled=True)
        gathered.append(pieces.reshape(x_size, y_size * PADDED, CHUNK))
    left = [a for piece in gathered for a in left_call(piece)]

    home = (zl // 2) == (y % 2)
    which = (zl + zl // 2 + y) % 2
    arrived = []
    for piece in gathered:
        mine = lax.dynamic_index_in_dim(piece, 2 * zh + y // 2, 0, keepdims=False)
        have = jnp.where(home, mine, crossing(mine))
        other = lax.ppermute(have, "zl", [(0, 1), (1, 0), (2, 3), (3, 2)])
        keep = jnp.where(which == aux, have, other)
        give = jnp.where(which == aux, other, have)
        given = swapped(give_call(*left, give), "aux")
        own, one, two, three = keep_call(x_here, *left, keep, given)
        arrived.append((own, shifted(two, "x", 2), shifted(one, "x", 1), shifted(three, "x", 3)))
    return jnp.concatenate([a + b + c + d for a, b, c, d in arrived], axis=-1)


def solution(mesh):
    fine = Mesh(mesh.devices.reshape(2, 4, 4, 2, 4), ("aux", "x", "zl", "zh", "y"))
    in_specs = (P("aux", ("x", "zl"), ("zh", "y")), P(("zh", "y"), None))
    out_specs = P(("x", "zl"), ("zh", "y", "aux"))
    return jax.shard_map(body, mesh=fine, in_specs=in_specs, out_specs=out_specs, check_vma=False)
```

time: 183 us -> 169 us (0.923)
  the two profiles are of different devices: /device:TPU:26 before, /device:TPU:1 now
where the time goes in v3:
time: 169 us; the launch traced here: 168 us
  starting transfers between devices  77.6 us (46%)
  waiting for transfers between devices  48.2 us (29%)
  Pallas kernels  23 us (14%)
  local copies, waits for them, and re-layouts  11.7 us (7%)
  other arithmetic  7.12 us (4%)
    ppermute x6, starting transfers between devices, swapped(): return lax.ppermute(value, axis, [(0, 1), (1, 0)])  27.3 us
    ppermute x18, starting transfers between devices, shifted(): lax.ppermute(value, axis, [(i, (i + distance) % size) for i in range(size)])  26 us
    ppermute x18, waiting for transfers between devices, shifted(): lax.ppermute(value, axis, [(i, (i + distance) % size) for i in range(size)])  23.9 us
    all_to_all x3, waiting for transfers between devices, body(): pieces = lax.all_to_all(pieces, ('x', 'y'), 0, 0, tiled=True)  20.5 us
    all_to_all x3, starting transfers between devices, body(): pieces = lax.all_to_all(pieces, ('x', 'y'), 0, 0, tiled=True)  18.1 us
    pallas_call x3, Pallas kernels, body(): own, one, two, three = keep_call(x_here, *left, keep, given)  7.59 us
    pallas_call x3, Pallas kernels, body(): given = swapped(give_call(*left, give), 'aux')  6.9 us
    pallas_call x3, Pallas kernels, body(): sends.append(half_call(y_here, block, occupied))  6.31 us
  transfers between devices with their start and end apart: 33, of which 12 were waited for; matrix products, arithmetic and copies ran while one was open for 6% of the time, Pallas kernels for 13%

profile of v3, /device:TPU:1, one launch (start us, length us, event | category | flops | bytes accessed | tf_op | source)
XLA Modules:
  0.0 168.1 jit_solution(927544408384791634)
XLA Ops:
  0.0 2.2 %copy.3.coeff_ref = f32[768,800]{1,0:T(8,128)S(1)} copy(f32[768,800]{0,1:T(8,128)} %param.3) | data formatting | bytes 4915200 | tf_op args[1]
  2.2 1.8 %fusion = (f32[2,128,768]{2,1,0:T(8,128)S(1)}, f32[2,128,768]{2,1,0:T(8,128)S(1)}, f32[2,128,768]{2,1,0:T(8,128)S(1)}) fusion(f32[2,384,768]{2,1,0:T(8,128)} %param.2), kind=kLoop, calls=%fused_computation.34 | loop fusion | bytes 4718592 | tf_op jit(solution)/shard_map/slice | solution.py:133
  4.0 1.9 %shard_map.28 = (f32[400,128]{1,0:T(8,128)S(1)}, f32[400,128]{1,0:T(8,128)S(1)}, f32[400,128]{1,0:T(8,128)S(1)}, f32[400,128]{1,0:T(8,128)S(1)}) custom-call(s32[1]{0:T(128)} %bitcast.1.here_ref, f32[2,128,768]{2,1,0:T(8,128)S(1)} %get-tuple-element.80.block_ref, f32[768,800]{1,0:T(8,128)S(1)} %copy.3.coeff_ref), custom_call_target="tpu_custom_call" | custom-call | tf_op jit(solution)/shard_map/pallas_call | solution.py:136
  5.8 3.8 %collective-permute-start = (f32[400,128]{1,0:T(8,128)S(1)}, f32[400,128]{1,0:T(8,128)S(1)}, u32[]{:S(2)}, u32[]{:S(2)}) collective-permute-start(f32[400,128]{1,0:T(8,128)S(1)} %get-tuple-element.43), channel_id=1, source_target_pairs={{0,2},{1,3},{2,0},{3,1},{4,6},{5,7},{6,4},{7,5},{8,10},{9,11},{10,... | collective-permute-start | bytes 614408 | tf_op jit(solution)/shard_map/ppermute | solution.py:98
  10.1 2.3 %collective-permute-start.2 = (f32[400,128]{1,0:T(8,128)S(1)}, f32[400,128]{1,0:T(8,128)S(1)}, u32[]{:S(2)}, u32[]{:S(2)}) collective-permute-start(f32[400,128]{1,0:T(8,128)S(1)} %get-tuple-element.45), channel_id=1, source_target_pairs={{0,3},{1,0},{2,1},{3,2},{4,7},{5,4},{6,5},{7,6},{8,11},{9,8},{10,9... | collective-permute-start | bytes 614408 | tf_op jit(solution)/shard_map/ppermute | solution.py:98
  12.3 1.2 collective-permute-done
  13.5 5.7 %collective-permute-done.1 = f32[400,128]{1,0:T(8,128)S(1)} collective-permute-done((f32[400,128]{1,0:T(8,128)S(1)}, f32[400,128]{1,0:T(8,128)S(1)}, u32[]{:S(2)}, u32[]{:S(2)}) %collective-permute-start.1) | collective-permute-done | bytes 204832 | tf_op jit(solution)/shard_map/ppermute | solution.py:98
  19.3 7.0 %collective-permute-start.3 = (f32[400,128]{1,0:T(8,128)S(1)}, f32[400,128]{1,0:T(8,128)S(1)}, u32[]{:S(2)}, u32[]{:S(2)}) collective-permute-start(f32[400,128]{1,0:T(8,128)S(1)} %add_add_fusion.2), channel_id=1, source_target_pairs={{0,4},{4,0},{1,5},{5,1},{2,6},{6,2},{3,7},{7,3},{8,12},{12,8},{9,1... | collective-permute-start | bytes 614408 | tf_op jit(solution)/shard_map/ppermute | solution.py:93
  26.3 1.9 %shard_map.30 = (f32[400,128]{1,0:T(8,128)S(1)}, f32[400,128]{1,0:T(8,128)S(1)}, f32[400,128]{1,0:T(8,128)S(1)}, f32[400,128]{1,0:T(8,128)S(1)}) custom-call(s32[1]{0:T(128)} %bitcast.1.here_ref, f32[2,128,768]{2,1,0:T(8,128)S(1)} %get-tuple-element.48.block_ref, f32[768,800]{1,0:T(8,128)S(1)} %copy.3.coeff_ref), custom_call_target="tpu_custom_call" | custom-call | tf_op jit(solution)/shard_map/pallas_call | solution.py:136
  28.2 1.8 %collective-permute-start.4 = (f32[400,128]{1,0:T(8,128)S(1)}, f32[400,128]{1,0:T(8,128)S(1)}, u32[]{:S(2)}, u32[]{:S(2)}) collective-permute-start(f32[400,128]{1,0:T(8,128)S(1)} %get-tuple-element.50), channel_id=1, source_target_pairs={{0,2},{1,3},{2,0},{3,1},{4,6},{5,7},{6,4},{7,5},{8,10},{9,11},{10,... | collective-permute-start | bytes 614408 | tf_op jit(solution)/shard_map/ppermute | solution.py:98
  30.0 2.6 %shard_map.32 = (f32[400,128]{1,0:T(8,128)S(1)}, f32[400,128]{1,0:T(8,128)S(1)}, f32[400,128]{1,0:T(8,128)}, f32[400,128]{1,0:T(8,128)S(1)}) custom-call(s32[1]{0:T(128)} %bitcast.1.here_ref, f32[2,128,768]{2,1,0:T(8,128)S(1)} %get-tuple-element.57.block_ref, f32[768,800]{1,0:T(8,128)S(1)} %copy.3.coeff_ref), custom_call_target="tpu_custom_call" | custom-call | tf_op jit(solution)/shard_map/pallas_call | solution.py:136
  32.6 1.5 collective-permute-start.5
  34.1 1.2 collective-permute-start.6
  36.2 3.1 %collective-permute-done.5 = f32[400,128]{1,0:T(8,128)S(1)} collective-permute-done((f32[400,128]{1,0:T(8,128)S(1)}, f32[400,128]{1,0:T(8,128)S(1)}, u32[]{:S(2)}, u32[]{:S(2)}) %collective-permute-start.5) | collective-permute-done | bytes 204832 | tf_op jit(solution)/shard_map/ppermute | solution.py:98
  40.0 4.5 %collective-permute-start.9 = (f32[400,128]{1,0:T(8,128)S(1)}, f32[400,128]{1,0:T(8,128)S(1)}, u32[]{:S(2)}, u32[]{:S(2)}) collective-permute-start(f32[400,128]{1,0:T(8,128)S(1)} %get-tuple-element.62), channel_id=1, source_target_pairs={{0,1},{1,2},{2,3},{3,0},{4,5},{5,6},{6,7},{7,4},{8,9},{9,10},{10,1... | collective-permute-start | bytes 614408 | tf_op jit(solution)/shard_map/ppermute | solution.py:98
  44.6 1.0 broadcast_in_dim.6
  45.6 5.7 %all-to-all-start = ((f32[16,104,128]{2,1,0:T(8,128)}), f32[16,104,128]{2,1,0:T(8,128)S(1)}, u32[]{:S(2)}, u32[]{:S(2)}) async-start(f32[16,104,128]{2,1,0:T(8,128)} %bitcast.6), calls=%async_computation | async-start | bytes 1703936 | tf_op jit(solution)/shard_map/all_to_all | solution.py:157
  51.4 5.1 %collective-permute-start.11 = (f32[400,128]{1,0:T(8,128)S(1)}, f32[400,128]{1,0:T(8,128)S(1)}, u32[]{:S(2)}, u32[]{:S(2)}) collective-permute-start(f32[400,128]{1,0:T(8,128)S(1)} %add_add_fusion), channel_id=1, source_target_pairs={{0,4},{4,0},{1,5},{5,1},{2,6},{6,2},{3,7},{7,3},{8,12},{12,8},{9,1... | collective-permute-start | bytes 614408 | tf_op jit(solution)/shard_map/ppermute | solution.py:93
  56.6 5.5 %all-to-all-done = f32[16,104,128]{2,1,0:T(8,128)S(1)} async-done(((f32[16,104,128]{2,1,0:T(8,128)}), f32[16,104,128]{2,1,0:T(8,128)S(1)}, u32[]{:S(2)}, u32[]{:S(2)}) %all-to-all-start) | async-done | bytes 852000 | tf_op jit(solution)/shard_map/all_to_all | solution.py:157
  62.1 1.0 broadcast_in_dim.7
  63.1 6.1 %all-to-all-start.1 = ((f32[16,104,128]{2,1,0:T(8,128)}), f32[16,104,128]{2,1,0:T(8,128)S(1)}, u32[]{:S(2)}, u32[]{:S(2)}) async-start(f32[16,104,128]{2,1,0:T(8,128)} %bitcast.12), calls=%async_computation.1 | async-start | bytes 1703936 | tf_op jit(solution)/shard_map/all_to_all | solution.py:157
  69.4 10.6 %all-to-all-done.1 = f32[16,104,128]{2,1,0:T(8,128)S(1)} async-done(((f32[16,104,128]{2,1,0:T(8,128)}), f32[16,104,128]{2,1,0:T(8,128)S(1)}, u32[]{:S(2)}, u32[]{:S(2)}) %all-to-all-start.1) | async-done | bytes 852000 | tf_op jit(solution)/shard_map/all_to_all | solution.py:157
  80.0 1.0 broadcast_in_dim.8
  81.0 6.2 %all-to-all-start.2 = ((f32[16,104,128]{2,1,0:T(8,128)}), f32[16,104,128]{2,1,0:T(8,128)}, u32[]{:S(2)}, u32[]{:S(2)}) async-start(f32[16,104,128]{2,1,0:T(8,128)} %bitcast.18), calls=%async_computation.2 | async-start | bytes 1703936 | tf_op jit(solution)/shard_map/all_to_all | solution.py:157
  87.3 1.3 collective-permute-start.12
  89.0 1.1 copy-done.1
  91.2 2.0 %collective-permute-start.18 = (f32[416,128]{1,0:T(8,128)}, f32[416,128]{1,0:T(8,128)}, u32[]{:S(2)}, u32[]{:S(2)}) collective-permute-start(f32[416,128]{1,0:T(8,128)} %dynamic-slice_bitcast_fusion.1), channel_id=1, source_target_pairs={{0,24},{16,9},{25,1},{9,16},{2,26},{18,11},{27,3},{11,18},{4,28},{... | collective-permute-start | bytes 638984 | tf_op jit(solution)/shard_map/ppermute | solution.py:114
  93.9 4.4 %all-to-all-done.2 = f32[16,104,128]{2,1,0:T(8,128)} async-done(((f32[16,104,128]{2,1,0:T(8,128)}), f32[16,104,128]{2,1,0:T(8,128)}, u32[]{:S(2)}, u32[]{:S(2)}) %all-to-all-start.2) | async-done | bytes 852000 | tf_op jit(solution)/shard_map/all_to_all | solution.py:157
  98.3 1.5 shard_map.33
  100.8 2.2 %collective-permute-start.24 = (f32[416,128]{1,0:T(8,128)S(1)}, f32[416,128]{1,0:T(8,128)S(1)}, u32[]{:S(2)}, u32[]{:S(2)}) collective-permute-start(f32[416,128]{1,0:T(8,128)S(1)} %dynamic-slice_bitcast_fusion), channel_id=1, source_target_pairs={{0,24},{16,9},{25,1},{9,16},{2,26},{18,11},{27,3},{11,18},{4,28},{... | collective-permute-start | bytes 638984 | tf_op jit(solution)/shard_map/ppermute | solution.py:114
  103.0 1.0 broadcast_select_fusion.1
  104.6 1.8 %broadcast_select_fusion.7 = (f32[416,128]{1,0:T(8,128)S(1)}, f32[416,128]{1,0:T(8,128)}) fusion(f32[416,128]{1,0:T(8,128)} %collective-permute-done.13, f32[416,128]{1,0:T(8,128)} %broadcast_select_fusion.2, pred[]{:T(512)S(6)} %eq.7), kind=kLoop, calls=%fused_computation.20 | loop fusion | flops 106496 | bytes 851969 | tf_op jit(solution)/shard_map/jit(_where)/select_n | solution.py:169
  106.4 2.3 %shard_map.34 = f32[4,384,128]{2,1,0:T(8,128)} custom-call(bf16[4,128,416]{2,1,0:T(8,128)(2,1)S(1)} %get-tuple-element.46.refs_0_, bf16[4,128,416]{2,1,0:T(8,128)(2,1)S(1)} %get-tuple-element.47.refs_1_, bf16[4,128,416]{2,1,0:T(8,128)(2,1)S(1)} %get-tuple-element.55.refs_2_, bf16[4,128,416]{2,1,0:T(8,128)(2,1)S(1)} %get-tuple-element.56.refs_3_, ...), custom_call_target="tpu_custom_call" | custom-call | tf_op jit(solution)/shard_map/pallas_call | solution.py:170
  108.7 13.9 %collective-permute-start.14 = (f32[4,384,128]{2,1,0:T(8,128)}, f32[4,384,128]{2,1,0:T(8,128)}, u32[]{:S(2)}, u32[]{:S(2)}) collective-permute-start(f32[4,384,128]{2,1,0:T(8,128)} %shard_map.34), channel_id=1, source_target_pairs={{0,128},{128,0},{1,129},{129,1},{2,130},{130,2},{3,131},{131,3},{4... | collective-permute-start | bytes 2359304 | tf_op jit(solution)/shard_map/ppermute | solution.py:93
  124.4 2.3 %shard_map.36 = f32[4,384,128]{2,1,0:T(8,128)} custom-call(bf16[4,128,416]{2,1,0:T(8,128)(2,1)S(1)} %get-tuple-element.46.refs_0_, bf16[4,128,416]{2,1,0:T(8,128)(2,1)S(1)} %get-tuple-element.47.refs_1_, bf16[4,128,416]{2,1,0:T(8,128)(2,1)S(1)} %get-tuple-element.55.refs_2_, bf16[4,128,416]{2,1,0:T(8,128)(2,1)S(1)} %get-tuple-element.56.refs_3_, ...), custom_call_target="tpu_custom_call" | custom-call | tf_op jit(solution)/shard_map/pallas_call | solution.py:170
  126.7 3.8 %collective-permute-done.25 = f32[416,128]{1,0:T(8,128)S(1)} collective-permute-done((f32[416,128]{1,0:T(8,128)S(1)}, f32[416,128]{1,0:T(8,128)S(1)}, u32[]{:S(2)}, u32[]{:S(2)}) %collective-permute-start.25) | collective-permute-done | bytes 213024 | tf_op jit(solution)/shard_map/ppermute | solution.py:167
  131.3 2.3 %shard_map.38 = f32[4,384,128]{2,1,0:T(8,128)} custom-call(bf16[4,128,416]{2,1,0:T(8,128)(2,1)S(1)} %get-tuple-element.46.refs_0_, bf16[4,128,416]{2,1,0:T(8,128)(2,1)S(1)} %get-tuple-element.47.refs_1_, bf16[4,128,416]{2,1,0:T(8,128)(2,1)S(1)} %get-tuple-element.55.refs_2_, bf16[4,128,416]{2,1,0:T(8,128)(2,1)S(1)} %get-tuple-element.56.refs_3_, ...), custom_call_target="tpu_custom_call" | custom-call | tf_op jit(solution)/shard_map/pallas_call | solution.py:170
  135.3 2.5 %shard_map.35 = (f32[384,128]{1,0:T(8,128)S(1)}, f32[384,128]{1,0:T(8,128)S(1)}, f32[384,128]{1,0:T(8,128)S(1)}, f32[384,128]{1,0:T(8,128)S(1)}) custom-call(s32[1]{0:T(128)} %bitcast.here_ref, bf16[4,128,416]{2,1,0:T(8,128)(2,1)S(1)} %get-tuple-element.46.refs_0_, bf16[4,128,416]{2,1,0:T(8,128)(2,1)S(1)} %get-tuple-element.47.refs_1_, ...), custom_call_target="tpu_custom_call" | custom-call | tf_op jit(solution)/shard_map/pallas_call | solution.py:171
  137.8 1.9 %collective-permute-start.15 = (f32[384,128]{1,0:T(8,128)S(1)}, f32[384,128]{1,0:T(8,128)S(1)}, u32[]{:S(2)}, u32[]{:S(2)}) collective-permute-start(f32[384,128]{1,0:T(8,128)S(1)} %get-tuple-element.68), channel_id=1, source_target_pairs={{0,64},{32,96},{64,0},{96,32},{1,65},{33,97},{65,1},{97,33},{2,66}... | collective-permute-start | bytes 589832 | tf_op jit(solution)/shard_map/ppermute | solution.py:98
  139.9 2.6 %collective-permute-start.17 = (f32[384,128]{1,0:T(8,128)S(1)}, f32[384,128]{1,0:T(8,128)S(1)}, u32[]{:S(2)}, u32[]{:S(2)}) collective-permute-start(f32[384,128]{1,0:T(8,128)S(1)} %get-tuple-element.70), channel_id=1, source_target_pairs={{0,96},{32,0},{64,32},{96,64},{1,97},{33,1},{65,33},{97,65},{2,98}... | collective-permute-start | bytes 589832 | tf_op jit(solution)/shard_map/ppermute | solution.py:98
  143.4 2.6 %shard_map.37 = (f32[384,128]{1,0:T(8,128)S(1)}, f32[384,128]{1,0:T(8,128)S(1)}, f32[384,128]{1,0:T(8,128)S(1)}, f32[384,128]{1,0:T(8,128)S(1)}) custom-call(s32[1]{0:T(128)} %bitcast.here_ref, bf16[4,128,416]{2,1,0:T(8,128)(2,1)S(1)} %get-tuple-element.46.refs_0_, bf16[4,128,416]{2,1,0:T(8,128)(2,1)S(1)} %get-tuple-element.47.refs_1_, ...), custom_call_target="tpu_custom_call" | custom-call | tf_op jit(solution)/shard_map/pallas_call | solution.py:171
  146.6 4.1 %collective-permute-done.16 = f32[384,128]{1,0:T(8,128)S(1)} collective-permute-done((f32[384,128]{1,0:T(8,128)S(1)}, f32[384,128]{1,0:T(8,128)S(1)}, u32[]{:S(2)}, u32[]{:S(2)}) %collective-permute-start.16) | collective-permute-done | bytes 196640 | tf_op jit(solution)/shard_map/ppermute | solution.py:98
  150.8 2.5 %shard_map.39 = (f32[384,128]{1,0:T(8,128)S(1)}, f32[384,128]{1,0:T(8,128)S(1)}, f32[384,128]{1,0:T(8,128)S(1)}, f32[384,128]{1,0:T(8,128)S(1)}) custom-call(s32[1]{0:T(128)} %bitcast.here_ref, bf16[4,128,416]{2,1,0:T(8,128)(2,1)S(1)} %get-tuple-element.46.refs_0_, bf16[4,128,416]{2,1,0:T(8,128)(2,1)S(1)} %get-tuple-element.47.refs_1_, ...), custom_call_target="tpu_custom_call" | custom-call | tf_op jit(solution)/shard_map/pallas_call | solution.py:171
  153.3 1.7 %collective-permute-start.27 = (f32[384,128]{1,0:T(8,128)S(1)}, f32[384,128]{1,0:T(8,128)S(1)}, u32[]{:S(2)}, u32[]{:S(2)}) collective-permute-start(f32[384,128]{1,0:T(8,128)S(1)} %get-tuple-element.76), channel_id=1, source_target_pairs={{0,64},{32,96},{64,0},{96,32},{1,65},{33,97},{65,1},{97,33},{2,66}... | collective-permute-start | bytes 589832 | tf_op jit(solution)/shard_map/ppermute | solution.py:98
  155.4 2.3 %collective-permute-start.29 = (f32[384,128]{1,0:T(8,128)S(1)}, f32[384,128]{1,0:T(8,128)S(1)}, u32[]{:S(2)}, u32[]{:S(2)}) collective-permute-start(f32[384,128]{1,0:T(8,128)S(1)} %get-tuple-element.78), channel_id=1, source_target_pairs={{0,96},{32,0},{64,32},{96,64},{1,97},{33,1},{65,33},{97,65},{2,98}... | collective-permute-start | bytes 589832 | tf_op jit(solution)/shard_map/ppermute | solution.py:98
  157.7 1.8 %collective-permute-done.22 = f32[384,128]{1,0:T(8,128)S(1)} collective-permute-done((f32[384,128]{1,0:T(8,128)S(1)}, f32[384,128]{1,0:T(8,128)S(1)}, u32[]{:S(2)}, u32[]{:S(2)}) %collective-permute-start.22) | collective-permute-done | bytes 196640 | tf_op jit(solution)/shard_map/ppermute | solution.py:98
  159.5 2.9 %collective-permute-done.27 = f32[384,128]{1,0:T(8,128)S(1)} collective-permute-done((f32[384,128]{1,0:T(8,128)S(1)}, f32[384,128]{1,0:T(8,128)S(1)}, u32[]{:S(2)}, u32[]{:S(2)}) %collective-permute-start.27) | collective-permute-done | bytes 196640 | tf_op jit(solution)/shard_map/ppermute | solution.py:98
  162.4 4.8 %collective-permute-done.28 = f32[384,128]{1,0:T(8,128)S(1)} collective-permute-done((f32[384,128]{1,0:T(8,128)S(1)}, f32[384,128]{1,0:T(8,128)S(1)}, u32[]{:S(2)}, u32[]{:S(2)}) %collective-permute-start.28) | collective-permute-done | bytes 196640 | tf_op jit(solution)/shard_map/ppermute | solution.py:98
  (76 shorter events, 13.4 us)
Async XLA Ops:
  5.8 7.7 %collective-permute-start = (f32[400,128]{1,0:T(8,128)S(1)}, f32[400,128]{1,0:T(8,128)S(1)}, u32[]{:S(2)}, u32[]{:S(2)}) collective-permute-start(f32[400,128]{1,0:T(8,128)S(1)} %get-tuple-element.43), channel_id=1, source_target_pairs={{0,2},{1,3},{2,0},{3,1},{4,6},{5,7},{6,4},{7,5},{8,10},{9,11},{10,... | collective-permute-start | bytes 614408 | tf_op jit(solution)/shard_map/ppermute | solution.py:98
  9.7 9.6 %collective-permute-start.1 = (f32[400,128]{1,0:T(8,128)S(1)}, f32[400,128]{1,0:T(8,128)S(1)}, u32[]{:S(2)}, u32[]{:S(2)}) collective-permute-start(f32[400,128]{1,0:T(8,128)S(1)} %get-tuple-element.44), channel_id=1, source_target_pairs={{0,1},{1,2},{2,3},{3,0},{4,5},{5,6},{6,7},{7,4},{8,9},{9,10},{10,1... | collective-permute-start | bytes 614408 | tf_op jit(solution)/shard_map/ppermute | solution.py:98
  10.1 9.2 %collective-permute-start.2 = (f32[400,128]{1,0:T(8,128)S(1)}, f32[400,128]{1,0:T(8,128)S(1)}, u32[]{:S(2)}, u32[]{:S(2)}) collective-permute-start(f32[400,128]{1,0:T(8,128)S(1)} %get-tuple-element.45), channel_id=1, source_target_pairs={{0,3},{1,0},{2,1},{3,2},{4,7},{5,4},{6,5},{7,6},{8,11},{9,8},{10,9... | collective-permute-start | bytes 614408 | tf_op jit(solution)/shard_map/ppermute | solution.py:98
  19.3 16.8 %collective-permute-start.3 = (f32[400,128]{1,0:T(8,128)S(1)}, f32[400,128]{1,0:T(8,128)S(1)}, u32[]{:S(2)}, u32[]{:S(2)}) collective-permute-start(f32[400,128]{1,0:T(8,128)S(1)} %add_add_fusion.2), channel_id=1, source_target_pairs={{0,4},{4,0},{1,5},{5,1},{2,6},{6,2},{3,7},{7,3},{8,12},{12,8},{9,1... | collective-permute-start | bytes 614408 | tf_op jit(solution)/shard_map/ppermute | solution.py:93
  28.2 8.0 %collective-permute-start.4 = (f32[400,128]{1,0:T(8,128)S(1)}, f32[400,128]{1,0:T(8,128)S(1)}, u32[]{:S(2)}, u32[]{:S(2)}) collective-permute-start(f32[400,128]{1,0:T(8,128)S(1)} %get-tuple-element.50), channel_id=1, source_target_pairs={{0,2},{1,3},{2,0},{3,1},{4,6},{5,7},{6,4},{7,5},{8,10},{9,11},{10,... | collective-permute-start | bytes 614408 | tf_op jit(solution)/shard_map/ppermute | solution.py:98
  32.6 6.7 %collective-permute-start.5 = (f32[400,128]{1,0:T(8,128)S(1)}, f32[400,128]{1,0:T(8,128)S(1)}, u32[]{:S(2)}, u32[]{:S(2)}) collective-permute-start(f32[400,128]{1,0:T(8,128)S(1)} %get-tuple-element.52), channel_id=1, source_target_pairs={{0,1},{1,2},{2,3},{3,0},{4,5},{5,6},{6,7},{7,4},{8,9},{9,10},{10,1... | collective-permute-start | bytes 614408 | tf_op jit(solution)/shard_map/ppermute | solution.py:98
  34.1 5.5 %collective-permute-start.6 = (f32[400,128]{1,0:T(8,128)S(1)}, f32[400,128]{1,0:T(8,128)S(1)}, u32[]{:S(2)}, u32[]{:S(2)}) collective-permute-start(f32[400,128]{1,0:T(8,128)S(1)} %get-tuple-element.54), channel_id=1, source_target_pairs={{0,3},{1,0},{2,1},{3,2},{4,7},{5,4},{6,5},{7,6},{8,11},{9,8},{10,9... | collective-permute-start | bytes 614408 | tf_op jit(solution)/shard_map/ppermute | solution.py:98
  35.3 16.1 %collective-permute-start.8 = (f32[400,128]{1,0:T(8,128)}, f32[400,128]{1,0:T(8,128)S(1)}, u32[]{:S(2)}, u32[]{:S(2)}) collective-permute-start(f32[400,128]{1,0:T(8,128)} %get-tuple-element.60), channel_id=1, source_target_pairs={{0,2},{1,3},{2,0},{3,1},{4,6},{5,7},{6,4},{7,5},{8,10},{9,11},{10,... | collective-permute-start | bytes 614408 | tf_op jit(solution)/shard_map/ppermute | solution.py:98
  39.6 16.9 %collective-permute-start.7 = (f32[400,128]{1,0:T(8,128)S(1)}, f32[400,128]{1,0:T(8,128)S(1)}, u32[]{:S(2)}, u32[]{:S(2)}) collective-permute-start(f32[400,128]{1,0:T(8,128)S(1)} %add_add_fusion.1), channel_id=1, source_target_pairs={{0,4},{4,0},{1,5},{5,1},{2,6},{6,2},{3,7},{7,3},{8,12},{12,8},{9,1... | collective-permute-start | bytes 614408 | tf_op jit(solution)/shard_map/ppermute | solution.py:93
  40.0 11.3 %collective-permute-start.9 = (f32[400,128]{1,0:T(8,128)S(1)}, f32[400,128]{1,0:T(8,128)S(1)}, u32[]{:S(2)}, u32[]{:S(2)}) collective-permute-start(f32[400,128]{1,0:T(8,128)S(1)} %get-tuple-element.62), channel_id=1, source_target_pairs={{0,1},{1,2},{2,3},{3,0},{4,5},{5,6},{6,7},{7,4},{8,9},{9,10},{10,1... | collective-permute-start | bytes 614408 | tf_op jit(solution)/shard_map/ppermute | solution.py:98
  44.6 6.8 %collective-permute-start.10 = (f32[400,128]{1,0:T(8,128)S(1)}, f32[400,128]{1,0:T(8,128)S(1)}, u32[]{:S(2)}, u32[]{:S(2)}) collective-permute-start(f32[400,128]{1,0:T(8,128)S(1)} %get-tuple-element.64), channel_id=1, source_target_pairs={{0,3},{1,0},{2,1},{3,2},{4,7},{5,4},{6,5},{7,6},{8,11},{9,8},{10,9... | collective-permute-start | bytes 614408 | tf_op jit(solution)/shard_map/ppermute | solution.py:98
  45.6 16.5 %all-to-all-start = ((f32[16,104,128]{2,1,0:T(8,128)}), f32[16,104,128]{2,1,0:T(8,128)S(1)}, u32[]{:S(2)}, u32[]{:S(2)}) async-start(f32[16,104,128]{2,1,0:T(8,128)} %bitcast.6), calls=%async_computation | async-start | bytes 1703936 | tf_op jit(solution)/shard_map/all_to_all | solution.py:157
  51.4 17.8 %collective-permute-start.11 = (f32[400,128]{1,0:T(8,128)S(1)}, f32[400,128]{1,0:T(8,128)S(1)}, u32[]{:S(2)}, u32[]{:S(2)}) collective-permute-start(f32[400,128]{1,0:T(8,128)S(1)} %add_add_fusion), channel_id=1, source_target_pairs={{0,4},{4,0},{1,5},{5,1},{2,6},{6,2},{3,7},{7,3},{8,12},{12,8},{9,1... | collective-permute-start | bytes 614408 | tf_op jit(solution)/shard_map/ppermute | solution.py:93
  63.1 16.9 %all-to-all-start.1 = ((f32[16,104,128]{2,1,0:T(8,128)}), f32[16,104,128]{2,1,0:T(8,128)S(1)}, u32[]{:S(2)}, u32[]{:S(2)}) async-start(f32[16,104,128]{2,1,0:T(8,128)} %bitcast.12), calls=%async_computation.1 | async-start | bytes 1703936 | tf_op jit(solution)/shard_map/all_to_all | solution.py:157
  80.0 9.0 %copy-start = (f32[16,104,128]{2,1,0:T(8,128)}, f32[16,104,128]{2,1,0:T(8,128)S(1)}, u32[]{:S(2)}) copy-start(f32[16,104,128]{2,1,0:T(8,128)S(1)} %all-to-all-done.1) | copy-start | bytes 2555908
  81.0 17.3 %all-to-all-start.2 = ((f32[16,104,128]{2,1,0:T(8,128)}), f32[16,104,128]{2,1,0:T(8,128)}, u32[]{:S(2)}, u32[]{:S(2)}) async-start(f32[16,104,128]{2,1,0:T(8,128)} %bitcast.18), calls=%async_computation.2 | async-start | bytes 1703936 | tf_op jit(solution)/shard_map/all_to_all | solution.py:157
  87.3 5.9 %collective-permute-start.12 = (f32[416,128]{1,0:T(8,128)S(1)}, f32[416,128]{1,0:T(8,128)S(1)}, u32[]{:S(2)}, u32[]{:S(2)}) collective-permute-start(f32[416,128]{1,0:T(8,128)S(1)} %dynamic-slice_bitcast_fusion.2), channel_id=1, source_target_pairs={{0,24},{16,9},{25,1},{9,16},{2,26},{18,11},{27,3},{11,18},{4,28},{... | collective-permute-start | bytes 638984 | tf_op jit(solution)/shard_map/ppermute | solution.py:114
  89.0 1.2 copy-start.1
  91.2 11.8 %collective-permute-start.18 = (f32[416,128]{1,0:T(8,128)}, f32[416,128]{1,0:T(8,128)}, u32[]{:S(2)}, u32[]{:S(2)}) collective-permute-start(f32[416,128]{1,0:T(8,128)} %dynamic-slice_bitcast_fusion.1), channel_id=1, source_target_pairs={{0,24},{16,9},{25,1},{9,16},{2,26},{18,11},{27,3},{11,18},{4,28},{... | collective-permute-start | bytes 638984 | tf_op jit(solution)/shard_map/ppermute | solution.py:114
  93.9 10.8 %collective-permute-start.13 = (f32[416,128]{1,0:T(8,128)}, f32[416,128]{1,0:T(8,128)}, u32[]{:S(2)}, u32[]{:S(2)}) collective-permute-start(f32[416,128]{1,0:T(8,128)} %broadcast_select_fusion.2), channel_id=1, source_target_pairs={{0,8},{8,0},{16,24},{24,16},{1,9},{9,1},{17,25},{25,17},{2,10},{10... | collective-permute-start | bytes 638984 | tf_op jit(solution)/shard_map/ppermute | solution.py:167
  100.8 21.9 %collective-permute-start.24 = (f32[416,128]{1,0:T(8,128)S(1)}, f32[416,128]{1,0:T(8,128)S(1)}, u32[]{:S(2)}, u32[]{:S(2)}) collective-permute-start(f32[416,128]{1,0:T(8,128)S(1)} %dynamic-slice_bitcast_fusion), channel_id=1, source_target_pairs={{0,24},{16,9},{25,1},{9,16},{2,26},{18,11},{27,3},{11,18},{4,28},{... | collective-permute-start | bytes 638984 | tf_op jit(solution)/shard_map/ppermute | solution.py:114
  104.0 19.7 %collective-permute-start.19 = (f32[416,128]{1,0:T(8,128)S(1)}, f32[416,128]{1,0:T(8,128)S(1)}, u32[]{:S(2)}, u32[]{:S(2)}) collective-permute-start(f32[416,128]{1,0:T(8,128)S(1)} %broadcast_select_fusion.1), channel_id=1, source_target_pairs={{0,8},{8,0},{16,24},{24,16},{1,9},{9,1},{17,25},{25,17},{2,10},{10... | collective-permute-start | bytes 638984 | tf_op jit(solution)/shard_map/ppermute | solution.py:167
  108.7 25.7 %collective-permute-start.14 = (f32[4,384,128]{2,1,0:T(8,128)}, f32[4,384,128]{2,1,0:T(8,128)}, u32[]{:S(2)}, u32[]{:S(2)}) collective-permute-start(f32[4,384,128]{2,1,0:T(8,128)} %shard_map.34), channel_id=1, source_target_pairs={{0,128},{128,0},{1,129},{129,1},{2,130},{130,2},{3,131},{131,3},{4... | collective-permute-start | bytes 2359304 | tf_op jit(solution)/shard_map/ppermute | solution.py:93
  123.6 7.0 %collective-permute-start.25 = (f32[416,128]{1,0:T(8,128)S(1)}, f32[416,128]{1,0:T(8,128)S(1)}, u32[]{:S(2)}, u32[]{:S(2)}) collective-permute-start(f32[416,128]{1,0:T(8,128)S(1)} %broadcast_select_fusion), channel_id=1, source_target_pairs={{0,8},{8,0},{16,24},{24,16},{1,9},{9,1},{17,25},{25,17},{2,10},{10... | collective-permute-start | bytes 638984 | tf_op jit(solution)/shard_map/ppermute | solution.py:167
  126.7 15.7 %collective-permute-start.20 = (f32[4,384,128]{2,1,0:T(8,128)}, f32[4,384,128]{2,1,0:T(8,128)}, u32[]{:S(2)}, u32[]{:S(2)}) collective-permute-start(f32[4,384,128]{2,1,0:T(8,128)} %shard_map.36), channel_id=1, source_target_pairs={{0,128},{128,0},{1,129},{129,1},{2,130},{130,2},{3,131},{131,3},{4... | collective-permute-start | bytes 2359304 | tf_op jit(solution)/shard_map/ppermute | solution.py:93
  133.6 17.2 %collective-permute-start.26 = (f32[4,384,128]{2,1,0:T(8,128)}, f32[4,384,128]{2,1,0:T(8,128)}, u32[]{:S(2)}, u32[]{:S(2)}) collective-permute-start(f32[4,384,128]{2,1,0:T(8,128)} %shard_map.38), channel_id=1, source_target_pairs={{0,128},{128,0},{1,129},{129,1},{2,130},{130,2},{3,131},{131,3},{4... | collective-permute-start | bytes 2359304 | tf_op jit(solution)/shard_map/ppermute | solution.py:93
  134.4 0.9 copy-start.3
  137.8 8.2 %collective-permute-start.15 = (f32[384,128]{1,0:T(8,128)S(1)}, f32[384,128]{1,0:T(8,128)S(1)}, u32[]{:S(2)}, u32[]{:S(2)}) collective-permute-start(f32[384,128]{1,0:T(8,128)S(1)} %get-tuple-element.68), channel_id=1, source_target_pairs={{0,64},{32,96},{64,0},{96,32},{1,65},{33,97},{65,1},{97,33},{2,66}... | collective-permute-start | bytes 589832 | tf_op jit(solution)/shard_map/ppermute | solution.py:98
  139.7 11.0 %collective-permute-start.16 = (f32[384,128]{1,0:T(8,128)S(1)}, f32[384,128]{1,0:T(8,128)S(1)}, u32[]{:S(2)}, u32[]{:S(2)}) collective-permute-start(f32[384,128]{1,0:T(8,128)S(1)} %get-tuple-element.69), channel_id=1, source_target_pairs={{0,32},{32,64},{64,96},{96,0},{1,33},{33,65},{65,97},{97,1},{2,34}... | collective-permute-start | bytes 589832 | tf_op jit(solution)/shard_map/ppermute | solution.py:98
  139.9 10.8 %collective-permute-start.17 = (f32[384,128]{1,0:T(8,128)S(1)}, f32[384,128]{1,0:T(8,128)S(1)}, u32[]{:S(2)}, u32[]{:S(2)}) collective-permute-start(f32[384,128]{1,0:T(8,128)S(1)} %get-tuple-element.70), channel_id=1, source_target_pairs={{0,96},{32,0},{64,32},{96,64},{1,97},{33,1},{65,33},{97,65},{2,98}... | collective-permute-start | bytes 589832 | tf_op jit(solution)/shard_map/ppermute | solution.py:98
  142.4 0.9 copy-start.4
  143.4 7.4 %copy-start.2 = (f32[416,128]{1,0:T(8,128)S(1)}, f32[416,128]{1,0:T(8,128)}, u32[]{:S(2)}) copy-start(f32[416,128]{1,0:T(8,128)} %get-tuple-element.87.refs_6_) | copy-start | bytes 638980
  145.9 9.5 %collective-permute-start.21 = (f32[384,128]{1,0:T(8,128)S(1)}, f32[384,128]{1,0:T(8,128)S(1)}, u32[]{:S(2)}, u32[]{:S(2)}) collective-permute-start(f32[384,128]{1,0:T(8,128)S(1)} %get-tuple-element.72), channel_id=1, source_target_pairs={{0,64},{32,96},{64,0},{96,32},{1,65},{33,97},{65,1},{97,33},{2,66}... | collective-permute-start | bytes 589832 | tf_op jit(solution)/shard_map/ppermute | solution.py:98
  146.0 13.4 %collective-permute-start.22 = (f32[384,128]{1,0:T(8,128)S(1)}, f32[384,128]{1,0:T(8,128)S(1)}, u32[]{:S(2)}, u32[]{:S(2)}) collective-permute-start(f32[384,128]{1,0:T(8,128)S(1)} %get-tuple-element.73), channel_id=1, source_target_pairs={{0,32},{32,64},{64,96},{96,0},{1,33},{33,65},{65,97},{97,1},{2,34}... | collective-permute-start | bytes 589832 | tf_op jit(solution)/shard_map/ppermute | solution.py:98
  150.7 8.7 %collective-permute-start.23 = (f32[384,128]{1,0:T(8,128)S(1)}, f32[384,128]{1,0:T(8,128)S(1)}, u32[]{:S(2)}, u32[]{:S(2)}) collective-permute-start(f32[384,128]{1,0:T(8,128)S(1)} %get-tuple-element.74), channel_id=1, source_target_pairs={{0,96},{32,0},{64,32},{96,64},{1,97},{33,1},{65,33},{97,65},{2,98}... | collective-permute-start | bytes 589832 | tf_op jit(solution)/shard_map/ppermute | solution.py:98
  153.3 9.1 %collective-permute-start.27 = (f32[384,128]{1,0:T(8,128)S(1)}, f32[384,128]{1,0:T(8,128)S(1)}, u32[]{:S(2)}, u32[]{:S(2)}) collective-permute-start(f32[384,128]{1,0:T(8,128)S(1)} %get-tuple-element.76), channel_id=1, source_target_pairs={{0,64},{32,96},{64,0},{96,32},{1,65},{33,97},{65,1},{97,33},{2,66}... | collective-permute-start | bytes 589832 | tf_op jit(solution)/shard_map/ppermute | solution.py:98
  155.0 12.2 %collective-permute-start.28 = (f32[384,128]{1,0:T(8,128)S(1)}, f32[384,128]{1,0:T(8,128)S(1)}, u32[]{:S(2)}, u32[]{:S(2)}) collective-permute-start(f32[384,128]{1,0:T(8,128)S(1)} %get-tuple-element.77), channel_id=1, source_target_pairs={{0,32},{32,64},{64,96},{96,0},{1,33},{33,65},{65,97},{97,1},{2,34}... | collective-permute-start | bytes 589832 | tf_op jit(solution)/shard_map/ppermute | solution.py:98
  155.4 11.8 %collective-permute-start.29 = (f32[384,128]{1,0:T(8,128)S(1)}, f32[384,128]{1,0:T(8,128)S(1)}, u32[]{:S(2)}, u32[]{:S(2)}) collective-permute-start(f32[384,128]{1,0:T(8,128)S(1)} %get-tuple-element.78), channel_id=1, source_target_pairs={{0,96},{32,0},{64,32},{96,64},{1,97},{33,1},{65,33},{97,65},{2,98}... | collective-permute-start | bytes 589832 | tf_op jit(solution)/shard_map/ppermute | solution.py:98

commit v4 on v0

v4 whole, which is shorter than its diff:
```python
import functools

import jax
import jax.numpy as jnp
from jax import lax
from jax.experimental import pallas as pl
from jax.experimental.pallas import tpu as pltpu
from jax.sharding import Mesh, PartitionSpec as P

CHUNK = 128
SPLIT = (104, 96, 104, 96)
PADDED = 104
DEPTH = 4 * PADDED
VMEM_LIMIT = 32 * 1024 * 1024
HALF_LIMIT = 60 * 1024 * 1024
COST = pl.CostEstimate(flops=int(20e9), bytes_accessed=int(74e6), transcendentals=0)


def halves(value):
    high = value.astype(jnp.bfloat16)
    low = (value - high.astype(jnp.float32)).astype(jnp.bfloat16)
    return high, low


def product(left, right, contract=(1, 0)):
    (lh, ll), (rh, rl) = left, right
    dims = (((contract[0],), (contract[1],)), ((), ()))
    dot = functools.partial(lax.dot_general, dimension_numbers=dims, preferred_element_type=jnp.float32)
    return dot(lh, rh) + (dot(lh, rl) + dot(ll, rh))


def call(kernel, out_shape, spaces, scratch=()):
    vmem = pl.BlockSpec(memory_space=pltpu.VMEM)
    smem = pl.BlockSpec(memory_space=pltpu.SMEM)
    return pl.pallas_call(
        kernel,
        out_shape=out_shape,
        in_specs=[smem if s == "s" else vmem for s in spaces],
        out_specs=jax.tree.map(lambda _: vmem, out_shape),
        scratch_shapes=scratch,
        cost_estimate=COST,
        compiler_params=pltpu.CompilerParams(vmem_limit_bytes=VMEM_LIMIT),
    )


def f32(*shape):
    return jax.ShapeDtypeStruct(shape, jnp.float32)


def bf16(*shape):
    return jax.ShapeDtypeStruct(shape, jnp.bfloat16)


def half_kernel(count, here_ref, coeff_ref, *refs):
    blocks, outs, pieces = refs[:count], refs[count:-1], refs[-1]
    part = pl.program_id(0)
    coeff = halves(coeff_ref[...])
    for c, block in enumerate(blocks):
        for p in range(2):
            pieces[c, 2 * p + part] = product(coeff, halves(block[p]), (1, 1))

    @pl.when(part == 1)
    def _():
        for c in range(count):
            for d in range(4):
                outs[4 * c + d][...] = pieces[c, (here_ref[0] + d) % 4]


def half_call(first, count, here, three_index, coeff):
    size, cols = coeff.shape[0] // 2, coeff.shape[1]
    blocks = [pl.BlockSpec((2, CHUNK, cols), lambda i, c=c: (0, c, 0)) for c in range(first, first + count)]
    return pl.pallas_call(
        functools.partial(half_kernel, count),
        out_shape=[f32(size, CHUNK)] * (4 * count),
        grid=(2,),
        in_specs=[pl.BlockSpec(memory_space=pltpu.SMEM), pl.BlockSpec((size, cols), lambda i: (i, 0))] + blocks,
        out_specs=[pl.BlockSpec((size, CHUNK), lambda i: (0, 0))] * (4 * count),
        scratch_shapes=[pltpu.VMEM((count, 4, size, CHUNK), jnp.float32)],
        cost_estimate=COST,
        compiler_params=pltpu.CompilerParams(vmem_limit_bytes=HALF_LIMIT if first == 0 else VMEM_LIMIT),
    )(here, coeff, *[three_index] * count)


def sum_kernel(a, b, c, d, out):
    out[...] = (a[...] + b[...]) + (c[...] + d[...])


def piece_kernel(one_ref, two_ref, out):
    at = 0
    for i, size in enumerate(SPLIT):
        out[i, :size] = one_ref[at : at + size] + two_ref[at : at + size]
        if size < PADDED:
            out[i, size:] = jnp.zeros((PADDED - size, CHUNK), jnp.float32)
        at += size


def left_kernel(here_ref, pick_ref, a, b, c, d, high_ref, low_ref, mine_ref, held):
    here = here_ref[0]
    for i, ref in enumerate((a, b, c, d)):
        slot = (here - i + 4) % 4
        for e in range(4):
            held[e, slot] = ref[e]
    for e in range(4):
        high, low = halves(held[e].reshape(DEPTH, CHUNK).T)
        high_ref[e] = high
        low_ref[e] = low
    mine_ref[...] = held[pick_ref[0]].reshape(DEPTH, CHUNK)


def have_kernel(flags_ref, mine, crossed, out):
    out[...] = jnp.where(flags_ref[0] == 1, mine[...], crossed[...])


def tile_kernel(flags_ref, *refs):
    left, (have, other), (give_ref, keep_ref) = refs[:6], refs[6:8], refs[8:]
    same = flags_ref[1] == 1
    give = jnp.where(same, other[...], have[...])
    keep = jnp.where(same, have[...], other[...])
    right = halves(jnp.concatenate([give, keep], axis=1))
    for c in range(3):
        rows = slice(c * CHUNK, (c + 1) * CHUNK)
        for e in range(4):
            tile = product((left[2 * c][e], left[2 * c + 1][e]), right)
            give_ref[e, rows] = tile[:, :CHUNK]
            keep_ref[e, rows] = tile[:, CHUNK:]


def add_kernel(here_ref, one_ref, two_ref, *outs):
    for d, out in enumerate(outs):
        x = (here_ref[0] + d) % 4
        out[...] = one_ref[x] + two_ref[x]


def last_kernel(one, two, a, b, c, d, out):
    out[:, :CHUNK] = one[...]
    out[:, CHUNK : 2 * CHUNK] = two[...]
    out[:, 2 * CHUNK :] = (a[...] + b[...]) + (c[...] + d[...])


def swapped(value, axis):
    return lax.ppermute(value, axis, [(0, 1), (1, 0)])


def shifted(value, axis, distance):
    size = lax.axis_size(axis)
    return lax.ppermute(value, axis, [(i, (i + distance) % size) for i in range(size)])


def tie(value, *others):
    return lax.optimization_barrier((value,) + others)[0]


def along(value, moves):
    pairs = [(z * 4 + y, to_z * 4 + to_y) for (z, y), (to_z, to_y) in moves.items()]
    return lax.ppermute(value, ("zl", "y"), pairs)


def crossing(value):
    moves = {}
    for y in range(4):
        if y % 2 == 0:
            moves |= {(0, y): (3, y), (2, y): (1, y ^ 1)}
        else:
            moves |= {(3, y): (0, y), (1, y): (2, y ^ 1)}
    return along(value, moves)


class Order:
    def __init__(self):
        self.last = None

    def __call__(self, kernel, *operands):
        if self.last is not None:
            operands = lax.optimization_barrier(operands + (self.last,))[:-1]
        result = kernel(*operands)
        self.last = result[0] if isinstance(result, (list, tuple)) else result
        return result

    def after(self, value):
        self.last = lax.optimization_barrier((self.last, value))[0]


def body(three_index, occupied):
    rows = three_index.shape[1]
    aux, x, zl, zh, y = (lax.axis_index(a) for a in ("aux", "x", "zl", "zh", "y"))
    home = (zl // 2) == (y % 2)
    same = (zl + zl // 2 + y) % 2 == aux
    scalar = lambda *v: jnp.stack([jnp.asarray(a, jnp.int32) for a in v])
    x_here, y_here = scalar(x), scalar(y)
    pick = scalar(2 * zh + y // 2)
    flags = scalar(home, same)

    coeff = occupied.T
    share = coeff.shape[0] // 2
    sum_call = call(sum_kernel, f32(share, CHUNK), "vvvv")
    piece_call = call(piece_kernel, f32(4, PADDED, CHUNK), "vv")
    left_call = call(
        left_kernel,
        [bf16(4, CHUNK, DEPTH)] * 2 + [f32(DEPTH, CHUNK)],
        "ssvvvv",
        [pltpu.VMEM((4, 4, PADDED, CHUNK), jnp.float32)],
    )
    have_call = call(have_kernel, f32(DEPTH, CHUNK), "svv")
    tile_call = call(tile_kernel, [f32(4, rows, CHUNK)] * 2, "s" + "v" * 8)
    add_call = call(add_kernel, [f32(rows, CHUNK)] * 4, "svv")
    out_call = call(sum_kernel, f32(rows, CHUNK), "vvvv")
    last_call = call(last_kernel, f32(rows, 3 * CHUNK), "v" * 6)

    order = Order()
    first = order(functools.partial(half_call, 0, 1), y_here, three_index, coeff)
    rest = order(functools.partial(half_call, 1, 2), y_here, three_index, coeff)
    sends = [first, rest[:4], rest[4:]]

    def sum_y(c):
        own, one, two, three = sends[c]
        if c == 2:
            one, two, three = lax.optimization_barrier((one, two, three, sums[0][0]))[:3]
        far, near, back = shifted(two, "y", 2), shifted(one, "y", 1), shifted(three, "y", 3)
        total = order(sum_call, own, far, near, back)
        return total, swapped(total, "zh")

    def over_x(total, other):
        return lax.all_to_all(order(piece_call, total, other), "x", 0, 0, tiled=True)

    def over_y(block):
        return [block] + [shifted(block, "y", d) for d in (1, 2, 3)]

    def left_of(blocks):
        high, low, mine = order(left_call, y_here, pick, *blocks)
        return [high, low], mine, crossing(mine)

    def pair_of(mine, crossed):
        have = order(have_call, flags, mine, crossed)
        return have, lax.ppermute(have, "zl", [(0, 1), (1, 0), (2, 3), (3, 2)])

    def tile_of(pair):
        give, keep = order(tile_call, flags, *lefts, *pair)
        return keep, swapped(give, "aux")

    def over_x_sum(keep, given):
        own, one, two, three = order(add_call, x_here, keep, given)
        return [own, shifted(two, "x", 2), shifted(one, "x", 1), shifted(three, "x", 3)]

    sums = []
    for c in range(3):
        sums.append(sum_y(c))
    blocks = []
    for c in range(3):
        block = over_x(*sums[c])
        order.after(block)
        blocks.append(over_y(block))
    left0, mine0, crossed0 = left_of(blocks[0])
    left1, mine1, crossed1 = left_of(blocks[1])
    pair0 = pair_of(mine0, crossed0)
    pair1 = pair_of(mine1, crossed1)
    left2, mine2, crossed2 = left_of(blocks[2])
    lefts = left0 + left1 + left2
    tile0 = tile_of(pair0)
    tile1 = tile_of(pair1)
    pair2 = pair_of(mine2, crossed2)
    out0 = over_x_sum(*tile0)
    out1 = over_x_sum(*tile1)
    tile2 = tile_of(pair2)
    out0 = order(out_call, *out0)
    out2 = over_x_sum(*tile2)
    out1 = order(out_call, *out1)
    return order(last_call, out0, out1, *out2)


def solution(mesh):
    fine = Mesh(mesh.devices.reshape(2, 4, 4, 2, 4), ("aux", "x", "zl", "zh", "y"))
    in_specs = (P("aux", ("x", "zl"), ("zh", "y")), P(("zh", "y"), None))
    out_specs = P(("x", "zl"), ("zh", "y", "aux"))
    return jax.shard_map(body, mesh=fine, in_specs=in_specs, out_specs=out_specs, check_vma=False)
```

time: 513 us -> 148 us (0.29)
  waiting for transfers between devices: 466 us -> 29.1 us
  starting transfers between devices: 0.27 us -> 95 us
  matrix products: 29.6 us -> 0 us
  Pallas kernels: 0 us -> 21.6 us
  between operations: 13.1 us -> 0.34 us
    psum x2 -> x0, waiting for transfers between devices: 454 us -> none  [the longest x1 227 us: body(): col_half = lax.psum(col_half, 'row')]
    ppermute x0 -> x39, starting transfers between devices: none -> 84.3 us  [the longest x6 36.9 us: swapped(): return lax.ppermute(value, axis, [(0, 1), (1, 0)])]
    dot_general x3 -> x0, matrix products: 29.6 us -> none  [the longest x1 11.1 us: body(): jnp.einsum('pml,mi->pli', three_index, coeff_local, precision=highest)]
    pallas_call x0 -> x23, Pallas kernels: none -> 21.6 us  [the longest x21 12.3 us: __call__(): result = kernel(*operands)]
    ppermute x0 -> x39, waiting for transfers between devices: none -> 18.7 us  [the longest x27 14.2 us: shifted(): lax.ppermute(value, axis, [(i, (i + distance) % size) for i in range(size)])]
    reduce_scatter x1 -> x0, waiting for transfers between devices: 12.5 us -> none  [body(): lax.psum_scatter(partial_tile, 'aux', scatter_dimension=1, tiled=True)]
    all_to_all x0 -> x3, starting transfers between devices: none -> 10.8 us  [over_x(): lax.all_to_all(order(piece_call, total, other), 'x', 0, 0, tiled=True)]
    all_to_all x0 -> x3, waiting for transfers between devices: none -> 10.4 us  [over_x(): lax.all_to_all(order(piece_call, total, other), 'x', 0, 0, tiled=True)]
  transfers between devices with their start and end apart: 3 -> 42, of which waited for: 3 -> 12; matrix products, arithmetic and copies ran while one was open for 0% -> 0% of each run, Pallas kernels for 0% -> 11%
where the time goes in v4:
time: 148 us
  starting transfers between devices  95 us (64%)
  waiting for transfers between devices  29.1 us (20%)
  Pallas kernels  21.6 us (15%)
  local copies, waits for them, and re-layouts  1.67 us (1%)
    ppermute x6, starting transfers between devices, swapped(): return lax.ppermute(value, axis, [(0, 1), (1, 0)])  36.9 us
    ppermute x27, starting transfers between devices, shifted(): lax.ppermute(value, axis, [(i, (i + distance) % size) for i in range(size)])  35.8 us
    ppermute x27, waiting for transfers between devices, shifted(): lax.ppermute(value, axis, [(i, (i + distance) % size) for i in range(size)])  14.2 us
    pallas_call x21, Pallas kernels, __call__(): result = kernel(*operands)  12.3 us
    ppermute x3, starting transfers between devices, along(): return lax.ppermute(value, ('zl', 'y'), pairs)  11.4 us
    all_to_all x3, starting transfers between devices, over_x(): lax.all_to_all(order(piece_call, total, other), 'x', 0, 0, tiled=True)  10.8 us
    all_to_all x3, waiting for transfers between devices, over_x(): lax.all_to_all(order(piece_call, total, other), 'x', 0, 0, tiled=True)  10.4 us
    pallas_call x2, Pallas kernels, half_call(): pl.pallas_call(functools.partial(half_kernel, count), out_shape=[f32(size...  9.26 us
  transfers between devices with their start and end apart: 42, of which 12 were waited for; matrix products, arithmetic and copies ran while one was open for 0% of the time, Pallas kernels for 11%

profile of v4, /device:TPU:1, one launch (start us, length us, event | category | flops | bytes accessed | tf_op | source)
XLA Modules:
  0.0 147.9 jit_solution(17850084678210997498)
XLA Ops:
  0.0 4.9 %shard_map.28 = (f32[400,128]{1,0:T(8,128)}, f32[400,128]{1,0:T(8,128)}, f32[400,128]{1,0:T(8,128)}, f32[400,128]{1,0:T(8,128)}) custom-call(s32[1]{0:T(128)} %bitcast.3.here_ref, f32[800,768]{1,0:T(8,128)} %bitcast.6, f32[2,384,768]{2,1,0:T(8,128)} %refs_1_), custom_call_target="tpu_custom_call" | custom-call | flops 20000000000 | bytes 74000000 | tf_op jit(solution)/shard_map/pallas_call | solution.py:72
  4.9 3.7 %collective-permute-start = (f32[400,128]{1,0:T(8,128)}, f32[400,128]{1,0:T(8,128)S(1)}, u32[]{:S(2)}, u32[]{:S(2)}) collective-permute-start(f32[400,128]{1,0:T(8,128)} %get-tuple-element.146), channel_id=1, source_target_pairs={{0,2},{1,3},{2,0},{3,1},{4,6},{5,7},{6,4},{7,5},{8,10},{9,11},{10,... | collective-permute-start | bytes 614408 | tf_op jit(solution)/shard_map/ppermute | solution.py:146
  9.0 2.3 %collective-permute-start.2 = (f32[400,128]{1,0:T(8,128)}, f32[400,128]{1,0:T(8,128)S(1)}, u32[]{:S(2)}, u32[]{:S(2)}) collective-permute-start(f32[400,128]{1,0:T(8,128)} %get-tuple-element.148), channel_id=1, source_target_pairs={{0,3},{1,0},{2,1},{3,2},{4,7},{5,4},{6,5},{7,6},{8,11},{9,8},{10,9... | collective-permute-start | bytes 614408 | tf_op jit(solution)/shard_map/ppermute | solution.py:146
  11.3 1.7 %copy-done.1 = f32[2,384,768]{2,1,0:T(8,128)S(1)} copy-done((f32[2,384,768]{2,1,0:T(8,128)S(1)}, f32[2,384,768]{2,1,0:T(8,128)}, u32[]{:S(2)}) %copy-start.1) | copy-done | bytes 2359320
  13.0 4.4 %shard_map.29 = (f32[400,128]{1,0:T(8,128)S(1)}, f32[400,128]{1,0:T(8,128)S(1)}, f32[400,128]{1,0:T(8,128)S(1)}, f32[400,128]{1,0:T(8,128)S(1)}, f32[400,128]{1,...) custom-call(s32[1]{0:T(128)} %bitcast.3.here_ref, f32[800,768]{1,0:T(8,128)S(1)} %bitcast.7, ...), custom_call_target="tpu_custom_call" | custom-call | flops 20000000000 | bytes 74000000 | tf_op jit(solution)/shard_map/pallas_call | solution.py:72
  18.0 2.2 %collective-permute-start.9 = (f32[400,128]{1,0:T(8,128)S(1)}, f32[400,128]{1,0:T(8,128)S(1)}, u32[]{:S(2)}, u32[]{:S(2)}) collective-permute-start(f32[400,128]{1,0:T(8,128)S(1)} %get-tuple-element.166), channel_id=1, source_target_pairs={{0,3},{1,0},{2,1},{3,2},{4,7},{5,4},{6,5},{7,6},{8,11},{9,8},{10,9... | collective-permute-start | bytes 614408 | tf_op jit(solution)/shard_map/ppermute | solution.py:146
  20.3 7.0 %collective-permute-start.3 = (f32[400,128]{1,0:T(8,128)S(1)}, f32[400,128]{1,0:T(8,128)S(1)}, u32[]{:S(2)}, u32[]{:S(2)}) collective-permute-start(f32[400,128]{1,0:T(8,128)S(1)} %shard_map.30.one_ref), channel_id=1, source_target_pairs={{0,4},{4,0},{1,5},{5,1},{2,6},{6,2},{3,7},{7,3},{8,12},{12,8},{9,1... | collective-permute-start | bytes 614408 | tf_op jit(solution)/shard_map/ppermute | solution.py:141
  27.3 1.7 %collective-permute-start.4 = (f32[400,128]{1,0:T(8,128)S(1)}, f32[400,128]{1,0:T(8,128)S(1)}, u32[]{:S(2)}, u32[]{:S(2)}) collective-permute-start(f32[400,128]{1,0:T(8,128)S(1)} %get-tuple-element.161), channel_id=1, source_target_pairs={{0,2},{1,3},{2,0},{3,1},{4,6},{5,7},{6,4},{7,5},{8,10},{9,11},{10,... | collective-permute-start | bytes 614408 | tf_op jit(solution)/shard_map/ppermute | solution.py:146
  29.0 1.0 collective-permute-done.8.c
  29.9 1.7 %collective-permute-start.6 = (f32[400,128]{1,0:T(8,128)S(1)}, f32[400,128]{1,0:T(8,128)S(1)}, u32[]{:S(2)}, u32[]{:S(2)}) collective-permute-start(f32[400,128]{1,0:T(8,128)S(1)} %get-tuple-element.163), channel_id=1, source_target_pairs={{0,3},{1,0},{2,1},{3,2},{4,7},{5,4},{6,5},{7,6},{8,11},{9,8},{10,9... | collective-permute-start | bytes 614408 | tf_op jit(solution)/shard_map/ppermute | solution.py:146
  31.7 6.7 %collective-permute-start.13 = (f32[400,128]{1,0:T(8,128)S(1)}, f32[400,128]{1,0:T(8,128)S(1)}, u32[]{:S(2)}, u32[]{:S(2)}) collective-permute-start(f32[400,128]{1,0:T(8,128)S(1)} %shard_map.31.one_ref), channel_id=1, source_target_pairs={{0,4},{4,0},{1,5},{5,1},{2,6},{6,2},{3,7},{7,3},{8,12},{12,8},{9,1... | collective-permute-start | bytes 614408 | tf_op jit(solution)/shard_map/ppermute | solution.py:141
  38.6 7.1 %collective-permute-start.17 = (f32[400,128]{1,0:T(8,128)S(1)}, f32[400,128]{1,0:T(8,128)S(1)}, u32[]{:S(2)}, u32[]{:S(2)}) collective-permute-start(f32[400,128]{1,0:T(8,128)S(1)} %shard_map.32.one_ref), channel_id=1, source_target_pairs={{0,4},{4,0},{1,5},{5,1},{2,6},{6,2},{3,7},{7,3},{8,12},{12,8},{9,1... | collective-permute-start | bytes 614408 | tf_op jit(solution)/shard_map/ppermute | solution.py:141
  45.8 0.7 shard_map.33
  46.5 4.0 %all-to-all-start = ((f32[4,104,128]{2,1,0:T(8,128)}), f32[4,104,128]{2,1,0:T(8,128)S(1)}, u32[]{:S(2)}, u32[]{:S(2)}) async-start(f32[4,104,128]{2,1,0:T(8,128)} %shard_map.33), calls=%async_computation | async-start | bytes 425984 | tf_op jit(solution)/shard_map/all_to_all | solution.py:223
  51.2 4.6 %all-to-all-done.a = f32[4,104,128]{2,1,0:T(8,128)S(1)} async-done(((f32[4,104,128]{2,1,0:T(8,128)}), f32[4,104,128]{2,1,0:T(8,128)S(1)}, u32[]{:S(2)}, u32[]{:S(2)}) %all-to-all-start) | async-done | bytes 213024 | tf_op jit(solution)/shard_map/all_to_all | solution.py:223
  55.8 3.4 %all-to-all-start.1 = ((f32[4,104,128]{2,1,0:T(8,128)}), f32[4,104,128]{2,1,0:T(8,128)S(1)}, u32[]{:S(2)}, u32[]{:S(2)}) async-start(f32[4,104,128]{2,1,0:T(8,128)} %shard_map.35), calls=%async_computation.1 | async-start | bytes 425984 | tf_op jit(solution)/shard_map/all_to_all | solution.py:223
  59.2 0.8 collective-permute-start.11
  60.0 0.8 collective-permute-start.10
  61.5 2.9 %all-to-all-done.1.a = f32[4,104,128]{2,1,0:T(8,128)S(1)} async-done(((f32[4,104,128]{2,1,0:T(8,128)}), f32[4,104,128]{2,1,0:T(8,128)S(1)}, u32[]{:S(2)}, u32[]{:S(2)}) %all-to-all-start.1) | async-done | bytes 213024 | tf_op jit(solution)/shard_map/all_to_all | solution.py:223
  64.4 3.4 %all-to-all-start.2 = ((f32[4,104,128]{2,1,0:T(8,128)}), f32[4,104,128]{2,1,0:T(8,128)S(1)}, u32[]{:S(2)}, u32[]{:S(2)}) async-start(f32[4,104,128]{2,1,0:T(8,128)} %shard_map.37), calls=%async_computation.2 | async-start | bytes 425984 | tf_op jit(solution)/shard_map/all_to_all | solution.py:223
  68.0 1.3 collective-permute-start.15
  69.3 0.8 collective-permute-start.14
  70.1 2.9 %all-to-all-done.2.a = f32[4,104,128]{2,1,0:T(8,128)S(1)} async-done(((f32[4,104,128]{2,1,0:T(8,128)}), f32[4,104,128]{2,1,0:T(8,128)S(1)}, u32[]{:S(2)}, u32[]{:S(2)}) %all-to-all-start.2) | async-done | bytes 213024 | tf_op jit(solution)/shard_map/all_to_all | solution.py:223
  73.5 1.0 collective-permute-start.19
  74.9 0.8 collective-permute-start.18
  75.7 1.6 %collective-permute-done.14.b = f32[4,104,128]{2,1,0:T(8,128)S(1)} collective-permute-done((f32[4,104,128]{2,1,0:T(8,128)S(1)}, f32[4,104,128]{2,1,0:T(8,128)S(1)}, u32[]{:S(2)}, u32[]{:S(2)}) %collective-permute-start.14) | collective-permute-done | bytes 213024 | tf_op jit(solution)/shard_map/ppermute | solution.py:146
  77.3 4.1 %collective-permute-start.22 = (f32[416,128]{1,0:T(8,128)S(1)}, f32[416,128]{1,0:T(8,128)S(1)}, u32[]{:S(2)}, u32[]{:S(2)}) collective-permute-start(f32[416,128]{1,0:T(8,128)S(1)} %get-tuple-element.200.mine), channel_id=1, source_target_pairs={{0,24},{16,9},{25,1},{9,16},{2,26},{18,11},{27,3},{11,18},{4,28},{... | collective-permute-start | bytes 638984 | tf_op jit(solution)/shard_map/ppermute | solution.py:155
  81.9 1.3 collective-permute-start.21
  83.2 1.0 collective-permute-done.22.crossed
  84.9 1.6 %collective-permute-done.21.crossed = f32[416,128]{1,0:T(8,128)S(1)} collective-permute-done((f32[416,128]{1,0:T(8,128)S(1)}, f32[416,128]{1,0:T(8,128)S(1)}, u32[]{:S(2)}, u32[]{:S(2)}) %collective-permute-start.21) | collective-permute-done | bytes 213024 | tf_op jit(solution)/shard_map/ppermute | solution.py:155
  87.6 5.9 %collective-permute-start.25 = (f32[416,128]{1,0:T(8,128)S(1)}, f32[416,128]{1,0:T(8,128)S(1)}, u32[]{:S(2)}, u32[]{:S(2)}) collective-permute-start(f32[416,128]{1,0:T(8,128)S(1)} %get-tuple-element.236.mine), channel_id=1, source_target_pairs={{0,24},{16,9},{25,1},{9,16},{2,26},{18,11},{27,3},{11,18},{4,28},{... | collective-permute-start | bytes 638984 | tf_op jit(solution)/shard_map/ppermute | solution.py:155
  93.6 2.0 %shard_map.41 = (f32[4,384,128]{2,1,0:T(8,128)S(1)}, f32[4,384,128]{2,1,0:T(8,128)S(1)}) custom-call(s32[2]{0:T(128)S(1)} %add_convert_fusion.flags_ref, bf16[4,128,416]{2,1,0:T(8,128)(2,1)S(1)} %get-tuple-element.251.refs_0_, bf16[4,128,416]{2,1,0:T(8,128)(2,1)S(1)} %get-tuple-element.252.refs_1_, bf16[4,128,416]{2,1,0:T(8,128)(2,1)S(1)} %get-tuple-element.253.refs_2_, ...), custom_call_target="tpu_custom_call" | custom-call | flops 20000000000 | bytes 74000000 | tf_op jit(solution)/shard_map/pallas_call | solution.py:175
  95.5 13.7 %collective-permute-start.24 = (f32[4,384,128]{2,1,0:T(8,128)S(1)}, f32[4,384,128]{2,1,0:T(8,128)S(1)}, u32[]{:S(2)}, u32[]{:S(2)}) collective-permute-start(f32[4,384,128]{2,1,0:T(8,128)S(1)} %get-tuple-element.223), channel_id=1, source_target_pairs={{0,128},{128,0},{1,129},{129,1},{2,130},{130,2},{3,131},{131,3},{4... | collective-permute-start | bytes 2359304 | tf_op jit(solution)/shard_map/ppermute | solution.py:141
  109.3 2.0 %shard_map.42 = (f32[4,384,128]{2,1,0:T(8,128)S(1)}, f32[4,384,128]{2,1,0:T(8,128)S(1)}) custom-call(s32[2]{0:T(128)S(1)} %add_convert_fusion.flags_ref, bf16[4,128,416]{2,1,0:T(8,128)(2,1)S(1)} %get-tuple-element.251.refs_0_, bf16[4,128,416]{2,1,0:T(8,128)(2,1)S(1)} %get-tuple-element.252.refs_1_, bf16[4,128,416]{2,1,0:T(8,128)(2,1)S(1)} %get-tuple-element.253.refs_2_, ...), custom_call_target="tpu_custom_call" | custom-call | flops 20000000000 | bytes 74000000 | tf_op jit(solution)/shard_map/pallas_call | solution.py:175
  112.2 4.3 %collective-permute-start.27 = (f32[384,128]{1,0:T(8,128)S(1)}, f32[384,128]{1,0:T(8,128)S(1)}, u32[]{:S(2)}, u32[]{:S(2)}) collective-permute-start(f32[384,128]{1,0:T(8,128)S(1)} %get-tuple-element.242), channel_id=1, source_target_pairs={{0,64},{32,96},{64,0},{96,32},{1,65},{33,97},{65,1},{97,33},{2,66}... | collective-permute-start | bytes 589832 | tf_op jit(solution)/shard_map/ppermute | solution.py:146
  116.7 2.4 %collective-permute-start.29 = (f32[384,128]{1,0:T(8,128)S(1)}, f32[384,128]{1,0:T(8,128)S(1)}, u32[]{:S(2)}, u32[]{:S(2)}) collective-permute-start(f32[384,128]{1,0:T(8,128)S(1)} %get-tuple-element.244), channel_id=1, source_target_pairs={{0,96},{32,0},{64,32},{96,64},{1,97},{33,1},{65,33},{97,65},{2,98}... | collective-permute-start | bytes 589832 | tf_op jit(solution)/shard_map/ppermute | solution.py:146
  119.2 3.3 %collective-permute-start.32 = (f32[384,128]{1,0:T(8,128)S(1)}, f32[384,128]{1,0:T(8,128)S(1)}, u32[]{:S(2)}, u32[]{:S(2)}) collective-permute-start(f32[384,128]{1,0:T(8,128)S(1)} %get-tuple-element.264), channel_id=1, source_target_pairs={{0,64},{32,96},{64,0},{96,32},{1,65},{33,97},{65,1},{97,33},{2,66}... | collective-permute-start | bytes 589832 | tf_op jit(solution)/shard_map/ppermute | solution.py:146
  122.9 2.0 %shard_map.46 = (f32[4,384,128]{2,1,0:T(8,128)S(1)}, f32[4,384,128]{2,1,0:T(8,128)S(1)}) custom-call(s32[2]{0:T(128)S(1)} %add_convert_fusion.flags_ref, bf16[4,128,416]{2,1,0:T(8,128)(2,1)S(1)} %get-tuple-element.251.refs_0_, bf16[4,128,416]{2,1,0:T(8,128)(2,1)S(1)} %get-tuple-element.252.refs_1_, bf16[4,128,416]{2,1,0:T(8,128)(2,1)S(1)} %get-tuple-element.253.refs_2_, ...), custom_call_target="tpu_custom_call" | custom-call | flops 20000000000 | bytes 74000000 | tf_op jit(solution)/shard_map/pallas_call | solution.py:175
  124.9 2.5 %collective-permute-start.34 = (f32[384,128]{1,0:T(8,128)S(1)}, f32[384,128]{1,0:T(8,128)S(1)}, u32[]{:S(2)}, u32[]{:S(2)}) collective-permute-start(f32[384,128]{1,0:T(8,128)S(1)} %get-tuple-element.266), channel_id=1, source_target_pairs={{0,96},{32,0},{64,32},{96,64},{1,97},{33,1},{65,33},{97,65},{2,98}... | collective-permute-start | bytes 589832 | tf_op jit(solution)/shard_map/ppermute | solution.py:146
  127.3 2.2 %collective-permute-start.35 = (f32[4,384,128]{2,1,0:T(8,128)S(1)}, f32[4,384,128]{2,1,0:T(8,128)S(1)}, u32[]{:S(2)}, u32[]{:S(2)}) collective-permute-start(f32[4,384,128]{2,1,0:T(8,128)S(1)} %get-tuple-element.259), channel_id=1, source_target_pairs={{0,128},{128,0},{1,129},{129,1},{2,130},{130,2},{3,131},{131,3},{4... | collective-permute-start | bytes 2359304 | tf_op jit(solution)/shard_map/ppermute | solution.py:141
  129.5 1.9 %collective-permute-done.35.two_ref = f32[4,384,128]{2,1,0:T(8,128)S(1)} collective-permute-done((f32[4,384,128]{2,1,0:T(8,128)S(1)}, f32[4,384,128]{2,1,0:T(8,128)S(1)}, u32[]{:S(2)}, u32[]{:S(2)}) %collective-permute-start.35) | collective-permute-done | bytes 786464 | tf_op jit(solution)/shard_map/ppermute | solution.py:141
  131.5 2.9 %collective-permute-done.33.c = f32[384,128]{1,0:T(8,128)S(1)} collective-permute-done((f32[384,128]{1,0:T(8,128)S(1)}, f32[384,128]{1,0:T(8,128)S(1)}, u32[]{:S(2)}, u32[]{:S(2)}) %collective-permute-start.33) | collective-permute-done | bytes 196640 | tf_op jit(solution)/shard_map/ppermute | solution.py:146
  134.5 1.3 collective-permute-start.36
  135.8 1.2 collective-permute-start.37
  137.0 1.5 collective-permute-start.38
  138.5 3.2 %collective-permute-done.36.b = f32[384,128]{1,0:T(8,128)S(1)} collective-permute-done((f32[384,128]{1,0:T(8,128)S(1)}, f32[384,128]{1,0:T(8,128)S(1)}, u32[]{:S(2)}, u32[]{:S(2)}) %collective-permute-start.36) | collective-permute-done | bytes 196640 | tf_op jit(solution)/shard_map/ppermute | solution.py:146
  141.7 5.3 %collective-permute-done.37.c = f32[384,128]{1,0:T(8,128)S(1)} collective-permute-done((f32[384,128]{1,0:T(8,128)S(1)}, f32[384,128]{1,0:T(8,128)S(1)}, u32[]{:S(2)}, u32[]{:S(2)}) %collective-permute-start.37) | collective-permute-done | bytes 196640 | tf_op jit(solution)/shard_map/ppermute | solution.py:146
  147.0 0.9 shard_map.50
  (66 shorter events, 7.9 us)
Async XLA Ops:
  0.0 11.3 %copy-start = (f32[768,800]{0,1:T(8,128)S(1)}, f32[768,800]{0,1:T(8,128)}, u32[]{:S(2)}) copy-start(f32[768,800]{0,1:T(8,128)} %param.3) | copy-start | bytes 7372804
  4.9 13.1 %collective-permute-start = (f32[400,128]{1,0:T(8,128)}, f32[400,128]{1,0:T(8,128)S(1)}, u32[]{:S(2)}, u32[]{:S(2)}) collective-permute-start(f32[400,128]{1,0:T(8,128)} %get-tuple-element.146), channel_id=1, source_target_pairs={{0,2},{1,3},{2,0},{3,1},{4,6},{5,7},{6,4},{7,5},{8,10},{9,11},{10,... | collective-permute-start | bytes 614408 | tf_op jit(solution)/shard_map/ppermute | solution.py:146
  8.6 11.6 %collective-permute-start.1 = (f32[400,128]{1,0:T(8,128)}, f32[400,128]{1,0:T(8,128)S(1)}, u32[]{:S(2)}, u32[]{:S(2)}) collective-permute-start(f32[400,128]{1,0:T(8,128)} %get-tuple-element.147), channel_id=1, source_target_pairs={{0,1},{1,2},{2,3},{3,0},{4,5},{5,6},{6,7},{7,4},{8,9},{9,10},{10,1... | collective-permute-start | bytes 614408 | tf_op jit(solution)/shard_map/ppermute | solution.py:146
  9.0 11.2 %collective-permute-start.2 = (f32[400,128]{1,0:T(8,128)}, f32[400,128]{1,0:T(8,128)S(1)}, u32[]{:S(2)}, u32[]{:S(2)}) collective-permute-start(f32[400,128]{1,0:T(8,128)} %get-tuple-element.148), channel_id=1, source_target_pairs={{0,3},{1,0},{2,1},{3,2},{4,7},{5,4},{6,5},{7,6},{8,11},{9,8},{10,9... | collective-permute-start | bytes 614408 | tf_op jit(solution)/shard_map/ppermute | solution.py:146
  11.3 1.7 %copy-start.1 = (f32[2,384,768]{2,1,0:T(8,128)S(1)}, f32[2,384,768]{2,1,0:T(8,128)}, u32[]{:S(2)}) copy-start(f32[2,384,768]{2,1,0:T(8,128)} %refs_1_) | copy-start | bytes 7077892
  13.0 7.2 %copy-start.2 = (f32[400,128]{1,0:T(8,128)S(1)}, f32[400,128]{1,0:T(8,128)}, u32[]{:S(2)}) copy-start(f32[400,128]{1,0:T(8,128)} %get-tuple-element.153.a) | copy-start | bytes 614404
  17.4 11.6 %collective-permute-start.7 = (f32[400,128]{1,0:T(8,128)S(1)}, f32[400,128]{1,0:T(8,128)S(1)}, u32[]{:S(2)}, u32[]{:S(2)}) collective-permute-start(f32[400,128]{1,0:T(8,128)S(1)} %get-tuple-element.164), channel_id=1, source_target_pairs={{0,2},{1,3},{2,0},{3,1},{4,6},{5,7},{6,4},{7,5},{8,10},{9,11},{10,... | collective-permute-start | bytes 614408 | tf_op jit(solution)/shard_map/ppermute | solution.py:146
  17.5 12.5 %collective-permute-start.8 = (f32[400,128]{1,0:T(8,128)S(1)}, f32[400,128]{1,0:T(8,128)S(1)}, u32[]{:S(2)}, u32[]{:S(2)}) collective-permute-start(f32[400,128]{1,0:T(8,128)S(1)} %get-tuple-element.165), channel_id=1, source_target_pairs={{0,1},{1,2},{2,3},{3,0},{4,5},{5,6},{6,7},{7,4},{8,9},{9,10},{10,1... | collective-permute-start | bytes 614408 | tf_op jit(solution)/shard_map/ppermute | solution.py:146
  18.0 13.6 %collective-permute-start.9 = (f32[400,128]{1,0:T(8,128)S(1)}, f32[400,128]{1,0:T(8,128)S(1)}, u32[]{:S(2)}, u32[]{:S(2)}) collective-permute-start(f32[400,128]{1,0:T(8,128)S(1)} %get-tuple-element.166), channel_id=1, source_target_pairs={{0,3},{1,0},{2,1},{3,2},{4,7},{5,4},{6,5},{7,6},{8,11},{9,8},{10,9... | collective-permute-start | bytes 614408 | tf_op jit(solution)/shard_map/ppermute | solution.py:146
  20.3 25.5 %collective-permute-start.3 = (f32[400,128]{1,0:T(8,128)S(1)}, f32[400,128]{1,0:T(8,128)S(1)}, u32[]{:S(2)}, u32[]{:S(2)}) collective-permute-start(f32[400,128]{1,0:T(8,128)S(1)} %shard_map.30.one_ref), channel_id=1, source_target_pairs={{0,4},{4,0},{1,5},{5,1},{2,6},{6,2},{3,7},{7,3},{8,12},{12,8},{9,1... | collective-permute-start | bytes 614408 | tf_op jit(solution)/shard_map/ppermute | solution.py:141
  27.3 11.2 %collective-permute-start.4 = (f32[400,128]{1,0:T(8,128)S(1)}, f32[400,128]{1,0:T(8,128)S(1)}, u32[]{:S(2)}, u32[]{:S(2)}) collective-permute-start(f32[400,128]{1,0:T(8,128)S(1)} %get-tuple-element.161), channel_id=1, source_target_pairs={{0,2},{1,3},{2,0},{3,1},{4,6},{5,7},{6,4},{7,5},{8,10},{9,11},{10,... | collective-permute-start | bytes 614408 | tf_op jit(solution)/shard_map/ppermute | solution.py:146
  29.0 9.6 %collective-permute-start.5 = (f32[400,128]{1,0:T(8,128)S(1)}, f32[400,128]{1,0:T(8,128)S(1)}, u32[]{:S(2)}, u32[]{:S(2)}) collective-permute-start(f32[400,128]{1,0:T(8,128)S(1)} %get-tuple-element.162), channel_id=1, source_target_pairs={{0,1},{1,2},{2,3},{3,0},{4,5},{5,6},{6,7},{7,4},{8,9},{9,10},{10,1... | collective-permute-start | bytes 614408 | tf_op jit(solution)/shard_map/ppermute | solution.py:146
  29.9 8.7 %collective-permute-start.6 = (f32[400,128]{1,0:T(8,128)S(1)}, f32[400,128]{1,0:T(8,128)S(1)}, u32[]{:S(2)}, u32[]{:S(2)}) collective-permute-start(f32[400,128]{1,0:T(8,128)S(1)} %get-tuple-element.163), channel_id=1, source_target_pairs={{0,3},{1,0},{2,1},{3,2},{4,7},{5,4},{6,5},{7,6},{8,11},{9,8},{10,9... | collective-permute-start | bytes 614408 | tf_op jit(solution)/shard_map/ppermute | solution.py:146
  31.7 18.8 %collective-permute-start.13 = (f32[400,128]{1,0:T(8,128)S(1)}, f32[400,128]{1,0:T(8,128)S(1)}, u32[]{:S(2)}, u32[]{:S(2)}) collective-permute-start(f32[400,128]{1,0:T(8,128)S(1)} %shard_map.31.one_ref), channel_id=1, source_target_pairs={{0,4},{4,0},{1,5},{5,1},{2,6},{6,2},{3,7},{7,3},{8,12},{12,8},{9,1... | collective-permute-start | bytes 614408 | tf_op jit(solution)/shard_map/ppermute | solution.py:141
  38.6 22.1 %collective-permute-start.17 = (f32[400,128]{1,0:T(8,128)S(1)}, f32[400,128]{1,0:T(8,128)S(1)}, u32[]{:S(2)}, u32[]{:S(2)}) collective-permute-start(f32[400,128]{1,0:T(8,128)S(1)} %shard_map.32.one_ref), channel_id=1, source_target_pairs={{0,4},{4,0},{1,5},{5,1},{2,6},{6,2},{3,7},{7,3},{8,12},{12,8},{9,1... | collective-permute-start | bytes 614408 | tf_op jit(solution)/shard_map/ppermute | solution.py:141
  46.5 9.3 %all-to-all-start = ((f32[4,104,128]{2,1,0:T(8,128)}), f32[4,104,128]{2,1,0:T(8,128)S(1)}, u32[]{:S(2)}, u32[]{:S(2)}) async-start(f32[4,104,128]{2,1,0:T(8,128)} %shard_map.33), calls=%async_computation | async-start | bytes 425984 | tf_op jit(solution)/shard_map/all_to_all | solution.py:223
  55.8 8.6 %all-to-all-start.1 = ((f32[4,104,128]{2,1,0:T(8,128)}), f32[4,104,128]{2,1,0:T(8,128)S(1)}, u32[]{:S(2)}, u32[]{:S(2)}) async-start(f32[4,104,128]{2,1,0:T(8,128)} %shard_map.35), calls=%async_computation.1 | async-start | bytes 425984 | tf_op jit(solution)/shard_map/all_to_all | solution.py:223
  59.1 10.2 %collective-permute-start.12 = (f32[4,104,128]{2,1,0:T(8,128)S(1)}, f32[4,104,128]{2,1,0:T(8,128)S(1)}, u32[]{:S(2)}, u32[]{:S(2)}) collective-permute-start(f32[4,104,128]{2,1,0:T(8,128)S(1)} %all-to-all-done.a), channel_id=1, source_target_pairs={{0,3},{1,0},{2,1},{3,2},{4,7},{5,4},{6,5},{7,6},{8,11},{9,8},{10,9... | collective-permute-start | bytes 638984 | tf_op jit(solution)/shard_map/ppermute | solution.py:146
  59.2 13.8 %collective-permute-start.11 = (f32[4,104,128]{2,1,0:T(8,128)S(1)}, f32[4,104,128]{2,1,0:T(8,128)S(1)}, u32[]{:S(2)}, u32[]{:S(2)}) collective-permute-start(f32[4,104,128]{2,1,0:T(8,128)S(1)} %all-to-all-done.a), channel_id=1, source_target_pairs={{0,2},{1,3},{2,0},{3,1},{4,6},{5,7},{6,4},{7,5},{8,10},{9,11},{10,... | collective-permute-start | bytes 638984 | tf_op jit(solution)/shard_map/ppermute | solution.py:146
  60.0 13.5 %collective-permute-start.10 = (f32[4,104,128]{2,1,0:T(8,128)S(1)}, f32[4,104,128]{2,1,0:T(8,128)S(1)}, u32[]{:S(2)}, u32[]{:S(2)}) collective-permute-start(f32[4,104,128]{2,1,0:T(8,128)S(1)} %all-to-all-done.a), channel_id=1, source_target_pairs={{0,1},{1,2},{2,3},{3,0},{4,5},{5,6},{6,7},{7,4},{8,9},{9,10},{10,1... | collective-permute-start | bytes 638984 | tf_op jit(solution)/shard_map/ppermute | solution.py:146
  64.4 8.6 %all-to-all-start.2 = ((f32[4,104,128]{2,1,0:T(8,128)}), f32[4,104,128]{2,1,0:T(8,128)S(1)}, u32[]{:S(2)}, u32[]{:S(2)}) async-start(f32[4,104,128]{2,1,0:T(8,128)} %shard_map.37), calls=%async_computation.2 | async-start | bytes 425984 | tf_op jit(solution)/shard_map/all_to_all | solution.py:223
  67.9 7.0 %collective-permute-start.16 = (f32[4,104,128]{2,1,0:T(8,128)S(1)}, f32[4,104,128]{2,1,0:T(8,128)S(1)}, u32[]{:S(2)}, u32[]{:S(2)}) collective-permute-start(f32[4,104,128]{2,1,0:T(8,128)S(1)} %all-to-all-done.1.a), channel_id=1, source_target_pairs={{0,3},{1,0},{2,1},{3,2},{4,7},{5,4},{6,5},{7,6},{8,11},{9,8},{10,9... | collective-permute-start | bytes 638984 | tf_op jit(solution)/shard_map/ppermute | solution.py:146
  68.0 7.7 %collective-permute-start.15 = (f32[4,104,128]{2,1,0:T(8,128)S(1)}, f32[4,104,128]{2,1,0:T(8,128)S(1)}, u32[]{:S(2)}, u32[]{:S(2)}) collective-permute-start(f32[4,104,128]{2,1,0:T(8,128)S(1)} %all-to-all-done.1.a), channel_id=1, source_target_pairs={{0,2},{1,3},{2,0},{3,1},{4,6},{5,7},{6,4},{7,5},{8,10},{9,11},{10,... | collective-permute-start | bytes 638984 | tf_op jit(solution)/shard_map/ppermute | solution.py:146
  69.3 8.0 %collective-permute-start.14 = (f32[4,104,128]{2,1,0:T(8,128)S(1)}, f32[4,104,128]{2,1,0:T(8,128)S(1)}, u32[]{:S(2)}, u32[]{:S(2)}) collective-permute-start(f32[4,104,128]{2,1,0:T(8,128)S(1)} %all-to-all-done.1.a), channel_id=1, source_target_pairs={{0,1},{1,2},{2,3},{3,0},{4,5},{5,6},{6,7},{7,4},{8,9},{9,10},{10,1... | collective-permute-start | bytes 638984 | tf_op jit(solution)/shard_map/ppermute | solution.py:146
  73.0 14.2 %collective-permute-start.20 = (f32[4,104,128]{2,1,0:T(8,128)S(1)}, f32[4,104,128]{2,1,0:T(8,128)S(1)}, u32[]{:S(2)}, u32[]{:S(2)}) collective-permute-start(f32[4,104,128]{2,1,0:T(8,128)S(1)} %all-to-all-done.2.a), channel_id=1, source_target_pairs={{0,3},{1,0},{2,1},{3,2},{4,7},{5,4},{6,5},{7,6},{8,11},{9,8},{10,9... | collective-permute-start | bytes 638984 | tf_op jit(solution)/shard_map/ppermute | solution.py:146
  73.5 13.7 %collective-permute-start.19 = (f32[4,104,128]{2,1,0:T(8,128)S(1)}, f32[4,104,128]{2,1,0:T(8,128)S(1)}, u32[]{:S(2)}, u32[]{:S(2)}) collective-permute-start(f32[4,104,128]{2,1,0:T(8,128)S(1)} %all-to-all-done.2.a), channel_id=1, source_target_pairs={{0,2},{1,3},{2,0},{3,1},{4,6},{5,7},{6,4},{7,5},{8,10},{9,11},{10,... | collective-permute-start | bytes 638984 | tf_op jit(solution)/shard_map/ppermute | solution.py:146
  74.9 12.3 %collective-permute-start.18 = (f32[4,104,128]{2,1,0:T(8,128)S(1)}, f32[4,104,128]{2,1,0:T(8,128)S(1)}, u32[]{:S(2)}, u32[]{:S(2)}) collective-permute-start(f32[4,104,128]{2,1,0:T(8,128)S(1)} %all-to-all-done.2.a), channel_id=1, source_target_pairs={{0,1},{1,2},{2,3},{3,0},{4,5},{5,6},{6,7},{7,4},{8,9},{9,10},{10,1... | collective-permute-start | bytes 638984 | tf_op jit(solution)/shard_map/ppermute | solution.py:146
  77.3 6.9 %collective-permute-start.22 = (f32[416,128]{1,0:T(8,128)S(1)}, f32[416,128]{1,0:T(8,128)S(1)}, u32[]{:S(2)}, u32[]{:S(2)}) collective-permute-start(f32[416,128]{1,0:T(8,128)S(1)} %get-tuple-element.200.mine), channel_id=1, source_target_pairs={{0,24},{16,9},{25,1},{9,16},{2,26},{18,11},{27,3},{11,18},{4,28},{... | collective-permute-start | bytes 638984 | tf_op jit(solution)/shard_map/ppermute | solution.py:155
  81.9 4.6 %collective-permute-start.21 = (f32[416,128]{1,0:T(8,128)S(1)}, f32[416,128]{1,0:T(8,128)S(1)}, u32[]{:S(2)}, u32[]{:S(2)}) collective-permute-start(f32[416,128]{1,0:T(8,128)S(1)} %get-tuple-element.203.mine), channel_id=1, source_target_pairs={{0,24},{16,9},{25,1},{9,16},{2,26},{18,11},{27,3},{11,18},{4,28},{... | collective-permute-start | bytes 638984 | tf_op jit(solution)/shard_map/ppermute | solution.py:155
  84.8 8.8 %collective-permute-start.23 = (f32[416,128]{1,0:T(8,128)S(1)}, f32[416,128]{1,0:T(8,128)S(1)}, u32[]{:S(2)}, u32[]{:S(2)}) collective-permute-start(f32[416,128]{1,0:T(8,128)S(1)} %shard_map.38.refs_6_), channel_id=1, source_target_pairs={{0,8},{8,0},{16,24},{24,16},{1,9},{9,1},{17,25},{25,17},{2,10},{10... | collective-permute-start | bytes 638984 | tf_op jit(solution)/shard_map/ppermute | solution.py:234
  87.1 22.2 %collective-permute-start.26 = (f32[416,128]{1,0:T(8,128)S(1)}, f32[416,128]{1,0:T(8,128)S(1)}, u32[]{:S(2)}, u32[]{:S(2)}) collective-permute-start(f32[416,128]{1,0:T(8,128)S(1)} %shard_map.39.refs_6_), channel_id=1, source_target_pairs={{0,8},{8,0},{16,24},{24,16},{1,9},{9,1},{17,25},{25,17},{2,10},{10... | collective-permute-start | bytes 638984 | tf_op jit(solution)/shard_map/ppermute | solution.py:234
  87.6 23.7 %collective-permute-start.25 = (f32[416,128]{1,0:T(8,128)S(1)}, f32[416,128]{1,0:T(8,128)S(1)}, u32[]{:S(2)}, u32[]{:S(2)}) collective-permute-start(f32[416,128]{1,0:T(8,128)S(1)} %get-tuple-element.236.mine), channel_id=1, source_target_pairs={{0,24},{16,9},{25,1},{9,16},{2,26},{18,11},{27,3},{11,18},{4,28},{... | collective-permute-start | bytes 638984 | tf_op jit(solution)/shard_map/ppermute | solution.py:155
  95.5 16.5 %collective-permute-start.24 = (f32[4,384,128]{2,1,0:T(8,128)S(1)}, f32[4,384,128]{2,1,0:T(8,128)S(1)}, u32[]{:S(2)}, u32[]{:S(2)}) collective-permute-start(f32[4,384,128]{2,1,0:T(8,128)S(1)} %get-tuple-element.223), channel_id=1, source_target_pairs={{0,128},{128,0},{1,129},{129,1},{2,130},{130,2},{3,131},{131,3},{4... | collective-permute-start | bytes 2359304 | tf_op jit(solution)/shard_map/ppermute | solution.py:141
  111.3 7.9 %collective-permute-start.31 = (f32[4,384,128]{2,1,0:T(8,128)S(1)}, f32[4,384,128]{2,1,0:T(8,128)S(1)}, u32[]{:S(2)}, u32[]{:S(2)}) collective-permute-start(f32[4,384,128]{2,1,0:T(8,128)S(1)} %get-tuple-element.234), channel_id=1, source_target_pairs={{0,128},{128,0},{1,129},{129,1},{2,130},{130,2},{3,131},{131,3},{4... | collective-permute-start | bytes 2359304 | tf_op jit(solution)/shard_map/ppermute | solution.py:141
  111.9 7.3 %collective-permute-start.30 = (f32[416,128]{1,0:T(8,128)S(1)}, f32[416,128]{1,0:T(8,128)S(1)}, u32[]{:S(2)}, u32[]{:S(2)}) collective-permute-start(f32[416,128]{1,0:T(8,128)S(1)} %shard_map.43.refs_6_), channel_id=1, source_target_pairs={{0,8},{8,0},{16,24},{24,16},{1,9},{9,1},{17,25},{25,17},{2,10},{10... | collective-permute-start | bytes 638984 | tf_op jit(solution)/shard_map/ppermute | solution.py:234
  112.2 12.7 %collective-permute-start.27 = (f32[384,128]{1,0:T(8,128)S(1)}, f32[384,128]{1,0:T(8,128)S(1)}, u32[]{:S(2)}, u32[]{:S(2)}) collective-permute-start(f32[384,128]{1,0:T(8,128)S(1)} %get-tuple-element.242), channel_id=1, source_target_pairs={{0,64},{32,96},{64,0},{96,32},{1,65},{33,97},{65,1},{97,33},{2,66}... | collective-permute-start | bytes 589832 | tf_op jit(solution)/shard_map/ppermute | solution.py:146
  116.4 10.9 %collective-permute-start.28 = (f32[384,128]{1,0:T(8,128)S(1)}, f32[384,128]{1,0:T(8,128)S(1)}, u32[]{:S(2)}, u32[]{:S(2)}) collective-permute-start(f32[384,128]{1,0:T(8,128)S(1)} %get-tuple-element.243), channel_id=1, source_target_pairs={{0,32},{32,64},{64,96},{96,0},{1,33},{33,65},{65,97},{97,1},{2,34}... | collective-permute-start | bytes 589832 | tf_op jit(solution)/shard_map/ppermute | solution.py:146
  116.7 12.8 %collective-permute-start.29 = (f32[384,128]{1,0:T(8,128)S(1)}, f32[384,128]{1,0:T(8,128)S(1)}, u32[]{:S(2)}, u32[]{:S(2)}) collective-permute-start(f32[384,128]{1,0:T(8,128)S(1)} %get-tuple-element.244), channel_id=1, source_target_pairs={{0,96},{32,0},{64,32},{96,64},{1,97},{33,1},{65,33},{97,65},{2,98}... | collective-permute-start | bytes 589832 | tf_op jit(solution)/shard_map/ppermute | solution.py:146
  119.2 12.3 %collective-permute-start.32 = (f32[384,128]{1,0:T(8,128)S(1)}, f32[384,128]{1,0:T(8,128)S(1)}, u32[]{:S(2)}, u32[]{:S(2)}) collective-permute-start(f32[384,128]{1,0:T(8,128)S(1)} %get-tuple-element.264), channel_id=1, source_target_pairs={{0,64},{32,96},{64,0},{96,32},{1,65},{33,97},{65,1},{97,33},{2,66}... | collective-permute-start | bytes 589832 | tf_op jit(solution)/shard_map/ppermute | solution.py:146
  122.6 11.9 %collective-permute-start.33 = (f32[384,128]{1,0:T(8,128)S(1)}, f32[384,128]{1,0:T(8,128)S(1)}, u32[]{:S(2)}, u32[]{:S(2)}) collective-permute-start(f32[384,128]{1,0:T(8,128)S(1)} %get-tuple-element.265), channel_id=1, source_target_pairs={{0,32},{32,64},{64,96},{96,0},{1,33},{33,65},{65,97},{97,1},{2,34}... | collective-permute-start | bytes 589832 | tf_op jit(solution)/shard_map/ppermute | solution.py:146
  124.9 9.6 %collective-permute-start.34 = (f32[384,128]{1,0:T(8,128)S(1)}, f32[384,128]{1,0:T(8,128)S(1)}, u32[]{:S(2)}, u32[]{:S(2)}) collective-permute-start(f32[384,128]{1,0:T(8,128)S(1)} %get-tuple-element.266), channel_id=1, source_target_pairs={{0,96},{32,0},{64,32},{96,64},{1,97},{33,1},{65,33},{97,65},{2,98}... | collective-permute-start | bytes 589832 | tf_op jit(solution)/shard_map/ppermute | solution.py:146
  127.3 4.1 %collective-permute-start.35 = (f32[4,384,128]{2,1,0:T(8,128)S(1)}, f32[4,384,128]{2,1,0:T(8,128)S(1)}, u32[]{:S(2)}, u32[]{:S(2)}) collective-permute-start(f32[4,384,128]{2,1,0:T(8,128)S(1)} %get-tuple-element.259), channel_id=1, source_target_pairs={{0,128},{128,0},{1,129},{129,1},{2,130},{130,2},{3,131},{131,3},{4... | collective-permute-start | bytes 2359304 | tf_op jit(solution)/shard_map/ppermute | solution.py:141
  134.5 7.2 %collective-permute-start.36 = (f32[384,128]{1,0:T(8,128)S(1)}, f32[384,128]{1,0:T(8,128)S(1)}, u32[]{:S(2)}, u32[]{:S(2)}) collective-permute-start(f32[384,128]{1,0:T(8,128)S(1)} %get-tuple-element.276), channel_id=1, source_target_pairs={{0,64},{32,96},{64,0},{96,32},{1,65},{33,97},{65,1},{97,33},{2,66}... | collective-permute-start | bytes 589832 | tf_op jit(solution)/shard_map/ppermute | solution.py:146
  135.8 11.2 %collective-permute-start.37 = (f32[384,128]{1,0:T(8,128)S(1)}, f32[384,128]{1,0:T(8,128)S(1)}, u32[]{:S(2)}, u32[]{:S(2)}) collective-permute-start(f32[384,128]{1,0:T(8,128)S(1)} %get-tuple-element.277), channel_id=1, source_target_pairs={{0,32},{32,64},{64,96},{96,0},{1,33},{33,65},{65,97},{97,1},{2,34}... | collective-permute-start | bytes 589832 | tf_op jit(solution)/shard_map/ppermute | solution.py:146
  137.0 10.0 %collective-permute-start.38 = (f32[384,128]{1,0:T(8,128)S(1)}, f32[384,128]{1,0:T(8,128)S(1)}, u32[]{:S(2)}, u32[]{:S(2)}) collective-permute-start(f32[384,128]{1,0:T(8,128)S(1)} %get-tuple-element.278), channel_id=1, source_target_pairs={{0,96},{32,0},{64,32},{96,64},{1,97},{33,1},{65,33},{97,65},{2,98}... | collective-permute-start | bytes 589832 | tf_op jit(solution)/shard_map/ppermute | solution.py:146

commit v5 on v4

--- a/solution.py
+++ b/solution.py
@@ -11,9 +11,9 @@
 SPLIT = (104, 96, 104, 96)
 PADDED = 104
 DEPTH = 4 * PADDED
-VMEM_LIMIT = 32 * 1024 * 1024
+VMEM_LIMIT = 24 * 1024 * 1024
 HALF_LIMIT = 60 * 1024 * 1024
-COST = pl.CostEstimate(flops=int(20e9), bytes_accessed=int(74e6), transcendentals=0)
+COST = pl.CostEstimate(flops=int(12e9), bytes_accessed=int(44e6), transcendentals=0)
 
 
 def halves(value):
@@ -211,12 +211,14 @@
     rest = order(functools.partial(half_call, 1, 2), y_here, three_index, coeff)
     sends = [first, rest[:4], rest[4:]]
 
-    def sum_y(c):
+    def send_y(c):
         own, one, two, three = sends[c]
         if c == 2:
             one, two, three = lax.optimization_barrier((one, two, three, sums[0][0]))[:3]
-        far, near, back = shifted(two, "y", 2), shifted(one, "y", 1), shifted(three, "y", 3)
-        total = order(sum_call, own, far, near, back)
+        return own, shifted(two, "y", 2), shifted(one, "y", 1), shifted(three, "y", 3)
+
+    def sum_y(parts):
+        total = order(sum_call, *parts)
         return total, swapped(total, "zh")
 
     def over_x(total, other):
@@ -227,7 +229,8 @@
 
     def left_of(blocks):
         high, low, mine = order(left_call, y_here, pick, *blocks)
-        return [high, low], mine, crossing(mine)
+        lefts.extend([high, low])
+        return mine, crossing(mine)
 
     def pair_of(mine, crossed):
         have = order(have_call, flags, mine, crossed)
@@ -241,23 +244,25 @@
         own, one, two, three = order(add_call, x_here, keep, given)
         return [own, shifted(two, "x", 2), shifted(one, "x", 1), shifted(three, "x", 3)]
 
-    sums = []
-    for c in range(3):
-        sums.append(sum_y(c))
-    blocks = []
-    for c in range(3):
-        block = over_x(*sums[c])
-        order.after(block)
-        blocks.append(over_y(block))
-    left0, mine0, crossed0 = left_of(blocks[0])
-    left1, mine1, crossed1 = left_of(blocks[1])
-    pair0 = pair_of(mine0, crossed0)
-    pair1 = pair_of(mine1, crossed1)
-    left2, mine2, crossed2 = left_of(blocks[2])
-    lefts = left0 + left1 + left2
+    sums, lefts = [], []
+    sums.append(sum_y(send_y(0)))
+    sums.append(sum_y(send_y(1)))
+    parts2 = send_y(2)
+    order.after(parts2[1])
+    block0 = over_x(*sums[0])
+    sums.append(sum_y(parts2))
+    block1 = over_x(*sums[1])
+    blocks0 = over_y(block0)
+    blocks1 = over_y(block1)
+    blocks2 = over_y(over_x(*sums[2]))
+    half0 = left_of(blocks0)
+    half1 = left_of(blocks1)
+    pair0 = pair_of(*half0)
+    half2 = left_of(blocks2)
+    pair1 = pair_of(*half1)
     tile0 = tile_of(pair0)
     tile1 = tile_of(pair1)
-    pair2 = pair_of(mine2, crossed2)
+    pair2 = pair_of(*half2)
     out0 = over_x_sum(*tile0)
     out1 = over_x_sum(*tile1)
     tile2 = tile_of(pair2)

time: 148 us -> 145 us (0.980)
  waiting for transfers between devices: 29.1 us -> 22.5 us
  starting transfers between devices: 95 us -> 97.3 us
    all_to_all x3, waiting for transfers between devices: 10.4 us -> 3.63 us  [over_x(): lax.all_to_all(order(piece_call, total, other), 'x', 0, 0, tiled=True)]
    ppermute x27, starting transfers between devices: 35.8 us -> 42.2 us  [shifted(): lax.ppermute(value, axis, [(i, (i + distance) % size) for i in range(size)])]
    ppermute x3, starting transfers between devices: 11.4 us -> 7.4 us  [along(): return lax.ppermute(value, ('zl', 'y'), pairs)]
    ppermute x6, starting transfers between devices: 36.9 us -> 34.4 us  [swapped(): return lax.ppermute(value, axis, [(0, 1), (1, 0)])]
    ppermute x3, starting transfers between devices: 0.28 us -> 2.42 us  [pair_of(): return (have, lax.ppermute(have, 'zl', [(0, 1), (1, 0), (2, 3), (3, 2)]))]
    ppermute x27, waiting for transfers between devices: 14.2 us -> 15.9 us  [shifted(): lax.ppermute(value, axis, [(i, (i + distance) % size) for i in range(size)])]
    ppermute x3, waiting for transfers between devices: 2.65 us -> 1.04 us  [along(): return lax.ppermute(value, ('zl', 'y'), pairs)]
  transfers between devices with their start and end apart: 42 -> 42, of which waited for: 12 -> 11; matrix products, arithmetic and copies ran while one was open for 0% -> 0% of each run, Pallas kernels for 11% -> 11%
where the time goes in v5:
time: 145 us; the launch traced here: 143 us
  starting transfers between devices  97.3 us (67%)
  waiting for transfers between devices  22.5 us (16%)
  Pallas kernels  21.6 us (15%)
  local copies, waits for them, and re-layouts  1.67 us (1%)
    ppermute x27, starting transfers between devices, shifted(): lax.ppermute(value, axis, [(i, (i + distance) % size) for i in range(size)])  42.2 us
    ppermute x6, starting transfers between devices, swapped(): return lax.ppermute(value, axis, [(0, 1), (1, 0)])  34.4 us
    ppermute x27, waiting for transfers between devices, shifted(): lax.ppermute(value, axis, [(i, (i + distance) % size) for i in range(size)])  15.9 us
    pallas_call x21, Pallas kernels, __call__(): result = kernel(*operands)  12.3 us
    all_to_all x3, starting transfers between devices, over_x(): lax.all_to_all(order(piece_call, total, other), 'x', 0, 0, tiled=True)  10.8 us
    pallas_call x2, Pallas kernels, half_call(): pl.pallas_call(functools.partial(half_kernel, count), out_shape=[f32(size...  9.26 us
    ppermute x3, starting transfers between devices, along(): return lax.ppermute(value, ('zl', 'y'), pairs)  7.4 us
    all_to_all x3, waiting for transfers between devices, over_x(): lax.all_to_all(order(piece_call, total, other), 'x', 0, 0, tiled=True)  3.63 us
  transfers between devices with their start and end apart: 42, of which 11 were waited for; matrix products, arithmetic and copies ran while one was open for 0% of the time, Pallas kernels for 11%

profile of v5, /device:TPU:1, one launch (start us, length us, event | category | flops | bytes accessed | tf_op | source)
XLA Modules:
  0.0 143.4 jit_solution(12022463694063588089)
XLA Ops:
  0.0 4.9 %shard_map.28 = (f32[400,128]{1,0:T(8,128)}, f32[400,128]{1,0:T(8,128)}, f32[400,128]{1,0:T(8,128)}, f32[400,128]{1,0:T(8,128)}) custom-call(s32[1]{0:T(128)} %bitcast.3.here_ref, f32[800,768]{1,0:T(8,128)} %bitcast.6, f32[2,384,768]{2,1,0:T(8,128)} %refs_1_), custom_call_target="tpu_custom_call" | custom-call | flops 12000000000 | bytes 44000000 | tf_op jit(solution)/shard_map/pallas_call | solution.py:72
  4.9 3.7 %collective-permute-start = (f32[400,128]{1,0:T(8,128)}, f32[400,128]{1,0:T(8,128)S(1)}, u32[]{:S(2)}, u32[]{:S(2)}) collective-permute-start(f32[400,128]{1,0:T(8,128)} %get-tuple-element.146), channel_id=1, source_target_pairs={{0,2},{1,3},{2,0},{3,1},{4,6},{5,7},{6,4},{7,5},{8,10},{9,11},{10,... | collective-permute-start | bytes 614408 | tf_op jit(solution)/shard_map/ppermute | solution.py:146
  9.0 2.3 %collective-permute-start.2 = (f32[400,128]{1,0:T(8,128)}, f32[400,128]{1,0:T(8,128)S(1)}, u32[]{:S(2)}, u32[]{:S(2)}) collective-permute-start(f32[400,128]{1,0:T(8,128)} %get-tuple-element.148), channel_id=1, source_target_pairs={{0,3},{1,0},{2,1},{3,2},{4,7},{5,4},{6,5},{7,6},{8,11},{9,8},{10,9... | collective-permute-start | bytes 614408 | tf_op jit(solution)/shard_map/ppermute | solution.py:146
  11.3 1.7 %copy-done.1 = f32[2,384,768]{2,1,0:T(8,128)S(1)} copy-done((f32[2,384,768]{2,1,0:T(8,128)S(1)}, f32[2,384,768]{2,1,0:T(8,128)}, u32[]{:S(2)}) %copy-start.1) | copy-done | bytes 2359320
  13.0 4.4 %shard_map.29 = (f32[400,128]{1,0:T(8,128)S(1)}, f32[400,128]{1,0:T(8,128)S(1)}, f32[400,128]{1,0:T(8,128)S(1)}, f32[400,128]{1,0:T(8,128)S(1)}, f32[400,128]{1,...) custom-call(s32[1]{0:T(128)} %bitcast.3.here_ref, f32[800,768]{1,0:T(8,128)S(1)} %bitcast.7, ...), custom_call_target="tpu_custom_call" | custom-call | flops 12000000000 | bytes 44000000 | tf_op jit(solution)/shard_map/pallas_call | solution.py:72
  18.0 2.2 %collective-permute-start.13 = (f32[400,128]{1,0:T(8,128)S(1)}, f32[400,128]{1,0:T(8,128)S(1)}, u32[]{:S(2)}, u32[]{:S(2)}) collective-permute-start(f32[400,128]{1,0:T(8,128)S(1)} %get-tuple-element.172), channel_id=1, source_target_pairs={{0,3},{1,0},{2,1},{3,2},{4,7},{5,4},{6,5},{7,6},{8,11},{9,8},{10,9... | collective-permute-start | bytes 614408 | tf_op jit(solution)/shard_map/ppermute | solution.py:146
  20.3 7.0 %collective-permute-start.3 = (f32[400,128]{1,0:T(8,128)S(1)}, f32[400,128]{1,0:T(8,128)S(1)}, u32[]{:S(2)}, u32[]{:S(2)}) collective-permute-start(f32[400,128]{1,0:T(8,128)S(1)} %shard_map.30.one_ref), channel_id=1, source_target_pairs={{0,4},{4,0},{1,5},{5,1},{2,6},{6,2},{3,7},{7,3},{8,12},{12,8},{9,1... | collective-permute-start | bytes 614408 | tf_op jit(solution)/shard_map/ppermute | solution.py:141
  27.3 1.7 %collective-permute-start.7 = (f32[400,128]{1,0:T(8,128)S(1)}, f32[400,128]{1,0:T(8,128)S(1)}, u32[]{:S(2)}, u32[]{:S(2)}) collective-permute-start(f32[400,128]{1,0:T(8,128)S(1)} %get-tuple-element.163), channel_id=1, source_target_pairs={{0,2},{1,3},{2,0},{3,1},{4,6},{5,7},{6,4},{7,5},{8,10},{9,11},{10,... | collective-permute-start | bytes 614408 | tf_op jit(solution)/shard_map/ppermute | solution.py:146
  29.0 1.0 collective-permute-done.12.c
  29.9 1.7 %collective-permute-start.9 = (f32[400,128]{1,0:T(8,128)S(1)}, f32[400,128]{1,0:T(8,128)S(1)}, u32[]{:S(2)}, u32[]{:S(2)}) collective-permute-start(f32[400,128]{1,0:T(8,128)S(1)} %get-tuple-element.165), channel_id=1, source_target_pairs={{0,3},{1,0},{2,1},{3,2},{4,7},{5,4},{6,5},{7,6},{8,11},{9,8},{10,9... | collective-permute-start | bytes 614408 | tf_op jit(solution)/shard_map/ppermute | solution.py:146
  31.7 6.7 %collective-permute-start.14 = (f32[400,128]{1,0:T(8,128)S(1)}, f32[400,128]{1,0:T(8,128)S(1)}, u32[]{:S(2)}, u32[]{:S(2)}) collective-permute-start(f32[400,128]{1,0:T(8,128)S(1)} %shard_map.33.one_ref), channel_id=1, source_target_pairs={{0,4},{4,0},{1,5},{5,1},{2,6},{6,2},{3,7},{7,3},{8,12},{12,8},{9,1... | collective-permute-start | bytes 614408 | tf_op jit(solution)/shard_map/ppermute | solution.py:141
  38.4 0.7 shard_map.31
  39.2 4.0 %all-to-all-start = ((f32[4,104,128]{2,1,0:T(8,128)}), f32[4,104,128]{2,1,0:T(8,128)S(1)}, u32[]{:S(2)}, u32[]{:S(2)}) async-start(f32[4,104,128]{2,1,0:T(8,128)} %shard_map.31), calls=%async_computation | async-start | bytes 425984 | tf_op jit(solution)/shard_map/all_to_all | solution.py:225
  43.2 2.5 %collective-permute-start.10 = (f32[400,128]{1,0:T(8,128)S(1)}, f32[400,128]{1,0:T(8,128)S(1)}, u32[]{:S(2)}, u32[]{:S(2)}) collective-permute-start(f32[400,128]{1,0:T(8,128)S(1)} %shard_map.32.one_ref), channel_id=1, source_target_pairs={{0,4},{4,0},{1,5},{5,1},{2,6},{6,2},{3,7},{7,3},{8,12},{12,8},{9,1... | collective-permute-start | bytes 614408 | tf_op jit(solution)/shard_map/ppermute | solution.py:141
  45.8 0.7 shard_map.34
  46.5 2.0 %all-to-all-done.a = f32[4,104,128]{2,1,0:T(8,128)S(1)} async-done(((f32[4,104,128]{2,1,0:T(8,128)}), f32[4,104,128]{2,1,0:T(8,128)S(1)}, u32[]{:S(2)}, u32[]{:S(2)}) %all-to-all-start) | async-done | bytes 213024 | tf_op jit(solution)/shard_map/all_to_all | solution.py:225
  48.4 3.4 %all-to-all-start.1 = ((f32[4,104,128]{2,1,0:T(8,128)}), f32[4,104,128]{2,1,0:T(8,128)S(1)}, u32[]{:S(2)}, u32[]{:S(2)}) async-start(f32[4,104,128]{2,1,0:T(8,128)} %shard_map.34), calls=%async_computation.1 | async-start | bytes 425984 | tf_op jit(solution)/shard_map/all_to_all | solution.py:225
  52.3 2.9 %collective-permute-start.5 = (f32[4,104,128]{2,1,0:T(8,128)S(1)}, f32[4,104,128]{2,1,0:T(8,128)S(1)}, u32[]{:S(2)}, u32[]{:S(2)}) collective-permute-start(f32[4,104,128]{2,1,0:T(8,128)S(1)} %all-to-all-done.a), channel_id=1, source_target_pairs={{0,2},{1,3},{2,0},{3,1},{4,6},{5,7},{6,4},{7,5},{8,10},{9,11},{10,... | collective-permute-start | bytes 638984 | tf_op jit(solution)/shard_map/ppermute | solution.py:146
  55.2 0.7 shard_map.35
  55.9 1.5 %all-to-all-done.1.a = f32[4,104,128]{2,1,0:T(8,128)S(1)} async-done(((f32[4,104,128]{2,1,0:T(8,128)}), f32[4,104,128]{2,1,0:T(8,128)S(1)}, u32[]{:S(2)}, u32[]{:S(2)}) %all-to-all-start.1) | async-done | bytes 213024 | tf_op jit(solution)/shard_map/all_to_all | solution.py:225
  57.3 3.4 %all-to-all-start.2 = ((f32[4,104,128]{2,1,0:T(8,128)}), f32[4,104,128]{2,1,0:T(8,128)S(1)}, u32[]{:S(2)}, u32[]{:S(2)}) async-start(f32[4,104,128]{2,1,0:T(8,128)} %shard_map.35), calls=%async_computation.2 | async-start | bytes 425984 | tf_op jit(solution)/shard_map/all_to_all | solution.py:225
  60.9 1.9 %collective-permute-start.17 = (f32[4,104,128]{2,1,0:T(8,128)S(1)}, f32[4,104,128]{2,1,0:T(8,128)S(1)}, u32[]{:S(2)}, u32[]{:S(2)}) collective-permute-start(f32[4,104,128]{2,1,0:T(8,128)S(1)} %all-to-all-done.1.a), channel_id=1, source_target_pairs={{0,3},{1,0},{2,1},{3,2},{4,7},{5,4},{6,5},{7,6},{8,11},{9,8},{10,9... | collective-permute-start | bytes 638984 | tf_op jit(solution)/shard_map/ppermute | solution.py:146
  62.7 3.0 %collective-permute-start.16 = (f32[4,104,128]{2,1,0:T(8,128)S(1)}, f32[4,104,128]{2,1,0:T(8,128)S(1)}, u32[]{:S(2)}, u32[]{:S(2)}) collective-permute-start(f32[4,104,128]{2,1,0:T(8,128)S(1)} %all-to-all-done.1.a), channel_id=1, source_target_pairs={{0,2},{1,3},{2,0},{3,1},{4,6},{5,7},{6,4},{7,5},{8,10},{9,11},{10,... | collective-permute-start | bytes 638984 | tf_op jit(solution)/shard_map/ppermute | solution.py:146
  66.0 2.5 %collective-permute-start.20 = (f32[4,104,128]{2,1,0:T(8,128)S(1)}, f32[4,104,128]{2,1,0:T(8,128)S(1)}, u32[]{:S(2)}, u32[]{:S(2)}) collective-permute-start(f32[4,104,128]{2,1,0:T(8,128)S(1)} %all-to-all-done.2.a), channel_id=1, source_target_pairs={{0,3},{1,0},{2,1},{3,2},{4,7},{5,4},{6,5},{7,6},{8,11},{9,8},{10,9... | collective-permute-start | bytes 638984 | tf_op jit(solution)/shard_map/ppermute | solution.py:146
  68.5 2.5 %collective-permute-start.19 = (f32[4,104,128]{2,1,0:T(8,128)S(1)}, f32[4,104,128]{2,1,0:T(8,128)S(1)}, u32[]{:S(2)}, u32[]{:S(2)}) collective-permute-start(f32[4,104,128]{2,1,0:T(8,128)S(1)} %all-to-all-done.2.a), channel_id=1, source_target_pairs={{0,2},{1,3},{2,0},{3,1},{4,6},{5,7},{6,4},{7,5},{8,10},{9,11},{10,... | collective-permute-start | bytes 638984 | tf_op jit(solution)/shard_map/ppermute | solution.py:146
  71.8 3.1 %collective-permute-start.21 = (f32[416,128]{1,0:T(8,128)S(1)}, f32[416,128]{1,0:T(8,128)S(1)}, u32[]{:S(2)}, u32[]{:S(2)}) collective-permute-start(f32[416,128]{1,0:T(8,128)S(1)} %get-tuple-element.199.mine), channel_id=1, source_target_pairs={{0,24},{16,9},{25,1},{9,16},{2,26},{18,11},{27,3},{11,18},{4,28},{... | collective-permute-start | bytes 638984 | tf_op jit(solution)/shard_map/ppermute | solution.py:155
  75.3 1.3 collective-permute-start.23
  76.6 1.0 collective-permute-done.21.crossed
  78.3 3.4 %collective-permute-done.18.b = f32[4,104,128]{2,1,0:T(8,128)S(1)} collective-permute-done((f32[4,104,128]{2,1,0:T(8,128)S(1)}, f32[4,104,128]{2,1,0:T(8,128)S(1)}, u32[]{:S(2)}, u32[]{:S(2)}) %collective-permute-start.18) | collective-permute-done | bytes 213024 | tf_op jit(solution)/shard_map/ppermute | solution.py:146
  82.7 2.2 %collective-permute-start.26 = (f32[416,128]{1,0:T(8,128)S(1)}, f32[416,128]{1,0:T(8,128)S(1)}, u32[]{:S(2)}, u32[]{:S(2)}) collective-permute-start(f32[416,128]{1,0:T(8,128)S(1)} %shard_map.40.refs_6_), channel_id=1, source_target_pairs={{0,8},{8,0},{16,24},{24,16},{1,9},{9,1},{17,25},{25,17},{2,10},{10... | collective-permute-start | bytes 638984 | tf_op jit(solution)/shard_map/ppermute | solution.py:237
  84.9 3.0 %collective-permute-start.25 = (f32[416,128]{1,0:T(8,128)S(1)}, f32[416,128]{1,0:T(8,128)S(1)}, u32[]{:S(2)}, u32[]{:S(2)}) collective-permute-start(f32[416,128]{1,0:T(8,128)S(1)} %get-tuple-element.236.mine), channel_id=1, source_target_pairs={{0,24},{16,9},{25,1},{9,16},{2,26},{18,11},{27,3},{11,18},{4,28},{... | collective-permute-start | bytes 638984 | tf_op jit(solution)/shard_map/ppermute | solution.py:155
  87.9 2.0 %shard_map.41 = (f32[4,384,128]{2,1,0:T(8,128)S(1)}, f32[4,384,128]{2,1,0:T(8,128)S(1)}) custom-call(s32[2]{0:T(128)S(1)} %add_convert_fusion.flags_ref, bf16[4,128,416]{2,1,0:T(8,128)(2,1)S(1)} %get-tuple-element.251.refs_0_, bf16[4,128,416]{2,1,0:T(8,128)(2,1)S(1)} %get-tuple-element.252.refs_1_, bf16[4,128,416]{2,1,0:T(8,128)(2,1)S(1)} %get-tuple-element.253.refs_2_, ...), custom_call_target="tpu_custom_call" | custom-call | flops 12000000000 | bytes 44000000 | tf_op jit(solution)/shard_map/pallas_call | solution.py:175
  89.9 15.9 %collective-permute-start.24 = (f32[4,384,128]{2,1,0:T(8,128)S(1)}, f32[4,384,128]{2,1,0:T(8,128)S(1)}, u32[]{:S(2)}, u32[]{:S(2)}) collective-permute-start(f32[4,384,128]{2,1,0:T(8,128)S(1)} %get-tuple-element.223), channel_id=1, source_target_pairs={{0,128},{128,0},{1,129},{129,1},{2,130},{130,2},{3,131},{131,3},{4... | collective-permute-start | bytes 2359304 | tf_op jit(solution)/shard_map/ppermute | solution.py:141
  105.8 2.0 %shard_map.42 = (f32[4,384,128]{2,1,0:T(8,128)S(1)}, f32[4,384,128]{2,1,0:T(8,128)S(1)}) custom-call(s32[2]{0:T(128)S(1)} %add_convert_fusion.flags_ref, bf16[4,128,416]{2,1,0:T(8,128)(2,1)S(1)} %get-tuple-element.251.refs_0_, bf16[4,128,416]{2,1,0:T(8,128)(2,1)S(1)} %get-tuple-element.252.refs_1_, bf16[4,128,416]{2,1,0:T(8,128)(2,1)S(1)} %get-tuple-element.253.refs_2_, ...), custom_call_target="tpu_custom_call" | custom-call | flops 12000000000 | bytes 44000000 | tf_op jit(solution)/shard_map/pallas_call | solution.py:175
  108.7 3.3 %collective-permute-start.27 = (f32[384,128]{1,0:T(8,128)S(1)}, f32[384,128]{1,0:T(8,128)S(1)}, u32[]{:S(2)}, u32[]{:S(2)}) collective-permute-start(f32[384,128]{1,0:T(8,128)S(1)} %get-tuple-element.242), channel_id=1, source_target_pairs={{0,64},{32,96},{64,0},{96,32},{1,65},{33,97},{65,1},{97,33},{2,66}... | collective-permute-start | bytes 589832 | tf_op jit(solution)/shard_map/ppermute | solution.py:146
  112.3 2.4 %collective-permute-start.29 = (f32[384,128]{1,0:T(8,128)S(1)}, f32[384,128]{1,0:T(8,128)S(1)}, u32[]{:S(2)}, u32[]{:S(2)}) collective-permute-start(f32[384,128]{1,0:T(8,128)S(1)} %get-tuple-element.244), channel_id=1, source_target_pairs={{0,96},{32,0},{64,32},{96,64},{1,97},{33,1},{65,33},{97,65},{2,98}... | collective-permute-start | bytes 589832 | tf_op jit(solution)/shard_map/ppermute | solution.py:146
  114.9 3.2 %collective-permute-start.32 = (f32[384,128]{1,0:T(8,128)S(1)}, f32[384,128]{1,0:T(8,128)S(1)}, u32[]{:S(2)}, u32[]{:S(2)}) collective-permute-start(f32[384,128]{1,0:T(8,128)S(1)} %get-tuple-element.264), channel_id=1, source_target_pairs={{0,64},{32,96},{64,0},{96,32},{1,65},{33,97},{65,1},{97,33},{2,66}... | collective-permute-start | bytes 589832 | tf_op jit(solution)/shard_map/ppermute | solution.py:146
  118.4 2.0 %shard_map.46 = (f32[4,384,128]{2,1,0:T(8,128)S(1)}, f32[4,384,128]{2,1,0:T(8,128)S(1)}) custom-call(s32[2]{0:T(128)S(1)} %add_convert_fusion.flags_ref, bf16[4,128,416]{2,1,0:T(8,128)(2,1)S(1)} %get-tuple-element.251.refs_0_, bf16[4,128,416]{2,1,0:T(8,128)(2,1)S(1)} %get-tuple-element.252.refs_1_, bf16[4,128,416]{2,1,0:T(8,128)(2,1)S(1)} %get-tuple-element.253.refs_2_, ...), custom_call_target="tpu_custom_call" | custom-call | flops 12000000000 | bytes 44000000 | tf_op jit(solution)/shard_map/pallas_call | solution.py:175
  120.4 2.5 %collective-permute-start.34 = (f32[384,128]{1,0:T(8,128)S(1)}, f32[384,128]{1,0:T(8,128)S(1)}, u32[]{:S(2)}, u32[]{:S(2)}) collective-permute-start(f32[384,128]{1,0:T(8,128)S(1)} %get-tuple-element.266), channel_id=1, source_target_pairs={{0,96},{32,0},{64,32},{96,64},{1,97},{33,1},{65,33},{97,65},{2,98}... | collective-permute-start | bytes 589832 | tf_op jit(solution)/shard_map/ppermute | solution.py:146
  122.9 2.1 %collective-permute-start.35 = (f32[4,384,128]{2,1,0:T(8,128)S(1)}, f32[4,384,128]{2,1,0:T(8,128)S(1)}, u32[]{:S(2)}, u32[]{:S(2)}) collective-permute-start(f32[4,384,128]{2,1,0:T(8,128)S(1)} %get-tuple-element.259), channel_id=1, source_target_pairs={{0,128},{128,0},{1,129},{129,1},{2,130},{130,2},{3,131},{131,3},{4... | collective-permute-start | bytes 2359304 | tf_op jit(solution)/shard_map/ppermute | solution.py:141
  125.1 1.9 %collective-permute-done.35.two_ref = f32[4,384,128]{2,1,0:T(8,128)S(1)} collective-permute-done((f32[4,384,128]{2,1,0:T(8,128)S(1)}, f32[4,384,128]{2,1,0:T(8,128)S(1)}, u32[]{:S(2)}, u32[]{:S(2)}) %collective-permute-start.35) | collective-permute-done | bytes 786464 | tf_op jit(solution)/shard_map/ppermute | solution.py:141
  127.0 3.0 %collective-permute-done.33.c = f32[384,128]{1,0:T(8,128)S(1)} collective-permute-done((f32[384,128]{1,0:T(8,128)S(1)}, f32[384,128]{1,0:T(8,128)S(1)}, u32[]{:S(2)}, u32[]{:S(2)}) %collective-permute-start.33) | collective-permute-done | bytes 196640 | tf_op jit(solution)/shard_map/ppermute | solution.py:146
  130.0 1.3 collective-permute-start.36
  131.3 1.2 collective-permute-start.37
  132.5 1.4 %collective-permute-start.38 = (f32[384,128]{1,0:T(8,128)S(1)}, f32[384,128]{1,0:T(8,128)S(1)}, u32[]{:S(2)}, u32[]{:S(2)}) collective-permute-start(f32[384,128]{1,0:T(8,128)S(1)} %get-tuple-element.278), channel_id=1, source_target_pairs={{0,96},{32,0},{64,32},{96,64},{1,97},{33,1},{65,33},{97,65},{2,98}... | collective-permute-start | bytes 589832 | tf_op jit(solution)/shard_map/ppermute | solution.py:146
  134.0 3.2 %collective-permute-done.36.b = f32[384,128]{1,0:T(8,128)S(1)} collective-permute-done((f32[384,128]{1,0:T(8,128)S(1)}, f32[384,128]{1,0:T(8,128)S(1)}, u32[]{:S(2)}, u32[]{:S(2)}) %collective-permute-start.36) | collective-permute-done | bytes 196640 | tf_op jit(solution)/shard_map/ppermute | solution.py:146
  137.2 5.3 %collective-permute-done.37.c = f32[384,128]{1,0:T(8,128)S(1)} collective-permute-done((f32[384,128]{1,0:T(8,128)S(1)}, f32[384,128]{1,0:T(8,128)S(1)}, u32[]{:S(2)}, u32[]{:S(2)}) %collective-permute-start.37) | collective-permute-done | bytes 196640 | tf_op jit(solution)/shard_map/ppermute | solution.py:146
  142.5 0.9 shard_map.50
  (66 shorter events, 6.7 us)
Async XLA Ops:
  0.0 11.3 %copy-start = (f32[768,800]{0,1:T(8,128)S(1)}, f32[768,800]{0,1:T(8,128)}, u32[]{:S(2)}) copy-start(f32[768,800]{0,1:T(8,128)} %param.3) | copy-start | bytes 7372804
  4.9 13.1 %collective-permute-start = (f32[400,128]{1,0:T(8,128)}, f32[400,128]{1,0:T(8,128)S(1)}, u32[]{:S(2)}, u32[]{:S(2)}) collective-permute-start(f32[400,128]{1,0:T(8,128)} %get-tuple-element.146), channel_id=1, source_target_pairs={{0,2},{1,3},{2,0},{3,1},{4,6},{5,7},{6,4},{7,5},{8,10},{9,11},{10,... | collective-permute-start | bytes 614408 | tf_op jit(solution)/shard_map/ppermute | solution.py:146
  8.6 11.6 %collective-permute-start.1 = (f32[400,128]{1,0:T(8,128)}, f32[400,128]{1,0:T(8,128)S(1)}, u32[]{:S(2)}, u32[]{:S(2)}) collective-permute-start(f32[400,128]{1,0:T(8,128)} %get-tuple-element.147), channel_id=1, source_target_pairs={{0,1},{1,2},{2,3},{3,0},{4,5},{5,6},{6,7},{7,4},{8,9},{9,10},{10,1... | collective-permute-start | bytes 614408 | tf_op jit(solution)/shard_map/ppermute | solution.py:146
  9.0 11.2 %collective-permute-start.2 = (f32[400,128]{1,0:T(8,128)}, f32[400,128]{1,0:T(8,128)S(1)}, u32[]{:S(2)}, u32[]{:S(2)}) collective-permute-start(f32[400,128]{1,0:T(8,128)} %get-tuple-element.148), channel_id=1, source_target_pairs={{0,3},{1,0},{2,1},{3,2},{4,7},{5,4},{6,5},{7,6},{8,11},{9,8},{10,9... | collective-permute-start | bytes 614408 | tf_op jit(solution)/shard_map/ppermute | solution.py:146
  11.3 1.7 %copy-start.1 = (f32[2,384,768]{2,1,0:T(8,128)S(1)}, f32[2,384,768]{2,1,0:T(8,128)}, u32[]{:S(2)}) copy-start(f32[2,384,768]{2,1,0:T(8,128)} %refs_1_) | copy-start | bytes 7077892
  13.0 7.2 %copy-start.2 = (f32[400,128]{1,0:T(8,128)S(1)}, f32[400,128]{1,0:T(8,128)}, u32[]{:S(2)}) copy-start(f32[400,128]{1,0:T(8,128)} %get-tuple-element.153.a) | copy-start | bytes 614404
  17.4 11.6 %collective-permute-start.11 = (f32[400,128]{1,0:T(8,128)S(1)}, f32[400,128]{1,0:T(8,128)S(1)}, u32[]{:S(2)}, u32[]{:S(2)}) collective-permute-start(f32[400,128]{1,0:T(8,128)S(1)} %get-tuple-element.170), channel_id=1, source_target_pairs={{0,2},{1,3},{2,0},{3,1},{4,6},{5,7},{6,4},{7,5},{8,10},{9,11},{10,... | collective-permute-start | bytes 614408 | tf_op jit(solution)/shard_map/ppermute | solution.py:146
  17.5 12.5 %collective-permute-start.12 = (f32[400,128]{1,0:T(8,128)S(1)}, f32[400,128]{1,0:T(8,128)S(1)}, u32[]{:S(2)}, u32[]{:S(2)}) collective-permute-start(f32[400,128]{1,0:T(8,128)S(1)} %get-tuple-element.171), channel_id=1, source_target_pairs={{0,1},{1,2},{2,3},{3,0},{4,5},{5,6},{6,7},{7,4},{8,9},{9,10},{10,1... | collective-permute-start | bytes 614408 | tf_op jit(solution)/shard_map/ppermute | solution.py:146
  18.0 13.6 %collective-permute-start.13 = (f32[400,128]{1,0:T(8,128)S(1)}, f32[400,128]{1,0:T(8,128)S(1)}, u32[]{:S(2)}, u32[]{:S(2)}) collective-permute-start(f32[400,128]{1,0:T(8,128)S(1)} %get-tuple-element.172), channel_id=1, source_target_pairs={{0,3},{1,0},{2,1},{3,2},{4,7},{5,4},{6,5},{7,6},{8,11},{9,8},{10,9... | collective-permute-start | bytes 614408 | tf_op jit(solution)/shard_map/ppermute | solution.py:146
  20.3 18.2 %collective-permute-start.3 = (f32[400,128]{1,0:T(8,128)S(1)}, f32[400,128]{1,0:T(8,128)S(1)}, u32[]{:S(2)}, u32[]{:S(2)}) collective-permute-start(f32[400,128]{1,0:T(8,128)S(1)} %shard_map.30.one_ref), channel_id=1, source_target_pairs={{0,4},{4,0},{1,5},{5,1},{2,6},{6,2},{3,7},{7,3},{8,12},{12,8},{9,1... | collective-permute-start | bytes 614408 | tf_op jit(solution)/shard_map/ppermute | solution.py:141
  27.3 15.9 %collective-permute-start.7 = (f32[400,128]{1,0:T(8,128)S(1)}, f32[400,128]{1,0:T(8,128)S(1)}, u32[]{:S(2)}, u32[]{:S(2)}) collective-permute-start(f32[400,128]{1,0:T(8,128)S(1)} %get-tuple-element.163), channel_id=1, source_target_pairs={{0,2},{1,3},{2,0},{3,1},{4,6},{5,7},{6,4},{7,5},{8,10},{9,11},{10,... | collective-permute-start | bytes 614408 | tf_op jit(solution)/shard_map/ppermute | solution.py:146
  29.0 14.2 %collective-permute-start.8 = (f32[400,128]{1,0:T(8,128)S(1)}, f32[400,128]{1,0:T(8,128)S(1)}, u32[]{:S(2)}, u32[]{:S(2)}) collective-permute-start(f32[400,128]{1,0:T(8,128)S(1)} %get-tuple-element.164), channel_id=1, source_target_pairs={{0,1},{1,2},{2,3},{3,0},{4,5},{5,6},{6,7},{7,4},{8,9},{9,10},{10,1... | collective-permute-start | bytes 614408 | tf_op jit(solution)/shard_map/ppermute | solution.py:146
  29.9 13.2 %collective-permute-start.9 = (f32[400,128]{1,0:T(8,128)S(1)}, f32[400,128]{1,0:T(8,128)S(1)}, u32[]{:S(2)}, u32[]{:S(2)}) collective-permute-start(f32[400,128]{1,0:T(8,128)S(1)} %get-tuple-element.165), channel_id=1, source_target_pairs={{0,3},{1,0},{2,1},{3,2},{4,7},{5,4},{6,5},{7,6},{8,11},{9,8},{10,9... | collective-permute-start | bytes 614408 | tf_op jit(solution)/shard_map/ppermute | solution.py:146
  31.7 14.1 %collective-permute-start.14 = (f32[400,128]{1,0:T(8,128)S(1)}, f32[400,128]{1,0:T(8,128)S(1)}, u32[]{:S(2)}, u32[]{:S(2)}) collective-permute-start(f32[400,128]{1,0:T(8,128)S(1)} %shard_map.33.one_ref), channel_id=1, source_target_pairs={{0,4},{4,0},{1,5},{5,1},{2,6},{6,2},{3,7},{7,3},{8,12},{12,8},{9,1... | collective-permute-start | bytes 614408 | tf_op jit(solution)/shard_map/ppermute | solution.py:141
  39.2 9.3 %all-to-all-start = ((f32[4,104,128]{2,1,0:T(8,128)}), f32[4,104,128]{2,1,0:T(8,128)S(1)}, u32[]{:S(2)}, u32[]{:S(2)}) async-start(f32[4,104,128]{2,1,0:T(8,128)} %shard_map.31), calls=%async_computation | async-start | bytes 425984 | tf_op jit(solution)/shard_map/all_to_all | solution.py:225
  43.2 11.9 %collective-permute-start.10 = (f32[400,128]{1,0:T(8,128)S(1)}, f32[400,128]{1,0:T(8,128)S(1)}, u32[]{:S(2)}, u32[]{:S(2)}) collective-permute-start(f32[400,128]{1,0:T(8,128)S(1)} %shard_map.32.one_ref), channel_id=1, source_target_pairs={{0,4},{4,0},{1,5},{5,1},{2,6},{6,2},{3,7},{7,3},{8,12},{12,8},{9,1... | collective-permute-start | bytes 614408 | tf_op jit(solution)/shard_map/ppermute | solution.py:141
  48.4 8.9 %all-to-all-start.1 = ((f32[4,104,128]{2,1,0:T(8,128)}), f32[4,104,128]{2,1,0:T(8,128)S(1)}, u32[]{:S(2)}, u32[]{:S(2)}) async-start(f32[4,104,128]{2,1,0:T(8,128)} %shard_map.34), calls=%async_computation.1 | async-start | bytes 425984 | tf_op jit(solution)/shard_map/all_to_all | solution.py:225
  51.8 14.0 %collective-permute-start.6 = (f32[4,104,128]{2,1,0:T(8,128)S(1)}, f32[4,104,128]{2,1,0:T(8,128)S(1)}, u32[]{:S(2)}, u32[]{:S(2)}) collective-permute-start(f32[4,104,128]{2,1,0:T(8,128)S(1)} %all-to-all-done.a), channel_id=1, source_target_pairs={{0,3},{1,0},{2,1},{3,2},{4,7},{5,4},{6,5},{7,6},{8,11},{9,8},{10,9... | collective-permute-start | bytes 638984 | tf_op jit(solution)/shard_map/ppermute | solution.py:146
  52.3 13.7 %collective-permute-start.5 = (f32[4,104,128]{2,1,0:T(8,128)S(1)}, f32[4,104,128]{2,1,0:T(8,128)S(1)}, u32[]{:S(2)}, u32[]{:S(2)}) collective-permute-start(f32[4,104,128]{2,1,0:T(8,128)S(1)} %all-to-all-done.a), channel_id=1, source_target_pairs={{0,2},{1,3},{2,0},{3,1},{4,6},{5,7},{6,4},{7,5},{8,10},{9,11},{10,... | collective-permute-start | bytes 638984 | tf_op jit(solution)/shard_map/ppermute | solution.py:146
  55.1 13.3 %collective-permute-start.4 = (f32[4,104,128]{2,1,0:T(8,128)S(1)}, f32[4,104,128]{2,1,0:T(8,128)S(1)}, u32[]{:S(2)}, u32[]{:S(2)}) collective-permute-start(f32[4,104,128]{2,1,0:T(8,128)S(1)} %all-to-all-done.a), channel_id=1, source_target_pairs={{0,1},{1,2},{2,3},{3,0},{4,5},{5,6},{6,7},{7,4},{8,9},{9,10},{10,1... | collective-permute-start | bytes 638984 | tf_op jit(solution)/shard_map/ppermute | solution.py:146
  57.3 8.6 %all-to-all-start.2 = ((f32[4,104,128]{2,1,0:T(8,128)}), f32[4,104,128]{2,1,0:T(8,128)S(1)}, u32[]{:S(2)}, u32[]{:S(2)}) async-start(f32[4,104,128]{2,1,0:T(8,128)} %shard_map.35), calls=%async_computation.2 | async-start | bytes 425984 | tf_op jit(solution)/shard_map/all_to_all | solution.py:225
  60.9 10.5 %collective-permute-start.17 = (f32[4,104,128]{2,1,0:T(8,128)S(1)}, f32[4,104,128]{2,1,0:T(8,128)S(1)}, u32[]{:S(2)}, u32[]{:S(2)}) collective-permute-start(f32[4,104,128]{2,1,0:T(8,128)S(1)} %all-to-all-done.1.a), channel_id=1, source_target_pairs={{0,3},{1,0},{2,1},{3,2},{4,7},{5,4},{6,5},{7,6},{8,11},{9,8},{10,9... | collective-permute-start | bytes 638984 | tf_op jit(solution)/shard_map/ppermute | solution.py:146
  62.7 9.0 %collective-permute-start.16 = (f32[4,104,128]{2,1,0:T(8,128)S(1)}, f32[4,104,128]{2,1,0:T(8,128)S(1)}, u32[]{:S(2)}, u32[]{:S(2)}) collective-permute-start(f32[4,104,128]{2,1,0:T(8,128)S(1)} %all-to-all-done.1.a), channel_id=1, source_target_pairs={{0,2},{1,3},{2,0},{3,1},{4,6},{5,7},{6,4},{7,5},{8,10},{9,11},{10,... | collective-permute-start | bytes 638984 | tf_op jit(solution)/shard_map/ppermute | solution.py:146
  65.8 6.0 %collective-permute-start.15 = (f32[4,104,128]{2,1,0:T(8,128)S(1)}, f32[4,104,128]{2,1,0:T(8,128)S(1)}, u32[]{:S(2)}, u32[]{:S(2)}) collective-permute-start(f32[4,104,128]{2,1,0:T(8,128)S(1)} %all-to-all-done.1.a), channel_id=1, source_target_pairs={{0,1},{1,2},{2,3},{3,0},{4,5},{5,6},{6,7},{7,4},{8,9},{9,10},{10,1... | collective-permute-start | bytes 638984 | tf_op jit(solution)/shard_map/ppermute | solution.py:146
  66.0 12.4 %collective-permute-start.20 = (f32[4,104,128]{2,1,0:T(8,128)S(1)}, f32[4,104,128]{2,1,0:T(8,128)S(1)}, u32[]{:S(2)}, u32[]{:S(2)}) collective-permute-start(f32[4,104,128]{2,1,0:T(8,128)S(1)} %all-to-all-done.2.a), channel_id=1, source_target_pairs={{0,3},{1,0},{2,1},{3,2},{4,7},{5,4},{6,5},{7,6},{8,11},{9,8},{10,9... | collective-permute-start | bytes 638984 | tf_op jit(solution)/shard_map/ppermute | solution.py:146
  68.5 9.9 %collective-permute-start.19 = (f32[4,104,128]{2,1,0:T(8,128)S(1)}, f32[4,104,128]{2,1,0:T(8,128)S(1)}, u32[]{:S(2)}, u32[]{:S(2)}) collective-permute-start(f32[4,104,128]{2,1,0:T(8,128)S(1)} %all-to-all-done.2.a), channel_id=1, source_target_pairs={{0,2},{1,3},{2,0},{3,1},{4,6},{5,7},{6,4},{7,5},{8,10},{9,11},{10,... | collective-permute-start | bytes 638984 | tf_op jit(solution)/shard_map/ppermute | solution.py:146
  71.4 10.3 %collective-permute-start.18 = (f32[4,104,128]{2,1,0:T(8,128)S(1)}, f32[4,104,128]{2,1,0:T(8,128)S(1)}, u32[]{:S(2)}, u32[]{:S(2)}) collective-permute-start(f32[4,104,128]{2,1,0:T(8,128)S(1)} %all-to-all-done.2.a), channel_id=1, source_target_pairs={{0,1},{1,2},{2,3},{3,0},{4,5},{5,6},{6,7},{7,4},{8,9},{9,10},{10,1... | collective-permute-start | bytes 638984 | tf_op jit(solution)/shard_map/ppermute | solution.py:146
  71.8 5.9 %collective-permute-start.21 = (f32[416,128]{1,0:T(8,128)S(1)}, f32[416,128]{1,0:T(8,128)S(1)}, u32[]{:S(2)}, u32[]{:S(2)}) collective-permute-start(f32[416,128]{1,0:T(8,128)S(1)} %get-tuple-element.199.mine), channel_id=1, source_target_pairs={{0,24},{16,9},{25,1},{9,16},{2,26},{18,11},{27,3},{11,18},{4,28},{... | collective-permute-start | bytes 638984 | tf_op jit(solution)/shard_map/ppermute | solution.py:155
  75.3 6.8 %collective-permute-start.23 = (f32[416,128]{1,0:T(8,128)S(1)}, f32[416,128]{1,0:T(8,128)S(1)}, u32[]{:S(2)}, u32[]{:S(2)}) collective-permute-start(f32[416,128]{1,0:T(8,128)S(1)} %get-tuple-element.211.mine), channel_id=1, source_target_pairs={{0,24},{16,9},{25,1},{9,16},{2,26},{18,11},{27,3},{11,18},{4,28},{... | collective-permute-start | bytes 638984 | tf_op jit(solution)/shard_map/ppermute | solution.py:155
  78.2 9.7 %collective-permute-start.22 = (f32[416,128]{1,0:T(8,128)S(1)}, f32[416,128]{1,0:T(8,128)S(1)}, u32[]{:S(2)}, u32[]{:S(2)}) collective-permute-start(f32[416,128]{1,0:T(8,128)S(1)} %shard_map.38.refs_6_), channel_id=1, source_target_pairs={{0,8},{8,0},{16,24},{24,16},{1,9},{9,1},{17,25},{25,17},{2,10},{10... | collective-permute-start | bytes 638984 | tf_op jit(solution)/shard_map/ppermute | solution.py:237
  82.7 23.1 %collective-permute-start.26 = (f32[416,128]{1,0:T(8,128)S(1)}, f32[416,128]{1,0:T(8,128)S(1)}, u32[]{:S(2)}, u32[]{:S(2)}) collective-permute-start(f32[416,128]{1,0:T(8,128)S(1)} %shard_map.40.refs_6_), channel_id=1, source_target_pairs={{0,8},{8,0},{16,24},{24,16},{1,9},{9,1},{17,25},{25,17},{2,10},{10... | collective-permute-start | bytes 638984 | tf_op jit(solution)/shard_map/ppermute | solution.py:237
  84.9 23.0 %collective-permute-start.25 = (f32[416,128]{1,0:T(8,128)S(1)}, f32[416,128]{1,0:T(8,128)S(1)}, u32[]{:S(2)}, u32[]{:S(2)}) collective-permute-start(f32[416,128]{1,0:T(8,128)S(1)} %get-tuple-element.236.mine), channel_id=1, source_target_pairs={{0,24},{16,9},{25,1},{9,16},{2,26},{18,11},{27,3},{11,18},{4,28},{... | collective-permute-start | bytes 638984 | tf_op jit(solution)/shard_map/ppermute | solution.py:155
  89.9 18.7 %collective-permute-start.24 = (f32[4,384,128]{2,1,0:T(8,128)S(1)}, f32[4,384,128]{2,1,0:T(8,128)S(1)}, u32[]{:S(2)}, u32[]{:S(2)}) collective-permute-start(f32[4,384,128]{2,1,0:T(8,128)S(1)} %get-tuple-element.223), channel_id=1, source_target_pairs={{0,128},{128,0},{1,129},{129,1},{2,130},{130,2},{3,131},{131,3},{4... | collective-permute-start | bytes 2359304 | tf_op jit(solution)/shard_map/ppermute | solution.py:141
  107.8 6.9 %collective-permute-start.31 = (f32[4,384,128]{2,1,0:T(8,128)S(1)}, f32[4,384,128]{2,1,0:T(8,128)S(1)}, u32[]{:S(2)}, u32[]{:S(2)}) collective-permute-start(f32[4,384,128]{2,1,0:T(8,128)S(1)} %get-tuple-element.234), channel_id=1, source_target_pairs={{0,128},{128,0},{1,129},{129,1},{2,130},{130,2},{3,131},{131,3},{4... | collective-permute-start | bytes 2359304 | tf_op jit(solution)/shard_map/ppermute | solution.py:141
  108.5 6.4 %collective-permute-start.30 = (f32[416,128]{1,0:T(8,128)S(1)}, f32[416,128]{1,0:T(8,128)S(1)}, u32[]{:S(2)}, u32[]{:S(2)}) collective-permute-start(f32[416,128]{1,0:T(8,128)S(1)} %shard_map.43.refs_6_), channel_id=1, source_target_pairs={{0,8},{8,0},{16,24},{24,16},{1,9},{9,1},{17,25},{25,17},{2,10},{10... | collective-permute-start | bytes 638984 | tf_op jit(solution)/shard_map/ppermute | solution.py:237
  108.7 11.7 %collective-permute-start.27 = (f32[384,128]{1,0:T(8,128)S(1)}, f32[384,128]{1,0:T(8,128)S(1)}, u32[]{:S(2)}, u32[]{:S(2)}) collective-permute-start(f32[384,128]{1,0:T(8,128)S(1)} %get-tuple-element.242), channel_id=1, source_target_pairs={{0,64},{32,96},{64,0},{96,32},{1,65},{33,97},{65,1},{97,33},{2,66}... | collective-permute-start | bytes 589832 | tf_op jit(solution)/shard_map/ppermute | solution.py:146
  112.0 10.9 %collective-permute-start.28 = (f32[384,128]{1,0:T(8,128)S(1)}, f32[384,128]{1,0:T(8,128)S(1)}, u32[]{:S(2)}, u32[]{:S(2)}) collective-permute-start(f32[384,128]{1,0:T(8,128)S(1)} %get-tuple-element.243), channel_id=1, source_target_pairs={{0,32},{32,64},{64,96},{96,0},{1,33},{33,65},{65,97},{97,1},{2,34}... | collective-permute-start | bytes 589832 | tf_op jit(solution)/shard_map/ppermute | solution.py:146
  112.3 12.7 %collective-permute-start.29 = (f32[384,128]{1,0:T(8,128)S(1)}, f32[384,128]{1,0:T(8,128)S(1)}, u32[]{:S(2)}, u32[]{:S(2)}) collective-permute-start(f32[384,128]{1,0:T(8,128)S(1)} %get-tuple-element.244), channel_id=1, source_target_pairs={{0,96},{32,0},{64,32},{96,64},{1,97},{33,1},{65,33},{97,65},{2,98}... | collective-permute-start | bytes 589832 | tf_op jit(solution)/shard_map/ppermute | solution.py:146
  114.9 12.1 %collective-permute-start.32 = (f32[384,128]{1,0:T(8,128)S(1)}, f32[384,128]{1,0:T(8,128)S(1)}, u32[]{:S(2)}, u32[]{:S(2)}) collective-permute-start(f32[384,128]{1,0:T(8,128)S(1)} %get-tuple-element.264), channel_id=1, source_target_pairs={{0,64},{32,96},{64,0},{96,32},{1,65},{33,97},{65,1},{97,33},{2,66}... | collective-permute-start | bytes 589832 | tf_op jit(solution)/shard_map/ppermute | solution.py:146
  118.1 11.9 %collective-permute-start.33 = (f32[384,128]{1,0:T(8,128)S(1)}, f32[384,128]{1,0:T(8,128)S(1)}, u32[]{:S(2)}, u32[]{:S(2)}) collective-permute-start(f32[384,128]{1,0:T(8,128)S(1)} %get-tuple-element.265), channel_id=1, source_target_pairs={{0,32},{32,64},{64,96},{96,0},{1,33},{33,65},{65,97},{97,1},{2,34}... | collective-permute-start | bytes 589832 | tf_op jit(solution)/shard_map/ppermute | solution.py:146
  120.4 9.6 %collective-permute-start.34 = (f32[384,128]{1,0:T(8,128)S(1)}, f32[384,128]{1,0:T(8,128)S(1)}, u32[]{:S(2)}, u32[]{:S(2)}) collective-permute-start(f32[384,128]{1,0:T(8,128)S(1)} %get-tuple-element.266), channel_id=1, source_target_pairs={{0,96},{32,0},{64,32},{96,64},{1,97},{33,1},{65,33},{97,65},{2,98}... | collective-permute-start | bytes 589832 | tf_op jit(solution)/shard_map/ppermute | solution.py:146
  122.9 4.1 %collective-permute-start.35 = (f32[4,384,128]{2,1,0:T(8,128)S(1)}, f32[4,384,128]{2,1,0:T(8,128)S(1)}, u32[]{:S(2)}, u32[]{:S(2)}) collective-permute-start(f32[4,384,128]{2,1,0:T(8,128)S(1)} %get-tuple-element.259), channel_id=1, source_target_pairs={{0,128},{128,0},{1,129},{129,1},{2,130},{130,2},{3,131},{131,3},{4... | collective-permute-start | bytes 2359304 | tf_op jit(solution)/shard_map/ppermute | solution.py:141
  130.0 7.2 %collective-permute-start.36 = (f32[384,128]{1,0:T(8,128)S(1)}, f32[384,128]{1,0:T(8,128)S(1)}, u32[]{:S(2)}, u32[]{:S(2)}) collective-permute-start(f32[384,128]{1,0:T(8,128)S(1)} %get-tuple-element.276), channel_id=1, source_target_pairs={{0,64},{32,96},{64,0},{96,32},{1,65},{33,97},{65,1},{97,33},{2,66}... | collective-permute-start | bytes 589832 | tf_op jit(solution)/shard_map/ppermute | solution.py:146
  131.3 11.2 %collective-permute-start.37 = (f32[384,128]{1,0:T(8,128)S(1)}, f32[384,128]{1,0:T(8,128)S(1)}, u32[]{:S(2)}, u32[]{:S(2)}) collective-permute-start(f32[384,128]{1,0:T(8,128)S(1)} %get-tuple-element.277), channel_id=1, source_target_pairs={{0,32},{32,64},{64,96},{96,0},{1,33},{33,65},{65,97},{97,1},{2,34}... | collective-permute-start | bytes 589832 | tf_op jit(solution)/shard_map/ppermute | solution.py:146
  132.5 10.0 %collective-permute-start.38 = (f32[384,128]{1,0:T(8,128)S(1)}, f32[384,128]{1,0:T(8,128)S(1)}, u32[]{:S(2)}, u32[]{:S(2)}) collective-permute-start(f32[384,128]{1,0:T(8,128)S(1)} %get-tuple-element.278), channel_id=1, source_target_pairs={{0,96},{32,0},{64,32},{96,64},{1,97},{33,1},{65,33},{97,65},{2,98}... | collective-permute-start | bytes 589832 | tf_op jit(solution)/shard_map/ppermute | solution.py:146

commit v6 on v5

--- a/solution.py
+++ b/solution.py
@@ -262,8 +262,8 @@
     pair1 = pair_of(*half1)
     tile0 = tile_of(pair0)
     tile1 = tile_of(pair1)
+    out0 = over_x_sum(*tile0)
     pair2 = pair_of(*half2)
-    out0 = over_x_sum(*tile0)
     out1 = over_x_sum(*tile1)
     tile2 = tile_of(pair2)
     out0 = order(out_call, *out0)

time: 145 us -> 142 us (0.979); the launches traced: 143 us -> 142 us
  starting transfers between devices: 97.3 us -> 95.1 us
    ppermute x3, waiting for transfers between devices: 0.14 us -> 4.94 us  [pair_of(): return (have, lax.ppermute(have, 'zl', [(0, 1), (1, 0), (2, 3), (3, 2)]))]
    ppermute x27, waiting for transfers between devices: 15.9 us -> 12.6 us  [shifted(): lax.ppermute(value, axis, [(i, (i + distance) % size) for i in range(size)])]
    ppermute x27, starting transfers between devices: 42.2 us -> 39.3 us  [shifted(): lax.ppermute(value, axis, [(i, (i + distance) % size) for i in range(size)])]
    ppermute x3, starting transfers between devices: 7.4 us -> 10.2 us  [along(): return lax.ppermute(value, ('zl', 'y'), pairs)]
where the time goes in v6:
time: 142 us
  starting transfers between devices  95.1 us (67%)
  waiting for transfers between devices  23.2 us (16%)
  Pallas kernels  21.6 us (15%)
  local copies, waits for them, and re-layouts  1.67 us (1%)
    ppermute x27, starting transfers between devices, shifted(): lax.ppermute(value, axis, [(i, (i + distance) % size) for i in range(size)])  39.3 us
    ppermute x6, starting transfers between devices, swapped(): return lax.ppermute(value, axis, [(0, 1), (1, 0)])  33.2 us
    ppermute x27, waiting for transfers between devices, shifted(): lax.ppermute(value, axis, [(i, (i + distance) % size) for i in range(size)])  12.6 us
    pallas_call x21, Pallas kernels, __call__(): result = kernel(*operands)  12.4 us
    all_to_all x3, starting transfers between devices, over_x(): lax.all_to_all(order(piece_call, total, other), 'x', 0, 0, tiled=True)  10.8 us
    ppermute x3, starting transfers between devices, along(): return lax.ppermute(value, ('zl', 'y'), pairs)  10.2 us
    pallas_call x2, Pallas kernels, half_call(): pl.pallas_call(functools.partial(half_kernel, count), out_shape=[f32(size...  9.26 us
    ppermute x3, waiting for transfers between devices, pair_of(): return (have, lax.ppermute(have, 'zl', [(0, 1), (1, 0), (2, 3), (3, 2)]))  4.94 us
  transfers between devices with their start and end apart: 42, of which 11 were waited for; matrix products, arithmetic and copies ran while one was open for 0% of the time, Pallas kernels for 11%

profile of v6, /device:TPU:1, one launch (start us, length us, event | category | flops | bytes accessed | tf_op | source)
XLA Modules:
  0.0 142.0 jit_solution(15324747810825345384)
XLA Ops:
  0.0 4.9 %shard_map.28 = (f32[400,128]{1,0:T(8,128)}, f32[400,128]{1,0:T(8,128)}, f32[400,128]{1,0:T(8,128)}, f32[400,128]{1,0:T(8,128)}) custom-call(s32[1]{0:T(128)} %bitcast.3.here_ref, f32[800,768]{1,0:T(8,128)} %bitcast.6, f32[2,384,768]{2,1,0:T(8,128)} %refs_1_), custom_call_target="tpu_custom_call" | custom-call | flops 12000000000 | bytes 44000000 | tf_op jit(solution)/shard_map/pallas_call | solution.py:72
  4.9 3.7 %collective-permute-start = (f32[400,128]{1,0:T(8,128)}, f32[400,128]{1,0:T(8,128)S(1)}, u32[]{:S(2)}, u32[]{:S(2)}) collective-permute-start(f32[400,128]{1,0:T(8,128)} %get-tuple-element.146), channel_id=1, source_target_pairs={{0,2},{1,3},{2,0},{3,1},{4,6},{5,7},{6,4},{7,5},{8,10},{9,11},{10,... | collective-permute-start | bytes 614408 | tf_op jit(solution)/shard_map/ppermute | solution.py:146
  9.0 2.3 %collective-permute-start.2 = (f32[400,128]{1,0:T(8,128)}, f32[400,128]{1,0:T(8,128)S(1)}, u32[]{:S(2)}, u32[]{:S(2)}) collective-permute-start(f32[400,128]{1,0:T(8,128)} %get-tuple-element.148), channel_id=1, source_target_pairs={{0,3},{1,0},{2,1},{3,2},{4,7},{5,4},{6,5},{7,6},{8,11},{9,8},{10,9... | collective-permute-start | bytes 614408 | tf_op jit(solution)/shard_map/ppermute | solution.py:146
  11.3 1.7 %copy-done.1 = f32[2,384,768]{2,1,0:T(8,128)S(1)} copy-done((f32[2,384,768]{2,1,0:T(8,128)S(1)}, f32[2,384,768]{2,1,0:T(8,128)}, u32[]{:S(2)}) %copy-start.1) | copy-done | bytes 2359320
  13.0 4.4 %shard_map.29 = (f32[400,128]{1,0:T(8,128)S(1)}, f32[400,128]{1,0:T(8,128)S(1)}, f32[400,128]{1,0:T(8,128)S(1)}, f32[400,128]{1,0:T(8,128)S(1)}, f32[400,128]{1,...) custom-call(s32[1]{0:T(128)} %bitcast.3.here_ref, f32[800,768]{1,0:T(8,128)S(1)} %bitcast.7, ...), custom_call_target="tpu_custom_call" | custom-call | flops 12000000000 | bytes 44000000 | tf_op jit(solution)/shard_map/pallas_call | solution.py:72
  18.0 2.2 %collective-permute-start.13 = (f32[400,128]{1,0:T(8,128)S(1)}, f32[400,128]{1,0:T(8,128)S(1)}, u32[]{:S(2)}, u32[]{:S(2)}) collective-permute-start(f32[400,128]{1,0:T(8,128)S(1)} %get-tuple-element.172), channel_id=1, source_target_pairs={{0,3},{1,0},{2,1},{3,2},{4,7},{5,4},{6,5},{7,6},{8,11},{9,8},{10,9... | collective-permute-start | bytes 614408 | tf_op jit(solution)/shard_map/ppermute | solution.py:146
  20.3 7.0 %collective-permute-start.3 = (f32[400,128]{1,0:T(8,128)S(1)}, f32[400,128]{1,0:T(8,128)S(1)}, u32[]{:S(2)}, u32[]{:S(2)}) collective-permute-start(f32[400,128]{1,0:T(8,128)S(1)} %shard_map.30.one_ref), channel_id=1, source_target_pairs={{0,4},{4,0},{1,5},{5,1},{2,6},{6,2},{3,7},{7,3},{8,12},{12,8},{9,1... | collective-permute-start | bytes 614408 | tf_op jit(solution)/shard_map/ppermute | solution.py:141
  27.3 1.7 %collective-permute-start.7 = (f32[400,128]{1,0:T(8,128)S(1)}, f32[400,128]{1,0:T(8,128)S(1)}, u32[]{:S(2)}, u32[]{:S(2)}) collective-permute-start(f32[400,128]{1,0:T(8,128)S(1)} %get-tuple-element.163), channel_id=1, source_target_pairs={{0,2},{1,3},{2,0},{3,1},{4,6},{5,7},{6,4},{7,5},{8,10},{9,11},{10,... | collective-permute-start | bytes 614408 | tf_op jit(solution)/shard_map/ppermute | solution.py:146
  29.0 1.0 collective-permute-done.12.c
  29.9 1.7 %collective-permute-start.9 = (f32[400,128]{1,0:T(8,128)S(1)}, f32[400,128]{1,0:T(8,128)S(1)}, u32[]{:S(2)}, u32[]{:S(2)}) collective-permute-start(f32[400,128]{1,0:T(8,128)S(1)} %get-tuple-element.165), channel_id=1, source_target_pairs={{0,3},{1,0},{2,1},{3,2},{4,7},{5,4},{6,5},{7,6},{8,11},{9,8},{10,9... | collective-permute-start | bytes 614408 | tf_op jit(solution)/shard_map/ppermute | solution.py:146
  31.7 6.7 %collective-permute-start.14 = (f32[400,128]{1,0:T(8,128)S(1)}, f32[400,128]{1,0:T(8,128)S(1)}, u32[]{:S(2)}, u32[]{:S(2)}) collective-permute-start(f32[400,128]{1,0:T(8,128)S(1)} %shard_map.33.one_ref), channel_id=1, source_target_pairs={{0,4},{4,0},{1,5},{5,1},{2,6},{6,2},{3,7},{7,3},{8,12},{12,8},{9,1... | collective-permute-start | bytes 614408 | tf_op jit(solution)/shard_map/ppermute | solution.py:141
  38.4 0.7 shard_map.31
  39.2 4.0 %all-to-all-start = ((f32[4,104,128]{2,1,0:T(8,128)}), f32[4,104,128]{2,1,0:T(8,128)S(1)}, u32[]{:S(2)}, u32[]{:S(2)}) async-start(f32[4,104,128]{2,1,0:T(8,128)} %shard_map.31), calls=%async_computation | async-start | bytes 425984 | tf_op jit(solution)/shard_map/all_to_all | solution.py:225
  43.2 2.5 %collective-permute-start.10 = (f32[400,128]{1,0:T(8,128)S(1)}, f32[400,128]{1,0:T(8,128)S(1)}, u32[]{:S(2)}, u32[]{:S(2)}) collective-permute-start(f32[400,128]{1,0:T(8,128)S(1)} %shard_map.32.one_ref), channel_id=1, source_target_pairs={{0,4},{4,0},{1,5},{5,1},{2,6},{6,2},{3,7},{7,3},{8,12},{12,8},{9,1... | collective-permute-start | bytes 614408 | tf_op jit(solution)/shard_map/ppermute | solution.py:141
  45.8 0.7 shard_map.34
  46.5 2.0 %all-to-all-done.a = f32[4,104,128]{2,1,0:T(8,128)S(1)} async-done(((f32[4,104,128]{2,1,0:T(8,128)}), f32[4,104,128]{2,1,0:T(8,128)S(1)}, u32[]{:S(2)}, u32[]{:S(2)}) %all-to-all-start) | async-done | bytes 213024 | tf_op jit(solution)/shard_map/all_to_all | solution.py:225
  48.4 3.4 %all-to-all-start.1 = ((f32[4,104,128]{2,1,0:T(8,128)}), f32[4,104,128]{2,1,0:T(8,128)S(1)}, u32[]{:S(2)}, u32[]{:S(2)}) async-start(f32[4,104,128]{2,1,0:T(8,128)} %shard_map.34), calls=%async_computation.1 | async-start | bytes 425984 | tf_op jit(solution)/shard_map/all_to_all | solution.py:225
  51.8 1.5 %collective-permute-start.4 = (f32[4,104,128]{2,1,0:T(8,128)S(1)}, f32[4,104,128]{2,1,0:T(8,128)S(1)}, u32[]{:S(2)}, u32[]{:S(2)}) collective-permute-start(f32[4,104,128]{2,1,0:T(8,128)S(1)} %all-to-all-done.a), channel_id=1, source_target_pairs={{0,1},{1,2},{2,3},{3,0},{4,5},{5,6},{6,7},{7,4},{8,9},{9,10},{10,1... | collective-permute-start | bytes 638984 | tf_op jit(solution)/shard_map/ppermute | solution.py:146
  53.5 2.4 %collective-permute-start.6 = (f32[4,104,128]{2,1,0:T(8,128)S(1)}, f32[4,104,128]{2,1,0:T(8,128)S(1)}, u32[]{:S(2)}, u32[]{:S(2)}) collective-permute-start(f32[4,104,128]{2,1,0:T(8,128)S(1)} %all-to-all-done.a), channel_id=1, source_target_pairs={{0,3},{1,0},{2,1},{3,2},{4,7},{5,4},{6,5},{7,6},{8,11},{9,8},{10,9... | collective-permute-start | bytes 638984 | tf_op jit(solution)/shard_map/ppermute | solution.py:146
  55.9 0.7 shard_map.35
  56.6 0.8 all-to-all-done.1.a
  57.3 3.4 %all-to-all-start.2 = ((f32[4,104,128]{2,1,0:T(8,128)}), f32[4,104,128]{2,1,0:T(8,128)S(1)}, u32[]{:S(2)}, u32[]{:S(2)}) async-start(f32[4,104,128]{2,1,0:T(8,128)} %shard_map.35), calls=%async_computation.2 | async-start | bytes 425984 | tf_op jit(solution)/shard_map/all_to_all | solution.py:225
  60.9 3.1 %collective-permute-start.15 = (f32[4,104,128]{2,1,0:T(8,128)S(1)}, f32[4,104,128]{2,1,0:T(8,128)S(1)}, u32[]{:S(2)}, u32[]{:S(2)}) collective-permute-start(f32[4,104,128]{2,1,0:T(8,128)S(1)} %all-to-all-done.1.a), channel_id=1, source_target_pairs={{0,1},{1,2},{2,3},{3,0},{4,5},{5,6},{6,7},{7,4},{8,9},{9,10},{10,1... | collective-permute-start | bytes 638984 | tf_op jit(solution)/shard_map/ppermute | solution.py:146
  64.0 2.5 %collective-permute-start.17 = (f32[4,104,128]{2,1,0:T(8,128)S(1)}, f32[4,104,128]{2,1,0:T(8,128)S(1)}, u32[]{:S(2)}, u32[]{:S(2)}) collective-permute-start(f32[4,104,128]{2,1,0:T(8,128)S(1)} %all-to-all-done.1.a), channel_id=1, source_target_pairs={{0,3},{1,0},{2,1},{3,2},{4,7},{5,4},{6,5},{7,6},{8,11},{9,8},{10,9... | collective-permute-start | bytes 638984 | tf_op jit(solution)/shard_map/ppermute | solution.py:146
  66.5 2.7 %collective-permute-start.18 = (f32[4,104,128]{2,1,0:T(8,128)S(1)}, f32[4,104,128]{2,1,0:T(8,128)S(1)}, u32[]{:S(2)}, u32[]{:S(2)}) collective-permute-start(f32[4,104,128]{2,1,0:T(8,128)S(1)} %all-to-all-done.2.a), channel_id=1, source_target_pairs={{0,1},{1,2},{2,3},{3,0},{4,5},{5,6},{6,7},{7,4},{8,9},{9,10},{10,1... | collective-permute-start | bytes 638984 | tf_op jit(solution)/shard_map/ppermute | solution.py:146
  69.6 2.6 %collective-permute-start.20 = (f32[4,104,128]{2,1,0:T(8,128)S(1)}, f32[4,104,128]{2,1,0:T(8,128)S(1)}, u32[]{:S(2)}, u32[]{:S(2)}) collective-permute-start(f32[4,104,128]{2,1,0:T(8,128)S(1)} %all-to-all-done.2.a), channel_id=1, source_target_pairs={{0,3},{1,0},{2,1},{3,2},{4,7},{5,4},{6,5},{7,6},{8,11},{9,8},{10,9... | collective-permute-start | bytes 638984 | tf_op jit(solution)/shard_map/ppermute | solution.py:146
  72.2 1.8 %collective-permute-start.21 = (f32[416,128]{1,0:T(8,128)S(1)}, f32[416,128]{1,0:T(8,128)S(1)}, u32[]{:S(2)}, u32[]{:S(2)}) collective-permute-start(f32[416,128]{1,0:T(8,128)S(1)} %get-tuple-element.199.mine), channel_id=1, source_target_pairs={{0,24},{16,9},{25,1},{9,16},{2,26},{18,11},{27,3},{11,18},{4,28},{... | collective-permute-start | bytes 638984 | tf_op jit(solution)/shard_map/ppermute | solution.py:155
  74.4 1.3 collective-permute-start.23
  75.7 1.0 collective-permute-done.21.crossed
  77.4 2.4 %collective-permute-done.19.c = f32[4,104,128]{2,1,0:T(8,128)S(1)} collective-permute-done((f32[4,104,128]{2,1,0:T(8,128)S(1)}, f32[4,104,128]{2,1,0:T(8,128)S(1)}, u32[]{:S(2)}, u32[]{:S(2)}) %collective-permute-start.19) | collective-permute-done | bytes 213024 | tf_op jit(solution)/shard_map/ppermute | solution.py:146
  81.1 1.4 collective-permute-start.25
  82.5 7.1 %collective-permute-start.29 = (f32[416,128]{1,0:T(8,128)S(1)}, f32[416,128]{1,0:T(8,128)S(1)}, u32[]{:S(2)}, u32[]{:S(2)}) collective-permute-start(f32[416,128]{1,0:T(8,128)S(1)} %get-tuple-element.243.mine), channel_id=1, source_target_pairs={{0,24},{16,9},{25,1},{9,16},{2,26},{18,11},{27,3},{11,18},{4,28},{... | collective-permute-start | bytes 638984 | tf_op jit(solution)/shard_map/ppermute | solution.py:155
  89.7 2.0 %shard_map.41 = (f32[4,384,128]{2,1,0:T(8,128)S(1)}, f32[4,384,128]{2,1,0:T(8,128)S(1)}) custom-call(s32[2]{0:T(128)S(1)} %add_convert_fusion.flags_ref, bf16[4,128,416]{2,1,0:T(8,128)(2,1)S(1)} %get-tuple-element.251.refs_0_, bf16[4,128,416]{2,1,0:T(8,128)(2,1)S(1)} %get-tuple-element.252.refs_1_, bf16[4,128,416]{2,1,0:T(8,128)(2,1)S(1)} %get-tuple-element.253.refs_2_, ...), custom_call_target="tpu_custom_call" | custom-call | flops 12000000000 | bytes 44000000 | tf_op jit(solution)/shard_map/pallas_call | solution.py:175
  91.7 14.0 %collective-permute-start.24 = (f32[4,384,128]{2,1,0:T(8,128)S(1)}, f32[4,384,128]{2,1,0:T(8,128)S(1)}, u32[]{:S(2)}, u32[]{:S(2)}) collective-permute-start(f32[4,384,128]{2,1,0:T(8,128)S(1)} %get-tuple-element.223), channel_id=1, source_target_pairs={{0,128},{128,0},{1,129},{129,1},{2,130},{130,2},{3,131},{131,3},{4... | collective-permute-start | bytes 2359304 | tf_op jit(solution)/shard_map/ppermute | solution.py:141
  105.7 2.0 %shard_map.42 = (f32[4,384,128]{2,1,0:T(8,128)S(1)}, f32[4,384,128]{2,1,0:T(8,128)S(1)}) custom-call(s32[2]{0:T(128)S(1)} %add_convert_fusion.flags_ref, bf16[4,128,416]{2,1,0:T(8,128)(2,1)S(1)} %get-tuple-element.251.refs_0_, bf16[4,128,416]{2,1,0:T(8,128)(2,1)S(1)} %get-tuple-element.252.refs_1_, bf16[4,128,416]{2,1,0:T(8,128)(2,1)S(1)} %get-tuple-element.253.refs_2_, ...), custom_call_target="tpu_custom_call" | custom-call | flops 12000000000 | bytes 44000000 | tf_op jit(solution)/shard_map/pallas_call | solution.py:175
  107.9 1.6 %collective-permute-start.26 = (f32[384,128]{1,0:T(8,128)S(1)}, f32[384,128]{1,0:T(8,128)S(1)}, u32[]{:S(2)}, u32[]{:S(2)}) collective-permute-start(f32[384,128]{1,0:T(8,128)S(1)} %get-tuple-element.238), channel_id=1, source_target_pairs={{0,64},{32,96},{64,0},{96,32},{1,65},{33,97},{65,1},{97,33},{2,66}... | collective-permute-start | bytes 589832 | tf_op jit(solution)/shard_map/ppermute | solution.py:146
  109.8 2.4 %collective-permute-start.28 = (f32[384,128]{1,0:T(8,128)S(1)}, f32[384,128]{1,0:T(8,128)S(1)}, u32[]{:S(2)}, u32[]{:S(2)}) collective-permute-start(f32[384,128]{1,0:T(8,128)S(1)} %get-tuple-element.240), channel_id=1, source_target_pairs={{0,96},{32,0},{64,32},{96,64},{1,97},{33,1},{65,33},{97,65},{2,98}... | collective-permute-start | bytes 589832 | tf_op jit(solution)/shard_map/ppermute | solution.py:146
  113.3 4.9 %collective-permute-done.30.refs_7_ = f32[416,128]{1,0:T(8,128)S(1)} collective-permute-done((f32[416,128]{1,0:T(8,128)S(1)}, f32[416,128]{1,0:T(8,128)S(1)}, u32[]{:S(2)}, u32[]{:S(2)}) %collective-permute-start.30) | collective-permute-done | bytes 213024 | tf_op jit(solution)/shard_map/ppermute | solution.py:237
  118.2 2.0 %shard_map.46 = (f32[4,384,128]{2,1,0:T(8,128)S(1)}, f32[4,384,128]{2,1,0:T(8,128)S(1)}) custom-call(s32[2]{0:T(128)S(1)} %add_convert_fusion.flags_ref, bf16[4,128,416]{2,1,0:T(8,128)(2,1)S(1)} %get-tuple-element.251.refs_0_, bf16[4,128,416]{2,1,0:T(8,128)(2,1)S(1)} %get-tuple-element.252.refs_1_, bf16[4,128,416]{2,1,0:T(8,128)(2,1)S(1)} %get-tuple-element.253.refs_2_, ...), custom_call_target="tpu_custom_call" | custom-call | flops 12000000000 | bytes 44000000 | tf_op jit(solution)/shard_map/pallas_call | solution.py:175
  120.2 2.8 %collective-permute-start.34 = (f32[384,128]{1,0:T(8,128)S(1)}, f32[384,128]{1,0:T(8,128)S(1)}, u32[]{:S(2)}, u32[]{:S(2)}) collective-permute-start(f32[384,128]{1,0:T(8,128)S(1)} %get-tuple-element.266), channel_id=1, source_target_pairs={{0,96},{32,0},{64,32},{96,64},{1,97},{33,1},{65,33},{97,65},{2,98}... | collective-permute-start | bytes 589832 | tf_op jit(solution)/shard_map/ppermute | solution.py:146
  123.0 2.8 %collective-permute-start.35 = (f32[4,384,128]{2,1,0:T(8,128)S(1)}, f32[4,384,128]{2,1,0:T(8,128)S(1)}, u32[]{:S(2)}, u32[]{:S(2)}) collective-permute-start(f32[4,384,128]{2,1,0:T(8,128)S(1)} %get-tuple-element.259), channel_id=1, source_target_pairs={{0,128},{128,0},{1,129},{129,1},{2,130},{130,2},{3,131},{131,3},{4... | collective-permute-start | bytes 2359304 | tf_op jit(solution)/shard_map/ppermute | solution.py:141
  125.8 1.9 %collective-permute-done.35.two_ref = f32[4,384,128]{2,1,0:T(8,128)S(1)} collective-permute-done((f32[4,384,128]{2,1,0:T(8,128)S(1)}, f32[4,384,128]{2,1,0:T(8,128)S(1)}, u32[]{:S(2)}, u32[]{:S(2)}) %collective-permute-start.35) | collective-permute-done | bytes 786464 | tf_op jit(solution)/shard_map/ppermute | solution.py:141
  127.8 0.8 collective-permute-done.33.c
  128.6 1.7 %collective-permute-start.36 = (f32[384,128]{1,0:T(8,128)S(1)}, f32[384,128]{1,0:T(8,128)S(1)}, u32[]{:S(2)}, u32[]{:S(2)}) collective-permute-start(f32[384,128]{1,0:T(8,128)S(1)} %get-tuple-element.276), channel_id=1, source_target_pairs={{0,64},{32,96},{64,0},{96,32},{1,65},{33,97},{65,1},{97,33},{2,66}... | collective-permute-start | bytes 589832 | tf_op jit(solution)/shard_map/ppermute | solution.py:146
  130.3 2.7 %collective-permute-start.38 = (f32[384,128]{1,0:T(8,128)S(1)}, f32[384,128]{1,0:T(8,128)S(1)}, u32[]{:S(2)}, u32[]{:S(2)}) collective-permute-start(f32[384,128]{1,0:T(8,128)S(1)} %get-tuple-element.278), channel_id=1, source_target_pairs={{0,96},{32,0},{64,32},{96,64},{1,97},{33,1},{65,33},{97,65},{2,98}... | collective-permute-start | bytes 589832 | tf_op jit(solution)/shard_map/ppermute | solution.py:146
  133.0 2.5 %collective-permute-done.36.b = f32[384,128]{1,0:T(8,128)S(1)} collective-permute-done((f32[384,128]{1,0:T(8,128)S(1)}, f32[384,128]{1,0:T(8,128)S(1)}, u32[]{:S(2)}, u32[]{:S(2)}) %collective-permute-start.36) | collective-permute-done | bytes 196640 | tf_op jit(solution)/shard_map/ppermute | solution.py:146
  135.6 5.6 %collective-permute-done.37.c = f32[384,128]{1,0:T(8,128)S(1)} collective-permute-done((f32[384,128]{1,0:T(8,128)S(1)}, f32[384,128]{1,0:T(8,128)S(1)}, u32[]{:S(2)}, u32[]{:S(2)}) %collective-permute-start.37) | collective-permute-done | bytes 196640 | tf_op jit(solution)/shard_map/ppermute | solution.py:146
  141.1 0.9 shard_map.50
  (66 shorter events, 6.1 us)
Async XLA Ops:
  0.0 11.3 %copy-start = (f32[768,800]{0,1:T(8,128)S(1)}, f32[768,800]{0,1:T(8,128)}, u32[]{:S(2)}) copy-start(f32[768,800]{0,1:T(8,128)} %param.3) | copy-start | bytes 7372804
  4.9 13.1 %collective-permute-start = (f32[400,128]{1,0:T(8,128)}, f32[400,128]{1,0:T(8,128)S(1)}, u32[]{:S(2)}, u32[]{:S(2)}) collective-permute-start(f32[400,128]{1,0:T(8,128)} %get-tuple-element.146), channel_id=1, source_target_pairs={{0,2},{1,3},{2,0},{3,1},{4,6},{5,7},{6,4},{7,5},{8,10},{9,11},{10,... | collective-permute-start | bytes 614408 | tf_op jit(solution)/shard_map/ppermute | solution.py:146
  8.6 11.6 %collective-permute-start.1 = (f32[400,128]{1,0:T(8,128)}, f32[400,128]{1,0:T(8,128)S(1)}, u32[]{:S(2)}, u32[]{:S(2)}) collective-permute-start(f32[400,128]{1,0:T(8,128)} %get-tuple-element.147), channel_id=1, source_target_pairs={{0,1},{1,2},{2,3},{3,0},{4,5},{5,6},{6,7},{7,4},{8,9},{9,10},{10,1... | collective-permute-start | bytes 614408 | tf_op jit(solution)/shard_map/ppermute | solution.py:146
  9.0 11.2 %collective-permute-start.2 = (f32[400,128]{1,0:T(8,128)}, f32[400,128]{1,0:T(8,128)S(1)}, u32[]{:S(2)}, u32[]{:S(2)}) collective-permute-start(f32[400,128]{1,0:T(8,128)} %get-tuple-element.148), channel_id=1, source_target_pairs={{0,3},{1,0},{2,1},{3,2},{4,7},{5,4},{6,5},{7,6},{8,11},{9,8},{10,9... | collective-permute-start | bytes 614408 | tf_op jit(solution)/shard_map/ppermute | solution.py:146
  11.3 1.7 %copy-start.1 = (f32[2,384,768]{2,1,0:T(8,128)S(1)}, f32[2,384,768]{2,1,0:T(8,128)}, u32[]{:S(2)}) copy-start(f32[2,384,768]{2,1,0:T(8,128)} %refs_1_) | copy-start | bytes 7077892
  13.0 7.2 %copy-start.2 = (f32[400,128]{1,0:T(8,128)S(1)}, f32[400,128]{1,0:T(8,128)}, u32[]{:S(2)}) copy-start(f32[400,128]{1,0:T(8,128)} %get-tuple-element.153.a) | copy-start | bytes 614404
  17.4 11.6 %collective-permute-start.11 = (f32[400,128]{1,0:T(8,128)S(1)}, f32[400,128]{1,0:T(8,128)S(1)}, u32[]{:S(2)}, u32[]{:S(2)}) collective-permute-start(f32[400,128]{1,0:T(8,128)S(1)} %get-tuple-element.170), channel_id=1, source_target_pairs={{0,2},{1,3},{2,0},{3,1},{4,6},{5,7},{6,4},{7,5},{8,10},{9,11},{10,... | collective-permute-start | bytes 614408 | tf_op jit(solution)/shard_map/ppermute | solution.py:146
  17.5 12.5 %collective-permute-start.12 = (f32[400,128]{1,0:T(8,128)S(1)}, f32[400,128]{1,0:T(8,128)S(1)}, u32[]{:S(2)}, u32[]{:S(2)}) collective-permute-start(f32[400,128]{1,0:T(8,128)S(1)} %get-tuple-element.171), channel_id=1, source_target_pairs={{0,1},{1,2},{2,3},{3,0},{4,5},{5,6},{6,7},{7,4},{8,9},{9,10},{10,1... | collective-permute-start | bytes 614408 | tf_op jit(solution)/shard_map/ppermute | solution.py:146
  18.0 13.6 %collective-permute-start.13 = (f32[400,128]{1,0:T(8,128)S(1)}, f32[400,128]{1,0:T(8,128)S(1)}, u32[]{:S(2)}, u32[]{:S(2)}) collective-permute-start(f32[400,128]{1,0:T(8,128)S(1)} %get-tuple-element.172), channel_id=1, source_target_pairs={{0,3},{1,0},{2,1},{3,2},{4,7},{5,4},{6,5},{7,6},{8,11},{9,8},{10,9... | collective-permute-start | bytes 614408 | tf_op jit(solution)/shard_map/ppermute | solution.py:146
  20.3 18.2 %collective-permute-start.3 = (f32[400,128]{1,0:T(8,128)S(1)}, f32[400,128]{1,0:T(8,128)S(1)}, u32[]{:S(2)}, u32[]{:S(2)}) collective-permute-start(f32[400,128]{1,0:T(8,128)S(1)} %shard_map.30.one_ref), channel_id=1, source_target_pairs={{0,4},{4,0},{1,5},{5,1},{2,6},{6,2},{3,7},{7,3},{8,12},{12,8},{9,1... | collective-permute-start | bytes 614408 | tf_op jit(solution)/shard_map/ppermute | solution.py:141
  27.3 15.9 %collective-permute-start.7 = (f32[400,128]{1,0:T(8,128)S(1)}, f32[400,128]{1,0:T(8,128)S(1)}, u32[]{:S(2)}, u32[]{:S(2)}) collective-permute-start(f32[400,128]{1,0:T(8,128)S(1)} %get-tuple-element.163), channel_id=1, source_target_pairs={{0,2},{1,3},{2,0},{3,1},{4,6},{5,7},{6,4},{7,5},{8,10},{9,11},{10,... | collective-permute-start | bytes 614408 | tf_op jit(solution)/shard_map/ppermute | solution.py:146
  29.0 14.2 %collective-permute-start.8 = (f32[400,128]{1,0:T(8,128)S(1)}, f32[400,128]{1,0:T(8,128)S(1)}, u32[]{:S(2)}, u32[]{:S(2)}) collective-permute-start(f32[400,128]{1,0:T(8,128)S(1)} %get-tuple-element.164), channel_id=1, source_target_pairs={{0,1},{1,2},{2,3},{3,0},{4,5},{5,6},{6,7},{7,4},{8,9},{9,10},{10,1... | collective-permute-start | bytes 614408 | tf_op jit(solution)/shard_map/ppermute | solution.py:146
  29.9 13.2 %collective-permute-start.9 = (f32[400,128]{1,0:T(8,128)S(1)}, f32[400,128]{1,0:T(8,128)S(1)}, u32[]{:S(2)}, u32[]{:S(2)}) collective-permute-start(f32[400,128]{1,0:T(8,128)S(1)} %get-tuple-element.165), channel_id=1, source_target_pairs={{0,3},{1,0},{2,1},{3,2},{4,7},{5,4},{6,5},{7,6},{8,11},{9,8},{10,9... | collective-permute-start | bytes 614408 | tf_op jit(solution)/shard_map/ppermute | solution.py:146
  31.7 14.1 %collective-permute-start.14 = (f32[400,128]{1,0:T(8,128)S(1)}, f32[400,128]{1,0:T(8,128)S(1)}, u32[]{:S(2)}, u32[]{:S(2)}) collective-permute-start(f32[400,128]{1,0:T(8,128)S(1)} %shard_map.33.one_ref), channel_id=1, source_target_pairs={{0,4},{4,0},{1,5},{5,1},{2,6},{6,2},{3,7},{7,3},{8,12},{12,8},{9,1... | collective-permute-start | bytes 614408 | tf_op jit(solution)/shard_map/ppermute | solution.py:141
  39.2 9.3 %all-to-all-start = ((f32[4,104,128]{2,1,0:T(8,128)}), f32[4,104,128]{2,1,0:T(8,128)S(1)}, u32[]{:S(2)}, u32[]{:S(2)}) async-start(f32[4,104,128]{2,1,0:T(8,128)} %shard_map.31), calls=%async_computation | async-start | bytes 425984 | tf_op jit(solution)/shard_map/all_to_all | solution.py:225
  43.2 12.6 %collective-permute-start.10 = (f32[400,128]{1,0:T(8,128)S(1)}, f32[400,128]{1,0:T(8,128)S(1)}, u32[]{:S(2)}, u32[]{:S(2)}) collective-permute-start(f32[400,128]{1,0:T(8,128)S(1)} %shard_map.32.one_ref), channel_id=1, source_target_pairs={{0,4},{4,0},{1,5},{5,1},{2,6},{6,2},{3,7},{7,3},{8,12},{12,8},{9,1... | collective-permute-start | bytes 614408 | tf_op jit(solution)/shard_map/ppermute | solution.py:141
  48.4 8.9 %all-to-all-start.1 = ((f32[4,104,128]{2,1,0:T(8,128)}), f32[4,104,128]{2,1,0:T(8,128)S(1)}, u32[]{:S(2)}, u32[]{:S(2)}) async-start(f32[4,104,128]{2,1,0:T(8,128)} %shard_map.34), calls=%async_computation.1 | async-start | bytes 425984 | tf_op jit(solution)/shard_map/all_to_all | solution.py:225
  51.8 12.2 %collective-permute-start.4 = (f32[4,104,128]{2,1,0:T(8,128)S(1)}, f32[4,104,128]{2,1,0:T(8,128)S(1)}, u32[]{:S(2)}, u32[]{:S(2)}) collective-permute-start(f32[4,104,128]{2,1,0:T(8,128)S(1)} %all-to-all-done.a), channel_id=1, source_target_pairs={{0,1},{1,2},{2,3},{3,0},{4,5},{5,6},{6,7},{7,4},{8,9},{9,10},{10,1... | collective-permute-start | bytes 638984 | tf_op jit(solution)/shard_map/ppermute | solution.py:146
  53.4 13.1 %collective-permute-start.5 = (f32[4,104,128]{2,1,0:T(8,128)S(1)}, f32[4,104,128]{2,1,0:T(8,128)S(1)}, u32[]{:S(2)}, u32[]{:S(2)}) collective-permute-start(f32[4,104,128]{2,1,0:T(8,128)S(1)} %all-to-all-done.a), channel_id=1, source_target_pairs={{0,2},{1,3},{2,0},{3,1},{4,6},{5,7},{6,4},{7,5},{8,10},{9,11},{10,... | collective-permute-start | bytes 638984 | tf_op jit(solution)/shard_map/ppermute | solution.py:146
  53.5 15.7 %collective-permute-start.6 = (f32[4,104,128]{2,1,0:T(8,128)S(1)}, f32[4,104,128]{2,1,0:T(8,128)S(1)}, u32[]{:S(2)}, u32[]{:S(2)}) collective-permute-start(f32[4,104,128]{2,1,0:T(8,128)S(1)} %all-to-all-done.a), channel_id=1, source_target_pairs={{0,3},{1,0},{2,1},{3,2},{4,7},{5,4},{6,5},{7,6},{8,11},{9,8},{10,9... | collective-permute-start | bytes 638984 | tf_op jit(solution)/shard_map/ppermute | solution.py:146
  57.3 9.1 %all-to-all-start.2 = ((f32[4,104,128]{2,1,0:T(8,128)}), f32[4,104,128]{2,1,0:T(8,128)S(1)}, u32[]{:S(2)}, u32[]{:S(2)}) async-start(f32[4,104,128]{2,1,0:T(8,128)} %shard_map.35), calls=%async_computation.2 | async-start | bytes 425984 | tf_op jit(solution)/shard_map/all_to_all | solution.py:225
  60.9 8.7 %collective-permute-start.15 = (f32[4,104,128]{2,1,0:T(8,128)S(1)}, f32[4,104,128]{2,1,0:T(8,128)S(1)}, u32[]{:S(2)}, u32[]{:S(2)}) collective-permute-start(f32[4,104,128]{2,1,0:T(8,128)S(1)} %all-to-all-done.1.a), channel_id=1, source_target_pairs={{0,1},{1,2},{2,3},{3,0},{4,5},{5,6},{6,7},{7,4},{8,9},{9,10},{10,1... | collective-permute-start | bytes 638984 | tf_op jit(solution)/shard_map/ppermute | solution.py:146
  64.0 8.2 %collective-permute-start.16 = (f32[4,104,128]{2,1,0:T(8,128)S(1)}, f32[4,104,128]{2,1,0:T(8,128)S(1)}, u32[]{:S(2)}, u32[]{:S(2)}) collective-permute-start(f32[4,104,128]{2,1,0:T(8,128)S(1)} %all-to-all-done.1.a), channel_id=1, source_target_pairs={{0,2},{1,3},{2,0},{3,1},{4,6},{5,7},{6,4},{7,5},{8,10},{9,11},{10,... | collective-permute-start | bytes 638984 | tf_op jit(solution)/shard_map/ppermute | solution.py:146
  64.0 8.2 %collective-permute-start.17 = (f32[4,104,128]{2,1,0:T(8,128)S(1)}, f32[4,104,128]{2,1,0:T(8,128)S(1)}, u32[]{:S(2)}, u32[]{:S(2)}) collective-permute-start(f32[4,104,128]{2,1,0:T(8,128)S(1)} %all-to-all-done.1.a), channel_id=1, source_target_pairs={{0,3},{1,0},{2,1},{3,2},{4,7},{5,4},{6,5},{7,6},{8,11},{9,8},{10,9... | collective-permute-start | bytes 638984 | tf_op jit(solution)/shard_map/ppermute | solution.py:146
  66.5 10.9 %collective-permute-start.18 = (f32[4,104,128]{2,1,0:T(8,128)S(1)}, f32[4,104,128]{2,1,0:T(8,128)S(1)}, u32[]{:S(2)}, u32[]{:S(2)}) collective-permute-start(f32[4,104,128]{2,1,0:T(8,128)S(1)} %all-to-all-done.2.a), channel_id=1, source_target_pairs={{0,1},{1,2},{2,3},{3,0},{4,5},{5,6},{6,7},{7,4},{8,9},{9,10},{10,1... | collective-permute-start | bytes 638984 | tf_op jit(solution)/shard_map/ppermute | solution.py:146
  69.2 10.6 %collective-permute-start.19 = (f32[4,104,128]{2,1,0:T(8,128)S(1)}, f32[4,104,128]{2,1,0:T(8,128)S(1)}, u32[]{:S(2)}, u32[]{:S(2)}) collective-permute-start(f32[4,104,128]{2,1,0:T(8,128)S(1)} %all-to-all-done.2.a), channel_id=1, source_target_pairs={{0,2},{1,3},{2,0},{3,1},{4,6},{5,7},{6,4},{7,5},{8,10},{9,11},{10,... | collective-permute-start | bytes 638984 | tf_op jit(solution)/shard_map/ppermute | solution.py:146
  69.6 10.6 %collective-permute-start.20 = (f32[4,104,128]{2,1,0:T(8,128)S(1)}, f32[4,104,128]{2,1,0:T(8,128)S(1)}, u32[]{:S(2)}, u32[]{:S(2)}) collective-permute-start(f32[4,104,128]{2,1,0:T(8,128)S(1)} %all-to-all-done.2.a), channel_id=1, source_target_pairs={{0,3},{1,0},{2,1},{3,2},{4,7},{5,4},{6,5},{7,6},{8,11},{9,8},{10,9... | collective-permute-start | bytes 638984 | tf_op jit(solution)/shard_map/ppermute | solution.py:146
  72.2 4.6 %collective-permute-start.21 = (f32[416,128]{1,0:T(8,128)S(1)}, f32[416,128]{1,0:T(8,128)S(1)}, u32[]{:S(2)}, u32[]{:S(2)}) collective-permute-start(f32[416,128]{1,0:T(8,128)S(1)} %get-tuple-element.199.mine), channel_id=1, source_target_pairs={{0,24},{16,9},{25,1},{9,16},{2,26},{18,11},{27,3},{11,18},{4,28},{... | collective-permute-start | bytes 638984 | tf_op jit(solution)/shard_map/ppermute | solution.py:155
  74.4 6.2 %collective-permute-start.23 = (f32[416,128]{1,0:T(8,128)S(1)}, f32[416,128]{1,0:T(8,128)S(1)}, u32[]{:S(2)}, u32[]{:S(2)}) collective-permute-start(f32[416,128]{1,0:T(8,128)S(1)} %get-tuple-element.211.mine), channel_id=1, source_target_pairs={{0,24},{16,9},{25,1},{9,16},{2,26},{18,11},{27,3},{11,18},{4,28},{... | collective-permute-start | bytes 638984 | tf_op jit(solution)/shard_map/ppermute | solution.py:155
  77.3 12.4 %collective-permute-start.22 = (f32[416,128]{1,0:T(8,128)S(1)}, f32[416,128]{1,0:T(8,128)S(1)}, u32[]{:S(2)}, u32[]{:S(2)}) collective-permute-start(f32[416,128]{1,0:T(8,128)S(1)} %shard_map.38.refs_6_), channel_id=1, source_target_pairs={{0,8},{8,0},{16,24},{24,16},{1,9},{9,1},{17,25},{25,17},{2,10},{10... | collective-permute-start | bytes 638984 | tf_op jit(solution)/shard_map/ppermute | solution.py:237
  81.1 24.6 %collective-permute-start.25 = (f32[416,128]{1,0:T(8,128)S(1)}, f32[416,128]{1,0:T(8,128)S(1)}, u32[]{:S(2)}, u32[]{:S(2)}) collective-permute-start(f32[416,128]{1,0:T(8,128)S(1)} %shard_map.40.refs_6_), channel_id=1, source_target_pairs={{0,8},{8,0},{16,24},{24,16},{1,9},{9,1},{17,25},{25,17},{2,10},{10... | collective-permute-start | bytes 638984 | tf_op jit(solution)/shard_map/ppermute | solution.py:237
  82.5 29.6 %collective-permute-start.29 = (f32[416,128]{1,0:T(8,128)S(1)}, f32[416,128]{1,0:T(8,128)S(1)}, u32[]{:S(2)}, u32[]{:S(2)}) collective-permute-start(f32[416,128]{1,0:T(8,128)S(1)} %get-tuple-element.243.mine), channel_id=1, source_target_pairs={{0,24},{16,9},{25,1},{9,16},{2,26},{18,11},{27,3},{11,18},{4,28},{... | collective-permute-start | bytes 638984 | tf_op jit(solution)/shard_map/ppermute | solution.py:155
  91.7 16.1 %collective-permute-start.24 = (f32[4,384,128]{2,1,0:T(8,128)S(1)}, f32[4,384,128]{2,1,0:T(8,128)S(1)}, u32[]{:S(2)}, u32[]{:S(2)}) collective-permute-start(f32[4,384,128]{2,1,0:T(8,128)S(1)} %get-tuple-element.223), channel_id=1, source_target_pairs={{0,128},{128,0},{1,129},{129,1},{2,130},{130,2},{3,131},{131,3},{4... | collective-permute-start | bytes 2359304 | tf_op jit(solution)/shard_map/ppermute | solution.py:141
  107.7 5.2 %collective-permute-start.31 = (f32[4,384,128]{2,1,0:T(8,128)S(1)}, f32[4,384,128]{2,1,0:T(8,128)S(1)}, u32[]{:S(2)}, u32[]{:S(2)}) collective-permute-start(f32[4,384,128]{2,1,0:T(8,128)S(1)} %get-tuple-element.233), channel_id=1, source_target_pairs={{0,128},{128,0},{1,129},{129,1},{2,130},{130,2},{3,131},{131,3},{4... | collective-permute-start | bytes 2359304 | tf_op jit(solution)/shard_map/ppermute | solution.py:141
  107.9 12.3 %collective-permute-start.26 = (f32[384,128]{1,0:T(8,128)S(1)}, f32[384,128]{1,0:T(8,128)S(1)}, u32[]{:S(2)}, u32[]{:S(2)}) collective-permute-start(f32[384,128]{1,0:T(8,128)S(1)} %get-tuple-element.238), channel_id=1, source_target_pairs={{0,64},{32,96},{64,0},{96,32},{1,65},{33,97},{65,1},{97,33},{2,66}... | collective-permute-start | bytes 589832 | tf_op jit(solution)/shard_map/ppermute | solution.py:146
  109.5 13.5 %collective-permute-start.27 = (f32[384,128]{1,0:T(8,128)S(1)}, f32[384,128]{1,0:T(8,128)S(1)}, u32[]{:S(2)}, u32[]{:S(2)}) collective-permute-start(f32[384,128]{1,0:T(8,128)S(1)} %get-tuple-element.239), channel_id=1, source_target_pairs={{0,32},{32,64},{64,96},{96,0},{1,33},{33,65},{65,97},{97,1},{2,34}... | collective-permute-start | bytes 589832 | tf_op jit(solution)/shard_map/ppermute | solution.py:146
  109.8 16.0 %collective-permute-start.28 = (f32[384,128]{1,0:T(8,128)S(1)}, f32[384,128]{1,0:T(8,128)S(1)}, u32[]{:S(2)}, u32[]{:S(2)}) collective-permute-start(f32[384,128]{1,0:T(8,128)S(1)} %get-tuple-element.240), channel_id=1, source_target_pairs={{0,96},{32,0},{64,32},{96,64},{1,97},{33,1},{65,33},{97,65},{2,98}... | collective-permute-start | bytes 589832 | tf_op jit(solution)/shard_map/ppermute | solution.py:146
  112.7 5.5 %collective-permute-start.30 = (f32[416,128]{1,0:T(8,128)S(1)}, f32[416,128]{1,0:T(8,128)S(1)}, u32[]{:S(2)}, u32[]{:S(2)}) collective-permute-start(f32[416,128]{1,0:T(8,128)S(1)} %shard_map.44.refs_6_), channel_id=1, source_target_pairs={{0,8},{8,0},{16,24},{24,16},{1,9},{9,1},{17,25},{25,17},{2,10},{10... | collective-permute-start | bytes 638984 | tf_op jit(solution)/shard_map/ppermute | solution.py:237
  112.9 14.9 %collective-permute-start.32 = (f32[384,128]{1,0:T(8,128)S(1)}, f32[384,128]{1,0:T(8,128)S(1)}, u32[]{:S(2)}, u32[]{:S(2)}) collective-permute-start(f32[384,128]{1,0:T(8,128)S(1)} %get-tuple-element.264), channel_id=1, source_target_pairs={{0,64},{32,96},{64,0},{96,32},{1,65},{33,97},{65,1},{97,33},{2,66}... | collective-permute-start | bytes 589832 | tf_op jit(solution)/shard_map/ppermute | solution.py:146
  118.2 10.3 %collective-permute-start.33 = (f32[384,128]{1,0:T(8,128)S(1)}, f32[384,128]{1,0:T(8,128)S(1)}, u32[]{:S(2)}, u32[]{:S(2)}) collective-permute-start(f32[384,128]{1,0:T(8,128)S(1)} %get-tuple-element.265), channel_id=1, source_target_pairs={{0,32},{32,64},{64,96},{96,0},{1,33},{33,65},{65,97},{97,1},{2,34}... | collective-permute-start | bytes 589832 | tf_op jit(solution)/shard_map/ppermute | solution.py:146
  120.2 8.4 %collective-permute-start.34 = (f32[384,128]{1,0:T(8,128)S(1)}, f32[384,128]{1,0:T(8,128)S(1)}, u32[]{:S(2)}, u32[]{:S(2)}) collective-permute-start(f32[384,128]{1,0:T(8,128)S(1)} %get-tuple-element.266), channel_id=1, source_target_pairs={{0,96},{32,0},{64,32},{96,64},{1,97},{33,1},{65,33},{97,65},{2,98}... | collective-permute-start | bytes 589832 | tf_op jit(solution)/shard_map/ppermute | solution.py:146
  123.0 4.7 %collective-permute-start.35 = (f32[4,384,128]{2,1,0:T(8,128)S(1)}, f32[4,384,128]{2,1,0:T(8,128)S(1)}, u32[]{:S(2)}, u32[]{:S(2)}) collective-permute-start(f32[4,384,128]{2,1,0:T(8,128)S(1)} %get-tuple-element.259), channel_id=1, source_target_pairs={{0,128},{128,0},{1,129},{129,1},{2,130},{130,2},{3,131},{131,3},{4... | collective-permute-start | bytes 2359304 | tf_op jit(solution)/shard_map/ppermute | solution.py:141
  128.6 7.0 %collective-permute-start.36 = (f32[384,128]{1,0:T(8,128)S(1)}, f32[384,128]{1,0:T(8,128)S(1)}, u32[]{:S(2)}, u32[]{:S(2)}) collective-permute-start(f32[384,128]{1,0:T(8,128)S(1)} %get-tuple-element.276), channel_id=1, source_target_pairs={{0,64},{32,96},{64,0},{96,32},{1,65},{33,97},{65,1},{97,33},{2,66}... | collective-permute-start | bytes 589832 | tf_op jit(solution)/shard_map/ppermute | solution.py:146
  130.3 10.8 %collective-permute-start.37 = (f32[384,128]{1,0:T(8,128)S(1)}, f32[384,128]{1,0:T(8,128)S(1)}, u32[]{:S(2)}, u32[]{:S(2)}) collective-permute-start(f32[384,128]{1,0:T(8,128)S(1)} %get-tuple-element.277), channel_id=1, source_target_pairs={{0,32},{32,64},{64,96},{96,0},{1,33},{33,65},{65,97},{97,1},{2,34}... | collective-permute-start | bytes 589832 | tf_op jit(solution)/shard_map/ppermute | solution.py:146
  130.3 10.8 %collective-permute-start.38 = (f32[384,128]{1,0:T(8,128)S(1)}, f32[384,128]{1,0:T(8,128)S(1)}, u32[]{:S(2)}, u32[]{:S(2)}) collective-permute-start(f32[384,128]{1,0:T(8,128)S(1)} %get-tuple-element.278), channel_id=1, source_target_pairs={{0,96},{32,0},{64,32},{96,64},{1,97},{33,1},{65,33},{97,65},{2,98}... | collective-permute-start | bytes 589832 | tf_op jit(solution)/shard_map/ppermute | solution.py:146

commit v7 on v5

--- a/solution.py
+++ b/solution.py
@@ -264,8 +264,8 @@
     tile1 = tile_of(pair1)
     pair2 = pair_of(*half2)
     out0 = over_x_sum(*tile0)
+    tile2 = tile_of(pair2)
     out1 = over_x_sum(*tile1)
-    tile2 = tile_of(pair2)
     out0 = order(out_call, *out0)
     out2 = over_x_sum(*tile2)
     out1 = order(out_call, *out1)

time: 145 us -> 143 us (0.986)
  starting transfers between devices: 97.3 us -> 95.7 us
    ppermute x6, waiting for transfers between devices: 1.88 us -> 0.02 us  [swapped(): return lax.ppermute(value, axis, [(0, 1), (1, 0)])]
where the time goes in v7:
time: 143 us; the launch traced here: 141 us
  starting transfers between devices  95.7 us (67%)
  Pallas kernels  21.6 us (15%)
  waiting for transfers between devices  21.3 us (15%)
  local copies, waits for them, and re-layouts  1.67 us (1%)
    ppermute x27, starting transfers between devices, shifted(): lax.ppermute(value, axis, [(i, (i + distance) % size) for i in range(size)])  41.4 us
    ppermute x6, starting transfers between devices, swapped(): return lax.ppermute(value, axis, [(0, 1), (1, 0)])  33.7 us
    ppermute x27, waiting for transfers between devices, shifted(): lax.ppermute(value, axis, [(i, (i + distance) % size) for i in range(size)])  16.4 us
    pallas_call x21, Pallas kernels, __call__(): result = kernel(*operands)  12.3 us
    all_to_all x3, starting transfers between devices, over_x(): lax.all_to_all(order(piece_call, total, other), 'x', 0, 0, tiled=True)  10.8 us
    pallas_call x2, Pallas kernels, half_call(): pl.pallas_call(functools.partial(half_kernel, count), out_shape=[f32(size...  9.26 us
    ppermute x3, starting transfers between devices, along(): return lax.ppermute(value, ('zl', 'y'), pairs)  7.4 us
    all_to_all x3, waiting for transfers between devices, over_x(): lax.all_to_all(order(piece_call, total, other), 'x', 0, 0, tiled=True)  3.63 us
  transfers between devices with their start and end apart: 42, of which 11 were waited for; matrix products, arithmetic and copies ran while one was open for 0% of the time, Pallas kernels for 11%

profile of v7, /device:TPU:1, one launch (start us, length us, event | category | flops | bytes accessed | tf_op | source)
XLA Modules:
  0.0 140.6 jit_solution(3311323219455338829)
XLA Ops:
  0.0 4.9 %shard_map.28 = (f32[400,128]{1,0:T(8,128)}, f32[400,128]{1,0:T(8,128)}, f32[400,128]{1,0:T(8,128)}, f32[400,128]{1,0:T(8,128)}) custom-call(s32[1]{0:T(128)} %bitcast.3.here_ref, f32[800,768]{1,0:T(8,128)} %bitcast.6, f32[2,384,768]{2,1,0:T(8,128)} %refs_1_), custom_call_target="tpu_custom_call" | custom-call | flops 12000000000 | bytes 44000000 | tf_op jit(solution)/shard_map/pallas_call | solution.py:72
  4.9 3.7 %collective-permute-start = (f32[400,128]{1,0:T(8,128)}, f32[400,128]{1,0:T(8,128)S(1)}, u32[]{:S(2)}, u32[]{:S(2)}) collective-permute-start(f32[400,128]{1,0:T(8,128)} %get-tuple-element.146), channel_id=1, source_target_pairs={{0,2},{1,3},{2,0},{3,1},{4,6},{5,7},{6,4},{7,5},{8,10},{9,11},{10,... | collective-permute-start | bytes 614408 | tf_op jit(solution)/shard_map/ppermute | solution.py:146
  9.0 2.3 %collective-permute-start.2 = (f32[400,128]{1,0:T(8,128)}, f32[400,128]{1,0:T(8,128)S(1)}, u32[]{:S(2)}, u32[]{:S(2)}) collective-permute-start(f32[400,128]{1,0:T(8,128)} %get-tuple-element.148), channel_id=1, source_target_pairs={{0,3},{1,0},{2,1},{3,2},{4,7},{5,4},{6,5},{7,6},{8,11},{9,8},{10,9... | collective-permute-start | bytes 614408 | tf_op jit(solution)/shard_map/ppermute | solution.py:146
  11.3 1.7 %copy-done.1 = f32[2,384,768]{2,1,0:T(8,128)S(1)} copy-done((f32[2,384,768]{2,1,0:T(8,128)S(1)}, f32[2,384,768]{2,1,0:T(8,128)}, u32[]{:S(2)}) %copy-start.1) | copy-done | bytes 2359320
  13.0 4.4 %shard_map.29 = (f32[400,128]{1,0:T(8,128)S(1)}, f32[400,128]{1,0:T(8,128)S(1)}, f32[400,128]{1,0:T(8,128)S(1)}, f32[400,128]{1,0:T(8,128)S(1)}, f32[400,128]{1,...) custom-call(s32[1]{0:T(128)} %bitcast.3.here_ref, f32[800,768]{1,0:T(8,128)S(1)} %bitcast.7, ...), custom_call_target="tpu_custom_call" | custom-call | flops 12000000000 | bytes 44000000 | tf_op jit(solution)/shard_map/pallas_call | solution.py:72
  17.5 0.6 collective-permute-start.12
  18.0 2.2 %collective-permute-start.13 = (f32[400,128]{1,0:T(8,128)S(1)}, f32[400,128]{1,0:T(8,128)S(1)}, u32[]{:S(2)}, u32[]{:S(2)}) collective-permute-start(f32[400,128]{1,0:T(8,128)S(1)} %get-tuple-element.172), channel_id=1, source_target_pairs={{0,3},{1,0},{2,1},{3,2},{4,7},{5,4},{6,5},{7,6},{8,11},{9,8},{10,9... | collective-permute-start | bytes 614408 | tf_op jit(solution)/shard_map/ppermute | solution.py:146
  20.3 7.0 %collective-permute-start.3 = (f32[400,128]{1,0:T(8,128)S(1)}, f32[400,128]{1,0:T(8,128)S(1)}, u32[]{:S(2)}, u32[]{:S(2)}) collective-permute-start(f32[400,128]{1,0:T(8,128)S(1)} %shard_map.30.one_ref), channel_id=1, source_target_pairs={{0,4},{4,0},{1,5},{5,1},{2,6},{6,2},{3,7},{7,3},{8,12},{12,8},{9,1... | collective-permute-start | bytes 614408 | tf_op jit(solution)/shard_map/ppermute | solution.py:141
  27.3 1.7 %collective-permute-start.7 = (f32[400,128]{1,0:T(8,128)S(1)}, f32[400,128]{1,0:T(8,128)S(1)}, u32[]{:S(2)}, u32[]{:S(2)}) collective-permute-start(f32[400,128]{1,0:T(8,128)S(1)} %get-tuple-element.163), channel_id=1, source_target_pairs={{0,2},{1,3},{2,0},{3,1},{4,6},{5,7},{6,4},{7,5},{8,10},{9,11},{10,... | collective-permute-start | bytes 614408 | tf_op jit(solution)/shard_map/ppermute | solution.py:146
  29.0 1.0 collective-permute-done.12.c
  29.9 1.7 %collective-permute-start.9 = (f32[400,128]{1,0:T(8,128)S(1)}, f32[400,128]{1,0:T(8,128)S(1)}, u32[]{:S(2)}, u32[]{:S(2)}) collective-permute-start(f32[400,128]{1,0:T(8,128)S(1)} %get-tuple-element.165), channel_id=1, source_target_pairs={{0,3},{1,0},{2,1},{3,2},{4,7},{5,4},{6,5},{7,6},{8,11},{9,8},{10,9... | collective-permute-start | bytes 614408 | tf_op jit(solution)/shard_map/ppermute | solution.py:146
  31.7 6.7 %collective-permute-start.14 = (f32[400,128]{1,0:T(8,128)S(1)}, f32[400,128]{1,0:T(8,128)S(1)}, u32[]{:S(2)}, u32[]{:S(2)}) collective-permute-start(f32[400,128]{1,0:T(8,128)S(1)} %shard_map.33.one_ref), channel_id=1, source_target_pairs={{0,4},{4,0},{1,5},{5,1},{2,6},{6,2},{3,7},{7,3},{8,12},{12,8},{9,1... | collective-permute-start | bytes 614408 | tf_op jit(solution)/shard_map/ppermute | solution.py:141
  38.4 0.7 shard_map.31
  39.2 4.0 %all-to-all-start = ((f32[4,104,128]{2,1,0:T(8,128)}), f32[4,104,128]{2,1,0:T(8,128)S(1)}, u32[]{:S(2)}, u32[]{:S(2)}) async-start(f32[4,104,128]{2,1,0:T(8,128)} %shard_map.31), calls=%async_computation | async-start | bytes 425984 | tf_op jit(solution)/shard_map/all_to_all | solution.py:225
  43.2 2.5 %collective-permute-start.10 = (f32[400,128]{1,0:T(8,128)S(1)}, f32[400,128]{1,0:T(8,128)S(1)}, u32[]{:S(2)}, u32[]{:S(2)}) collective-permute-start(f32[400,128]{1,0:T(8,128)S(1)} %shard_map.32.one_ref), channel_id=1, source_target_pairs={{0,4},{4,0},{1,5},{5,1},{2,6},{6,2},{3,7},{7,3},{8,12},{12,8},{9,1... | collective-permute-start | bytes 614408 | tf_op jit(solution)/shard_map/ppermute | solution.py:141
  45.8 0.7 shard_map.34
  46.5 2.0 %all-to-all-done.a = f32[4,104,128]{2,1,0:T(8,128)S(1)} async-done(((f32[4,104,128]{2,1,0:T(8,128)}), f32[4,104,128]{2,1,0:T(8,128)S(1)}, u32[]{:S(2)}, u32[]{:S(2)}) %all-to-all-start) | async-done | bytes 213024 | tf_op jit(solution)/shard_map/all_to_all | solution.py:225
  48.4 3.4 %all-to-all-start.1 = ((f32[4,104,128]{2,1,0:T(8,128)}), f32[4,104,128]{2,1,0:T(8,128)S(1)}, u32[]{:S(2)}, u32[]{:S(2)}) async-start(f32[4,104,128]{2,1,0:T(8,128)} %shard_map.34), calls=%async_computation.1 | async-start | bytes 425984 | tf_op jit(solution)/shard_map/all_to_all | solution.py:225
  52.3 2.9 %collective-permute-start.5 = (f32[4,104,128]{2,1,0:T(8,128)S(1)}, f32[4,104,128]{2,1,0:T(8,128)S(1)}, u32[]{:S(2)}, u32[]{:S(2)}) collective-permute-start(f32[4,104,128]{2,1,0:T(8,128)S(1)} %all-to-all-done.a), channel_id=1, source_target_pairs={{0,2},{1,3},{2,0},{3,1},{4,6},{5,7},{6,4},{7,5},{8,10},{9,11},{10,... | collective-permute-start | bytes 638984 | tf_op jit(solution)/shard_map/ppermute | solution.py:146
  55.2 0.7 shard_map.35
  55.9 1.5 %all-to-all-done.1.a = f32[4,104,128]{2,1,0:T(8,128)S(1)} async-done(((f32[4,104,128]{2,1,0:T(8,128)}), f32[4,104,128]{2,1,0:T(8,128)S(1)}, u32[]{:S(2)}, u32[]{:S(2)}) %all-to-all-start.1) | async-done | bytes 213024 | tf_op jit(solution)/shard_map/all_to_all | solution.py:225
  57.3 3.4 %all-to-all-start.2 = ((f32[4,104,128]{2,1,0:T(8,128)}), f32[4,104,128]{2,1,0:T(8,128)S(1)}, u32[]{:S(2)}, u32[]{:S(2)}) async-start(f32[4,104,128]{2,1,0:T(8,128)} %shard_map.35), calls=%async_computation.2 | async-start | bytes 425984 | tf_op jit(solution)/shard_map/all_to_all | solution.py:225
  60.9 1.9 %collective-permute-start.17 = (f32[4,104,128]{2,1,0:T(8,128)S(1)}, f32[4,104,128]{2,1,0:T(8,128)S(1)}, u32[]{:S(2)}, u32[]{:S(2)}) collective-permute-start(f32[4,104,128]{2,1,0:T(8,128)S(1)} %all-to-all-done.1.a), channel_id=1, source_target_pairs={{0,3},{1,0},{2,1},{3,2},{4,7},{5,4},{6,5},{7,6},{8,11},{9,8},{10,9... | collective-permute-start | bytes 638984 | tf_op jit(solution)/shard_map/ppermute | solution.py:146
  62.7 3.0 %collective-permute-start.16 = (f32[4,104,128]{2,1,0:T(8,128)S(1)}, f32[4,104,128]{2,1,0:T(8,128)S(1)}, u32[]{:S(2)}, u32[]{:S(2)}) collective-permute-start(f32[4,104,128]{2,1,0:T(8,128)S(1)} %all-to-all-done.1.a), channel_id=1, source_target_pairs={{0,2},{1,3},{2,0},{3,1},{4,6},{5,7},{6,4},{7,5},{8,10},{9,11},{10,... | collective-permute-start | bytes 638984 | tf_op jit(solution)/shard_map/ppermute | solution.py:146
  66.0 2.5 %collective-permute-start.20 = (f32[4,104,128]{2,1,0:T(8,128)S(1)}, f32[4,104,128]{2,1,0:T(8,128)S(1)}, u32[]{:S(2)}, u32[]{:S(2)}) collective-permute-start(f32[4,104,128]{2,1,0:T(8,128)S(1)} %all-to-all-done.2.a), channel_id=1, source_target_pairs={{0,3},{1,0},{2,1},{3,2},{4,7},{5,4},{6,5},{7,6},{8,11},{9,8},{10,9... | collective-permute-start | bytes 638984 | tf_op jit(solution)/shard_map/ppermute | solution.py:146
  68.5 2.5 %collective-permute-start.19 = (f32[4,104,128]{2,1,0:T(8,128)S(1)}, f32[4,104,128]{2,1,0:T(8,128)S(1)}, u32[]{:S(2)}, u32[]{:S(2)}) collective-permute-start(f32[4,104,128]{2,1,0:T(8,128)S(1)} %all-to-all-done.2.a), channel_id=1, source_target_pairs={{0,2},{1,3},{2,0},{3,1},{4,6},{5,7},{6,4},{7,5},{8,10},{9,11},{10,... | collective-permute-start | bytes 638984 | tf_op jit(solution)/shard_map/ppermute | solution.py:146
  71.8 3.1 %collective-permute-start.21 = (f32[416,128]{1,0:T(8,128)S(1)}, f32[416,128]{1,0:T(8,128)S(1)}, u32[]{:S(2)}, u32[]{:S(2)}) collective-permute-start(f32[416,128]{1,0:T(8,128)S(1)} %get-tuple-element.199.mine), channel_id=1, source_target_pairs={{0,24},{16,9},{25,1},{9,16},{2,26},{18,11},{27,3},{11,18},{4,28},{... | collective-permute-start | bytes 638984 | tf_op jit(solution)/shard_map/ppermute | solution.py:155
  75.3 1.3 collective-permute-start.23
  76.6 1.0 collective-permute-done.21.crossed
  78.3 3.4 %collective-permute-done.18.b = f32[4,104,128]{2,1,0:T(8,128)S(1)} collective-permute-done((f32[4,104,128]{2,1,0:T(8,128)S(1)}, f32[4,104,128]{2,1,0:T(8,128)S(1)}, u32[]{:S(2)}, u32[]{:S(2)}) %collective-permute-start.18) | collective-permute-done | bytes 213024 | tf_op jit(solution)/shard_map/ppermute | solution.py:146
  82.7 2.2 %collective-permute-start.26 = (f32[416,128]{1,0:T(8,128)S(1)}, f32[416,128]{1,0:T(8,128)S(1)}, u32[]{:S(2)}, u32[]{:S(2)}) collective-permute-start(f32[416,128]{1,0:T(8,128)S(1)} %shard_map.40.refs_6_), channel_id=1, source_target_pairs={{0,8},{8,0},{16,24},{24,16},{1,9},{9,1},{17,25},{25,17},{2,10},{10... | collective-permute-start | bytes 638984 | tf_op jit(solution)/shard_map/ppermute | solution.py:237
  84.9 3.0 %collective-permute-start.25 = (f32[416,128]{1,0:T(8,128)S(1)}, f32[416,128]{1,0:T(8,128)S(1)}, u32[]{:S(2)}, u32[]{:S(2)}) collective-permute-start(f32[416,128]{1,0:T(8,128)S(1)} %get-tuple-element.236.mine), channel_id=1, source_target_pairs={{0,24},{16,9},{25,1},{9,16},{2,26},{18,11},{27,3},{11,18},{4,28},{... | collective-permute-start | bytes 638984 | tf_op jit(solution)/shard_map/ppermute | solution.py:155
  87.9 2.0 %shard_map.41 = (f32[4,384,128]{2,1,0:T(8,128)S(1)}, f32[4,384,128]{2,1,0:T(8,128)S(1)}) custom-call(s32[2]{0:T(128)S(1)} %add_convert_fusion.flags_ref, bf16[4,128,416]{2,1,0:T(8,128)(2,1)S(1)} %get-tuple-element.247.refs_0_, bf16[4,128,416]{2,1,0:T(8,128)(2,1)S(1)} %get-tuple-element.248.refs_1_, bf16[4,128,416]{2,1,0:T(8,128)(2,1)S(1)} %get-tuple-element.249.refs_2_, ...), custom_call_target="tpu_custom_call" | custom-call | flops 12000000000 | bytes 44000000 | tf_op jit(solution)/shard_map/pallas_call | solution.py:175
  89.9 15.9 %collective-permute-start.24 = (f32[4,384,128]{2,1,0:T(8,128)S(1)}, f32[4,384,128]{2,1,0:T(8,128)S(1)}, u32[]{:S(2)}, u32[]{:S(2)}) collective-permute-start(f32[4,384,128]{2,1,0:T(8,128)S(1)} %get-tuple-element.223), channel_id=1, source_target_pairs={{0,128},{128,0},{1,129},{129,1},{2,130},{130,2},{3,131},{131,3},{4... | collective-permute-start | bytes 2359304 | tf_op jit(solution)/shard_map/ppermute | solution.py:141
  105.8 2.0 %shard_map.42 = (f32[4,384,128]{2,1,0:T(8,128)S(1)}, f32[4,384,128]{2,1,0:T(8,128)S(1)}) custom-call(s32[2]{0:T(128)S(1)} %add_convert_fusion.flags_ref, bf16[4,128,416]{2,1,0:T(8,128)(2,1)S(1)} %get-tuple-element.247.refs_0_, bf16[4,128,416]{2,1,0:T(8,128)(2,1)S(1)} %get-tuple-element.248.refs_1_, bf16[4,128,416]{2,1,0:T(8,128)(2,1)S(1)} %get-tuple-element.249.refs_2_, ...), custom_call_target="tpu_custom_call" | custom-call | flops 12000000000 | bytes 44000000 | tf_op jit(solution)/shard_map/pallas_call | solution.py:175
  108.7 3.3 %collective-permute-start.27 = (f32[384,128]{1,0:T(8,128)S(1)}, f32[384,128]{1,0:T(8,128)S(1)}, u32[]{:S(2)}, u32[]{:S(2)}) collective-permute-start(f32[384,128]{1,0:T(8,128)S(1)} %get-tuple-element.242), channel_id=1, source_target_pairs={{0,64},{32,96},{64,0},{96,32},{1,65},{33,97},{65,1},{97,33},{2,66}... | collective-permute-start | bytes 589832 | tf_op jit(solution)/shard_map/ppermute | solution.py:146
  112.3 2.4 %collective-permute-start.29 = (f32[384,128]{1,0:T(8,128)S(1)}, f32[384,128]{1,0:T(8,128)S(1)}, u32[]{:S(2)}, u32[]{:S(2)}) collective-permute-start(f32[384,128]{1,0:T(8,128)S(1)} %get-tuple-element.244), channel_id=1, source_target_pairs={{0,96},{32,0},{64,32},{96,64},{1,97},{33,1},{65,33},{97,65},{2,98}... | collective-permute-start | bytes 589832 | tf_op jit(solution)/shard_map/ppermute | solution.py:146
  114.9 2.0 %shard_map.45 = (f32[4,384,128]{2,1,0:T(8,128)S(1)}, f32[4,384,128]{2,1,0:T(8,128)S(1)}) custom-call(s32[2]{0:T(128)S(1)} %add_convert_fusion.flags_ref, bf16[4,128,416]{2,1,0:T(8,128)(2,1)S(1)} %get-tuple-element.247.refs_0_, bf16[4,128,416]{2,1,0:T(8,128)(2,1)S(1)} %get-tuple-element.248.refs_1_, bf16[4,128,416]{2,1,0:T(8,128)(2,1)S(1)} %get-tuple-element.249.refs_2_, ...), custom_call_target="tpu_custom_call" | custom-call | flops 12000000000 | bytes 44000000 | tf_op jit(solution)/shard_map/pallas_call | solution.py:175
  116.9 1.4 collective-permute-start.35
  118.4 3.3 %collective-permute-start.32 = (f32[384,128]{1,0:T(8,128)S(1)}, f32[384,128]{1,0:T(8,128)S(1)}, u32[]{:S(2)}, u32[]{:S(2)}) collective-permute-start(f32[384,128]{1,0:T(8,128)S(1)} %get-tuple-element.264), channel_id=1, source_target_pairs={{0,64},{32,96},{64,0},{96,32},{1,65},{33,97},{65,1},{97,33},{2,66}... | collective-permute-start | bytes 589832 | tf_op jit(solution)/shard_map/ppermute | solution.py:146
  122.0 2.4 %collective-permute-start.34 = (f32[384,128]{1,0:T(8,128)S(1)}, f32[384,128]{1,0:T(8,128)S(1)}, u32[]{:S(2)}, u32[]{:S(2)}) collective-permute-start(f32[384,128]{1,0:T(8,128)S(1)} %get-tuple-element.266), channel_id=1, source_target_pairs={{0,96},{32,0},{64,32},{96,64},{1,97},{33,1},{65,33},{97,65},{2,98}... | collective-permute-start | bytes 589832 | tf_op jit(solution)/shard_map/ppermute | solution.py:146
  124.6 0.6 collective-permute-start.37
  125.2 1.7 %collective-permute-done.32.b = f32[384,128]{1,0:T(8,128)S(1)} collective-permute-done((f32[384,128]{1,0:T(8,128)S(1)}, f32[384,128]{1,0:T(8,128)S(1)}, u32[]{:S(2)}, u32[]{:S(2)}) %collective-permute-start.32) | collective-permute-done | bytes 196640 | tf_op jit(solution)/shard_map/ppermute | solution.py:146
  126.9 2.5 %collective-permute-start.38 = (f32[384,128]{1,0:T(8,128)S(1)}, f32[384,128]{1,0:T(8,128)S(1)}, u32[]{:S(2)}, u32[]{:S(2)}) collective-permute-start(f32[384,128]{1,0:T(8,128)S(1)} %get-tuple-element.278), channel_id=1, source_target_pairs={{0,96},{32,0},{64,32},{96,64},{1,97},{33,1},{65,33},{97,65},{2,98}... | collective-permute-start | bytes 589832 | tf_op jit(solution)/shard_map/ppermute | solution.py:146
  129.4 2.0 %collective-permute-done.33.c = f32[384,128]{1,0:T(8,128)S(1)} collective-permute-done((f32[384,128]{1,0:T(8,128)S(1)}, f32[384,128]{1,0:T(8,128)S(1)}, u32[]{:S(2)}, u32[]{:S(2)}) %collective-permute-start.33) | collective-permute-done | bytes 196640 | tf_op jit(solution)/shard_map/ppermute | solution.py:146
  131.5 3.9 %collective-permute-done.36.b = f32[384,128]{1,0:T(8,128)S(1)} collective-permute-done((f32[384,128]{1,0:T(8,128)S(1)}, f32[384,128]{1,0:T(8,128)S(1)}, u32[]{:S(2)}, u32[]{:S(2)}) %collective-permute-start.36) | collective-permute-done | bytes 196640 | tf_op jit(solution)/shard_map/ppermute | solution.py:146
  135.4 4.3 %collective-permute-done.37.c = f32[384,128]{1,0:T(8,128)S(1)} collective-permute-done((f32[384,128]{1,0:T(8,128)S(1)}, f32[384,128]{1,0:T(8,128)S(1)}, u32[]{:S(2)}, u32[]{:S(2)}) %collective-permute-start.37) | collective-permute-done | bytes 196640 | tf_op jit(solution)/shard_map/ppermute | solution.py:146
  139.7 0.9 shard_map.50
  (66 shorter events, 6.3 us)
Async XLA Ops:
  0.0 11.3 %copy-start = (f32[768,800]{0,1:T(8,128)S(1)}, f32[768,800]{0,1:T(8,128)}, u32[]{:S(2)}) copy-start(f32[768,800]{0,1:T(8,128)} %param.3) | copy-start | bytes 7372804
  4.9 13.1 %collective-permute-start = (f32[400,128]{1,0:T(8,128)}, f32[400,128]{1,0:T(8,128)S(1)}, u32[]{:S(2)}, u32[]{:S(2)}) collective-permute-start(f32[400,128]{1,0:T(8,128)} %get-tuple-element.146), channel_id=1, source_target_pairs={{0,2},{1,3},{2,0},{3,1},{4,6},{5,7},{6,4},{7,5},{8,10},{9,11},{10,... | collective-permute-start | bytes 614408 | tf_op jit(solution)/shard_map/ppermute | solution.py:146
  8.6 11.6 %collective-permute-start.1 = (f32[400,128]{1,0:T(8,128)}, f32[400,128]{1,0:T(8,128)S(1)}, u32[]{:S(2)}, u32[]{:S(2)}) collective-permute-start(f32[400,128]{1,0:T(8,128)} %get-tuple-element.147), channel_id=1, source_target_pairs={{0,1},{1,2},{2,3},{3,0},{4,5},{5,6},{6,7},{7,4},{8,9},{9,10},{10,1... | collective-permute-start | bytes 614408 | tf_op jit(solution)/shard_map/ppermute | solution.py:146
  9.0 11.2 %collective-permute-start.2 = (f32[400,128]{1,0:T(8,128)}, f32[400,128]{1,0:T(8,128)S(1)}, u32[]{:S(2)}, u32[]{:S(2)}) collective-permute-start(f32[400,128]{1,0:T(8,128)} %get-tuple-element.148), channel_id=1, source_target_pairs={{0,3},{1,0},{2,1},{3,2},{4,7},{5,4},{6,5},{7,6},{8,11},{9,8},{10,9... | collective-permute-start | bytes 614408 | tf_op jit(solution)/shard_map/ppermute | solution.py:146
  11.3 1.7 %copy-start.1 = (f32[2,384,768]{2,1,0:T(8,128)S(1)}, f32[2,384,768]{2,1,0:T(8,128)}, u32[]{:S(2)}) copy-start(f32[2,384,768]{2,1,0:T(8,128)} %refs_1_) | copy-start | bytes 7077892
  13.0 7.2 %copy-start.2 = (f32[400,128]{1,0:T(8,128)S(1)}, f32[400,128]{1,0:T(8,128)}, u32[]{:S(2)}) copy-start(f32[400,128]{1,0:T(8,128)} %get-tuple-element.153.a) | copy-start | bytes 614404
  17.4 11.6 %collective-permute-start.11 = (f32[400,128]{1,0:T(8,128)S(1)}, f32[400,128]{1,0:T(8,128)S(1)}, u32[]{:S(2)}, u32[]{:S(2)}) collective-permute-start(f32[400,128]{1,0:T(8,128)S(1)} %get-tuple-element.170), channel_id=1, source_target_pairs={{0,2},{1,3},{2,0},{3,1},{4,6},{5,7},{6,4},{7,5},{8,10},{9,11},{10,... | collective-permute-start | bytes 614408 | tf_op jit(solution)/shard_map/ppermute | solution.py:146
  17.5 12.5 %collective-permute-start.12 = (f32[400,128]{1,0:T(8,128)S(1)}, f32[400,128]{1,0:T(8,128)S(1)}, u32[]{:S(2)}, u32[]{:S(2)}) collective-permute-start(f32[400,128]{1,0:T(8,128)S(1)} %get-tuple-element.171), channel_id=1, source_target_pairs={{0,1},{1,2},{2,3},{3,0},{4,5},{5,6},{6,7},{7,4},{8,9},{9,10},{10,1... | collective-permute-start | bytes 614408 | tf_op jit(solution)/shard_map/ppermute | solution.py:146
  18.0 13.6 %collective-permute-start.13 = (f32[400,128]{1,0:T(8,128)S(1)}, f32[400,128]{1,0:T(8,128)S(1)}, u32[]{:S(2)}, u32[]{:S(2)}) collective-permute-start(f32[400,128]{1,0:T(8,128)S(1)} %get-tuple-element.172), channel_id=1, source_target_pairs={{0,3},{1,0},{2,1},{3,2},{4,7},{5,4},{6,5},{7,6},{8,11},{9,8},{10,9... | collective-permute-start | bytes 614408 | tf_op jit(solution)/shard_map/ppermute | solution.py:146
  20.3 18.2 %collective-permute-start.3 = (f32[400,128]{1,0:T(8,128)S(1)}, f32[400,128]{1,0:T(8,128)S(1)}, u32[]{:S(2)}, u32[]{:S(2)}) collective-permute-start(f32[400,128]{1,0:T(8,128)S(1)} %shard_map.30.one_ref), channel_id=1, source_target_pairs={{0,4},{4,0},{1,5},{5,1},{2,6},{6,2},{3,7},{7,3},{8,12},{12,8},{9,1... | collective-permute-start | bytes 614408 | tf_op jit(solution)/shard_map/ppermute | solution.py:141
  27.3 15.9 %collective-permute-start.7 = (f32[400,128]{1,0:T(8,128)S(1)}, f32[400,128]{1,0:T(8,128)S(1)}, u32[]{:S(2)}, u32[]{:S(2)}) collective-permute-start(f32[400,128]{1,0:T(8,128)S(1)} %get-tuple-element.163), channel_id=1, source_target_pairs={{0,2},{1,3},{2,0},{3,1},{4,6},{5,7},{6,4},{7,5},{8,10},{9,11},{10,... | collective-permute-start | bytes 614408 | tf_op jit(solution)/shard_map/ppermute | solution.py:146
  29.0 14.2 %collective-permute-start.8 = (f32[400,128]{1,0:T(8,128)S(1)}, f32[400,128]{1,0:T(8,128)S(1)}, u32[]{:S(2)}, u32[]{:S(2)}) collective-permute-start(f32[400,128]{1,0:T(8,128)S(1)} %get-tuple-element.164), channel_id=1, source_target_pairs={{0,1},{1,2},{2,3},{3,0},{4,5},{5,6},{6,7},{7,4},{8,9},{9,10},{10,1... | collective-permute-start | bytes 614408 | tf_op jit(solution)/shard_map/ppermute | solution.py:146
  29.9 13.2 %collective-permute-start.9 = (f32[400,128]{1,0:T(8,128)S(1)}, f32[400,128]{1,0:T(8,128)S(1)}, u32[]{:S(2)}, u32[]{:S(2)}) collective-permute-start(f32[400,128]{1,0:T(8,128)S(1)} %get-tuple-element.165), channel_id=1, source_target_pairs={{0,3},{1,0},{2,1},{3,2},{4,7},{5,4},{6,5},{7,6},{8,11},{9,8},{10,9... | collective-permute-start | bytes 614408 | tf_op jit(solution)/shard_map/ppermute | solution.py:146
  31.7 14.1 %collective-permute-start.14 = (f32[400,128]{1,0:T(8,128)S(1)}, f32[400,128]{1,0:T(8,128)S(1)}, u32[]{:S(2)}, u32[]{:S(2)}) collective-permute-start(f32[400,128]{1,0:T(8,128)S(1)} %shard_map.33.one_ref), channel_id=1, source_target_pairs={{0,4},{4,0},{1,5},{5,1},{2,6},{6,2},{3,7},{7,3},{8,12},{12,8},{9,1... | collective-permute-start | bytes 614408 | tf_op jit(solution)/shard_map/ppermute | solution.py:141
  39.2 9.3 %all-to-all-start = ((f32[4,104,128]{2,1,0:T(8,128)}), f32[4,104,128]{2,1,0:T(8,128)S(1)}, u32[]{:S(2)}, u32[]{:S(2)}) async-start(f32[4,104,128]{2,1,0:T(8,128)} %shard_map.31), calls=%async_computation | async-start | bytes 425984 | tf_op jit(solution)/shard_map/all_to_all | solution.py:225
  43.2 11.9 %collective-permute-start.10 = (f32[400,128]{1,0:T(8,128)S(1)}, f32[400,128]{1,0:T(8,128)S(1)}, u32[]{:S(2)}, u32[]{:S(2)}) collective-permute-start(f32[400,128]{1,0:T(8,128)S(1)} %shard_map.32.one_ref), channel_id=1, source_target_pairs={{0,4},{4,0},{1,5},{5,1},{2,6},{6,2},{3,7},{7,3},{8,12},{12,8},{9,1... | collective-permute-start | bytes 614408 | tf_op jit(solution)/shard_map/ppermute | solution.py:141
  48.4 8.9 %all-to-all-start.1 = ((f32[4,104,128]{2,1,0:T(8,128)}), f32[4,104,128]{2,1,0:T(8,128)S(1)}, u32[]{:S(2)}, u32[]{:S(2)}) async-start(f32[4,104,128]{2,1,0:T(8,128)} %shard_map.34), calls=%async_computation.1 | async-start | bytes 425984 | tf_op jit(solution)/shard_map/all_to_all | solution.py:225
  51.8 14.0 %collective-permute-start.6 = (f32[4,104,128]{2,1,0:T(8,128)S(1)}, f32[4,104,128]{2,1,0:T(8,128)S(1)}, u32[]{:S(2)}, u32[]{:S(2)}) collective-permute-start(f32[4,104,128]{2,1,0:T(8,128)S(1)} %all-to-all-done.a), channel_id=1, source_target_pairs={{0,3},{1,0},{2,1},{3,2},{4,7},{5,4},{6,5},{7,6},{8,11},{9,8},{10,9... | collective-permute-start | bytes 638984 | tf_op jit(solution)/shard_map/ppermute | solution.py:146
  52.3 13.7 %collective-permute-start.5 = (f32[4,104,128]{2,1,0:T(8,128)S(1)}, f32[4,104,128]{2,1,0:T(8,128)S(1)}, u32[]{:S(2)}, u32[]{:S(2)}) collective-permute-start(f32[4,104,128]{2,1,0:T(8,128)S(1)} %all-to-all-done.a), channel_id=1, source_target_pairs={{0,2},{1,3},{2,0},{3,1},{4,6},{5,7},{6,4},{7,5},{8,10},{9,11},{10,... | collective-permute-start | bytes 638984 | tf_op jit(solution)/shard_map/ppermute | solution.py:146
  55.1 13.3 %collective-permute-start.4 = (f32[4,104,128]{2,1,0:T(8,128)S(1)}, f32[4,104,128]{2,1,0:T(8,128)S(1)}, u32[]{:S(2)}, u32[]{:S(2)}) collective-permute-start(f32[4,104,128]{2,1,0:T(8,128)S(1)} %all-to-all-done.a), channel_id=1, source_target_pairs={{0,1},{1,2},{2,3},{3,0},{4,5},{5,6},{6,7},{7,4},{8,9},{9,10},{10,1... | collective-permute-start | bytes 638984 | tf_op jit(solution)/shard_map/ppermute | solution.py:146
  57.3 8.6 %all-to-all-start.2 = ((f32[4,104,128]{2,1,0:T(8,128)}), f32[4,104,128]{2,1,0:T(8,128)S(1)}, u32[]{:S(2)}, u32[]{:S(2)}) async-start(f32[4,104,128]{2,1,0:T(8,128)} %shard_map.35), calls=%async_computation.2 | async-start | bytes 425984 | tf_op jit(solution)/shard_map/all_to_all | solution.py:225
  60.9 10.5 %collective-permute-start.17 = (f32[4,104,128]{2,1,0:T(8,128)S(1)}, f32[4,104,128]{2,1,0:T(8,128)S(1)}, u32[]{:S(2)}, u32[]{:S(2)}) collective-permute-start(f32[4,104,128]{2,1,0:T(8,128)S(1)} %all-to-all-done.1.a), channel_id=1, source_target_pairs={{0,3},{1,0},{2,1},{3,2},{4,7},{5,4},{6,5},{7,6},{8,11},{9,8},{10,9... | collective-permute-start | bytes 638984 | tf_op jit(solution)/shard_map/ppermute | solution.py:146
  62.7 9.0 %collective-permute-start.16 = (f32[4,104,128]{2,1,0:T(8,128)S(1)}, f32[4,104,128]{2,1,0:T(8,128)S(1)}, u32[]{:S(2)}, u32[]{:S(2)}) collective-permute-start(f32[4,104,128]{2,1,0:T(8,128)S(1)} %all-to-all-done.1.a), channel_id=1, source_target_pairs={{0,2},{1,3},{2,0},{3,1},{4,6},{5,7},{6,4},{7,5},{8,10},{9,11},{10,... | collective-permute-start | bytes 638984 | tf_op jit(solution)/shard_map/ppermute | solution.py:146
  65.8 6.0 %collective-permute-start.15 = (f32[4,104,128]{2,1,0:T(8,128)S(1)}, f32[4,104,128]{2,1,0:T(8,128)S(1)}, u32[]{:S(2)}, u32[]{:S(2)}) collective-permute-start(f32[4,104,128]{2,1,0:T(8,128)S(1)} %all-to-all-done.1.a), channel_id=1, source_target_pairs={{0,1},{1,2},{2,3},{3,0},{4,5},{5,6},{6,7},{7,4},{8,9},{9,10},{10,1... | collective-permute-start | bytes 638984 | tf_op jit(solution)/shard_map/ppermute | solution.py:146
  66.0 12.4 %collective-permute-start.20 = (f32[4,104,128]{2,1,0:T(8,128)S(1)}, f32[4,104,128]{2,1,0:T(8,128)S(1)}, u32[]{:S(2)}, u32[]{:S(2)}) collective-permute-start(f32[4,104,128]{2,1,0:T(8,128)S(1)} %all-to-all-done.2.a), channel_id=1, source_target_pairs={{0,3},{1,0},{2,1},{3,2},{4,7},{5,4},{6,5},{7,6},{8,11},{9,8},{10,9... | collective-permute-start | bytes 638984 | tf_op jit(solution)/shard_map/ppermute | solution.py:146
  68.5 9.9 %collective-permute-start.19 = (f32[4,104,128]{2,1,0:T(8,128)S(1)}, f32[4,104,128]{2,1,0:T(8,128)S(1)}, u32[]{:S(2)}, u32[]{:S(2)}) collective-permute-start(f32[4,104,128]{2,1,0:T(8,128)S(1)} %all-to-all-done.2.a), channel_id=1, source_target_pairs={{0,2},{1,3},{2,0},{3,1},{4,6},{5,7},{6,4},{7,5},{8,10},{9,11},{10,... | collective-permute-start | bytes 638984 | tf_op jit(solution)/shard_map/ppermute | solution.py:146
  71.4 10.3 %collective-permute-start.18 = (f32[4,104,128]{2,1,0:T(8,128)S(1)}, f32[4,104,128]{2,1,0:T(8,128)S(1)}, u32[]{:S(2)}, u32[]{:S(2)}) collective-permute-start(f32[4,104,128]{2,1,0:T(8,128)S(1)} %all-to-all-done.2.a), channel_id=1, source_target_pairs={{0,1},{1,2},{2,3},{3,0},{4,5},{5,6},{6,7},{7,4},{8,9},{9,10},{10,1... | collective-permute-start | bytes 638984 | tf_op jit(solution)/shard_map/ppermute | solution.py:146
  71.8 5.9 %collective-permute-start.21 = (f32[416,128]{1,0:T(8,128)S(1)}, f32[416,128]{1,0:T(8,128)S(1)}, u32[]{:S(2)}, u32[]{:S(2)}) collective-permute-start(f32[416,128]{1,0:T(8,128)S(1)} %get-tuple-element.199.mine), channel_id=1, source_target_pairs={{0,24},{16,9},{25,1},{9,16},{2,26},{18,11},{27,3},{11,18},{4,28},{... | collective-permute-start | bytes 638984 | tf_op jit(solution)/shard_map/ppermute | solution.py:155
  75.3 6.8 %collective-permute-start.23 = (f32[416,128]{1,0:T(8,128)S(1)}, f32[416,128]{1,0:T(8,128)S(1)}, u32[]{:S(2)}, u32[]{:S(2)}) collective-permute-start(f32[416,128]{1,0:T(8,128)S(1)} %get-tuple-element.211.mine), channel_id=1, source_target_pairs={{0,24},{16,9},{25,1},{9,16},{2,26},{18,11},{27,3},{11,18},{4,28},{... | collective-permute-start | bytes 638984 | tf_op jit(solution)/shard_map/ppermute | solution.py:155
  78.2 9.7 %collective-permute-start.22 = (f32[416,128]{1,0:T(8,128)S(1)}, f32[416,128]{1,0:T(8,128)S(1)}, u32[]{:S(2)}, u32[]{:S(2)}) collective-permute-start(f32[416,128]{1,0:T(8,128)S(1)} %shard_map.38.refs_6_), channel_id=1, source_target_pairs={{0,8},{8,0},{16,24},{24,16},{1,9},{9,1},{17,25},{25,17},{2,10},{10... | collective-permute-start | bytes 638984 | tf_op jit(solution)/shard_map/ppermute | solution.py:237
  82.7 23.1 %collective-permute-start.26 = (f32[416,128]{1,0:T(8,128)S(1)}, f32[416,128]{1,0:T(8,128)S(1)}, u32[]{:S(2)}, u32[]{:S(2)}) collective-permute-start(f32[416,128]{1,0:T(8,128)S(1)} %shard_map.40.refs_6_), channel_id=1, source_target_pairs={{0,8},{8,0},{16,24},{24,16},{1,9},{9,1},{17,25},{25,17},{2,10},{10... | collective-permute-start | bytes 638984 | tf_op jit(solution)/shard_map/ppermute | solution.py:237
  84.9 23.0 %collective-permute-start.25 = (f32[416,128]{1,0:T(8,128)S(1)}, f32[416,128]{1,0:T(8,128)S(1)}, u32[]{:S(2)}, u32[]{:S(2)}) collective-permute-start(f32[416,128]{1,0:T(8,128)S(1)} %get-tuple-element.236.mine), channel_id=1, source_target_pairs={{0,24},{16,9},{25,1},{9,16},{2,26},{18,11},{27,3},{11,18},{4,28},{... | collective-permute-start | bytes 638984 | tf_op jit(solution)/shard_map/ppermute | solution.py:155
  89.9 18.7 %collective-permute-start.24 = (f32[4,384,128]{2,1,0:T(8,128)S(1)}, f32[4,384,128]{2,1,0:T(8,128)S(1)}, u32[]{:S(2)}, u32[]{:S(2)}) collective-permute-start(f32[4,384,128]{2,1,0:T(8,128)S(1)} %get-tuple-element.223), channel_id=1, source_target_pairs={{0,128},{128,0},{1,129},{129,1},{2,130},{130,2},{3,131},{131,3},{4... | collective-permute-start | bytes 2359304 | tf_op jit(solution)/shard_map/ppermute | solution.py:141
  107.8 10.5 %collective-permute-start.30 = (f32[4,384,128]{2,1,0:T(8,128)S(1)}, f32[4,384,128]{2,1,0:T(8,128)S(1)}, u32[]{:S(2)}, u32[]{:S(2)}) collective-permute-start(f32[4,384,128]{2,1,0:T(8,128)S(1)} %get-tuple-element.234), channel_id=1, source_target_pairs={{0,128},{128,0},{1,129},{129,1},{2,130},{130,2},{3,131},{131,3},{4... | collective-permute-start | bytes 2359304 | tf_op jit(solution)/shard_map/ppermute | solution.py:141
  108.5 6.4 %collective-permute-start.31 = (f32[416,128]{1,0:T(8,128)S(1)}, f32[416,128]{1,0:T(8,128)S(1)}, u32[]{:S(2)}, u32[]{:S(2)}) collective-permute-start(f32[416,128]{1,0:T(8,128)S(1)} %shard_map.43.refs_6_), channel_id=1, source_target_pairs={{0,8},{8,0},{16,24},{24,16},{1,9},{9,1},{17,25},{25,17},{2,10},{10... | collective-permute-start | bytes 638984 | tf_op jit(solution)/shard_map/ppermute | solution.py:237
  108.7 13.0 %collective-permute-start.27 = (f32[384,128]{1,0:T(8,128)S(1)}, f32[384,128]{1,0:T(8,128)S(1)}, u32[]{:S(2)}, u32[]{:S(2)}) collective-permute-start(f32[384,128]{1,0:T(8,128)S(1)} %get-tuple-element.242), channel_id=1, source_target_pairs={{0,64},{32,96},{64,0},{96,32},{1,65},{33,97},{65,1},{97,33},{2,66}... | collective-permute-start | bytes 589832 | tf_op jit(solution)/shard_map/ppermute | solution.py:146
  112.0 10.0 %collective-permute-start.28 = (f32[384,128]{1,0:T(8,128)S(1)}, f32[384,128]{1,0:T(8,128)S(1)}, u32[]{:S(2)}, u32[]{:S(2)}) collective-permute-start(f32[384,128]{1,0:T(8,128)S(1)} %get-tuple-element.243), channel_id=1, source_target_pairs={{0,32},{32,64},{64,96},{96,0},{1,33},{33,65},{65,97},{97,1},{2,34}... | collective-permute-start | bytes 589832 | tf_op jit(solution)/shard_map/ppermute | solution.py:146
  112.3 12.1 %collective-permute-start.29 = (f32[384,128]{1,0:T(8,128)S(1)}, f32[384,128]{1,0:T(8,128)S(1)}, u32[]{:S(2)}, u32[]{:S(2)}) collective-permute-start(f32[384,128]{1,0:T(8,128)S(1)} %get-tuple-element.244), channel_id=1, source_target_pairs={{0,96},{32,0},{64,32},{96,64},{1,97},{33,1},{65,33},{97,65},{2,98}... | collective-permute-start | bytes 589832 | tf_op jit(solution)/shard_map/ppermute | solution.py:146
  116.9 7.6 %collective-permute-start.35 = (f32[4,384,128]{2,1,0:T(8,128)S(1)}, f32[4,384,128]{2,1,0:T(8,128)S(1)}, u32[]{:S(2)}, u32[]{:S(2)}) collective-permute-start(f32[4,384,128]{2,1,0:T(8,128)S(1)} %get-tuple-element.255), channel_id=1, source_target_pairs={{0,128},{128,0},{1,129},{129,1},{2,130},{130,2},{3,131},{131,3},{4... | collective-permute-start | bytes 2359304 | tf_op jit(solution)/shard_map/ppermute | solution.py:141
  118.4 8.6 %collective-permute-start.32 = (f32[384,128]{1,0:T(8,128)S(1)}, f32[384,128]{1,0:T(8,128)S(1)}, u32[]{:S(2)}, u32[]{:S(2)}) collective-permute-start(f32[384,128]{1,0:T(8,128)S(1)} %get-tuple-element.264), channel_id=1, source_target_pairs={{0,64},{32,96},{64,0},{96,32},{1,65},{33,97},{65,1},{97,33},{2,66}... | collective-permute-start | bytes 589832 | tf_op jit(solution)/shard_map/ppermute | solution.py:146
  121.7 9.7 %collective-permute-start.33 = (f32[384,128]{1,0:T(8,128)S(1)}, f32[384,128]{1,0:T(8,128)S(1)}, u32[]{:S(2)}, u32[]{:S(2)}) collective-permute-start(f32[384,128]{1,0:T(8,128)S(1)} %get-tuple-element.265), channel_id=1, source_target_pairs={{0,32},{32,64},{64,96},{96,0},{1,33},{33,65},{65,97},{97,1},{2,34}... | collective-permute-start | bytes 589832 | tf_op jit(solution)/shard_map/ppermute | solution.py:146
  122.0 9.4 %collective-permute-start.34 = (f32[384,128]{1,0:T(8,128)S(1)}, f32[384,128]{1,0:T(8,128)S(1)}, u32[]{:S(2)}, u32[]{:S(2)}) collective-permute-start(f32[384,128]{1,0:T(8,128)S(1)} %get-tuple-element.266), channel_id=1, source_target_pairs={{0,96},{32,0},{64,32},{96,64},{1,97},{33,1},{65,33},{97,65},{2,98}... | collective-permute-start | bytes 589832 | tf_op jit(solution)/shard_map/ppermute | solution.py:146
  124.5 10.9 %collective-permute-start.36 = (f32[384,128]{1,0:T(8,128)S(1)}, f32[384,128]{1,0:T(8,128)S(1)}, u32[]{:S(2)}, u32[]{:S(2)}) collective-permute-start(f32[384,128]{1,0:T(8,128)S(1)} %get-tuple-element.276), channel_id=1, source_target_pairs={{0,64},{32,96},{64,0},{96,32},{1,65},{33,97},{65,1},{97,33},{2,66}... | collective-permute-start | bytes 589832 | tf_op jit(solution)/shard_map/ppermute | solution.py:146
  124.6 15.1 %collective-permute-start.37 = (f32[384,128]{1,0:T(8,128)S(1)}, f32[384,128]{1,0:T(8,128)S(1)}, u32[]{:S(2)}, u32[]{:S(2)}) collective-permute-start(f32[384,128]{1,0:T(8,128)S(1)} %get-tuple-element.277), channel_id=1, source_target_pairs={{0,32},{32,64},{64,96},{96,0},{1,33},{33,65},{65,97},{97,1},{2,34}... | collective-permute-start | bytes 589832 | tf_op jit(solution)/shard_map/ppermute | solution.py:146
  126.9 12.8 %collective-permute-start.38 = (f32[384,128]{1,0:T(8,128)S(1)}, f32[384,128]{1,0:T(8,128)S(1)}, u32[]{:S(2)}, u32[]{:S(2)}) collective-permute-start(f32[384,128]{1,0:T(8,128)S(1)} %get-tuple-element.278), channel_id=1, source_target_pairs={{0,96},{32,0},{64,32},{96,64},{1,97},{33,1},{65,33},{97,65},{2,98}... | collective-permute-start | bytes 589832 | tf_op jit(solution)/shard_map/ppermute | solution.py:146
